TPU v7x, 32 devices: a whole 2x2x4 slice. The times are simulated.
32 devices in a mesh: groups: 2 (over y), gx: 16 (over z, x, core).
Axes of the slice: x: 2, y: 2, z: 4, core: 2. Of those that a mesh axis runs over, the one named last changes fastest.
Arguments:
- grad_out: bfloat16 [64, 4, 128, 128], P(('groups', 'gx')), parts along dimension 0, may hold values from -6 to 6
- inputs: bfloat16 [64, 4, 128, 128], P(('groups', 'gx')), parts along dimension 0, may hold values from -6 to 6
- pre_first: bfloat16 [64, 4, 128, 128], P(('groups', 'gx')), parts along dimension 0, may hold values from -6 to 6
- pre_second: bfloat16 [64, 4, 128, 128], P(('groups', 'gx')), parts along dimension 0, may hold values from -6 to 6
- filter_first: bfloat16 [3456, 128], P('gx'), may hold values from -0.109375 to 0.109375
- filter_second: bfloat16 [3456, 128], P('gx'), may hold values from -0.109375 to 0.109375
Outputs:
- grad_inputs: bfloat16 [64, 4, 128, 128], P(('groups', 'gx')), parts along dimension 0
- grad_filter_first: float32 [3456, 256], P('gx', 'groups'), parts along dimension 1
- grad_filter_second: float32 [3456, 256], P('gx', 'groups'), parts along dimension 1
There are 2 independent parts, one for each index of `groups`. A program takes and returns all parts, laid end to end along the dimension named above; an argument that names none is the same for every part. Nothing has to cross between parts.
All inputs are finite; a program needn't handle non-finite values.
Results may differ from a plain program's by a relative error of at most 0.0058.
Values may be sent and summed in bfloat16 or wider, within the bound.
No kernel may reach another device: no remote copies, remote signals or barrier semaphores. Data moves between devices by JAX's collectives and lax.ppermute only.
A program may use at most 64 MiB of HBM per device.

v0:
```python
import math

import jax
import jax.numpy as jnp
from jax import lax
from jax.sharding import PartitionSpec as P

inv_root_two = 0.7071067811865476
inv_root_twopi = 0.3989422804014327
tap_shifts = ((-1, -1), (-1, 0), (-1, 1), (0, -1), (0, 0), (0, 1), (1, -1), (1, 0), (1, 1))


def with_halo(block, sides, width):
    for axis, dim in sides:
        count = lax.axis_size(axis)
        forward = [(i, i + 1) for i in range(count - 1)]
        backward = [(target, source) for source, target in forward]
        low = lax.ppermute(
            lax.slice_in_dim(block, block.shape[dim] - width, None, axis=dim), axis, forward
        )
        high = lax.ppermute(lax.slice_in_dim(block, 0, width, axis=dim), axis, backward)
        block = jnp.concatenate([low, block, high], axis=dim)
    return block


def gelu_parts(value):
    normal_cdf = 0.5 * (1.0 + lax.erf(value * inv_root_two))
    return (value * normal_cdf, normal_cdf + value * jnp.exp(-0.5 * value * value) * inv_root_twopi)


def pad_sides(extended):
    return jnp.pad(extended, ((0, 0), (1, 1), (1, 1), (0, 0)))


def stack_taps(padded, direction, z_cells):
    return jnp.concatenate(
        [
            padded[:, :, 1 + direction * shift_z : 1 + direction * shift_z + z_cells]
            for shift_z in (-1, 0, 1)
        ],
        axis=3,
    )


def window(stacked, direction, shift_x, shift_y, x_cells, y_cells):
    start_x = 1 + direction * shift_x
    start_y = 1 + direction * shift_y
    return stacked[start_x : start_x + x_cells, start_y : start_y + y_cells]


def back_data(stacked, full_filter, shape):
    x_cells, y_cells, z_cells, channels = shape
    kernel = full_filter.reshape(3, 3, 3, channels, channels)
    running = jnp.zeros((x_cells * y_cells * z_cells, channels), jnp.float32)
    for shift_x, shift_y in tap_shifts:
        tap_matrix = jnp.transpose(kernel[shift_x + 1, shift_y + 1], (0, 2, 1)).reshape(
            3 * channels, channels
        )
        piece = window(stacked, -1, shift_x, shift_y, x_cells, y_cells).reshape(-1, 3 * channels)
        running = running + jnp.dot(piece, tap_matrix, preferred_element_type=jnp.float32)
    return running.reshape(shape)


def filter_from_inputs(stacked, grads, shape):
    x_cells, y_cells, z_cells, channels = shape
    flat_grads = grads.reshape(-1, channels)
    blocks = []
    for shift_x, shift_y in tap_shifts:
        piece = window(stacked, 1, shift_x, shift_y, x_cells, y_cells).reshape(-1, 3 * channels)
        product = lax.dot_general(
            piece, flat_grads, (((0,), (0,)), ((), ())), preferred_element_type=jnp.float32
        )
        blocks.append(product.reshape(3, channels, channels))
    return jnp.stack(blocks).reshape(27 * channels, channels)


def on_device(grad_out, inputs, pre_first, pre_second, filter_first, filter_second):
    shape = grad_out.shape
    x_cells, y_cells, z_cells, channels = shape
    full_first, full_second = (
        lax.all_gather(filter_first, "gx", axis=0, tiled=True),
        lax.all_gather(filter_second, "gx", axis=0, tiled=True),
    )
    grad_scale = 1.0 / math.sqrt(x_cells * lax.axis_size("gx") * y_cells * z_cells)
    unused_value, slope_two = gelu_parts(pre_second.astype(jnp.float32))
    grad_two = (grad_out.astype(jnp.float32) * slope_two).astype(jnp.bfloat16)
    act_one, slope_one = gelu_parts(pre_first.astype(jnp.float32))
    act_one = act_one.astype(jnp.bfloat16)
    extended_two = pad_sides(with_halo(grad_two, (("gx", 0),), 1))
    stacked_two = stack_taps(extended_two, -1, z_cells)
    grad_act = back_data(stacked_two, full_second, shape)
    extended_act = pad_sides(with_halo(act_one, (("gx", 0),), 1))
    filt_two = filter_from_inputs(stack_taps(extended_act, 1, z_cells), grad_two, shape)
    owned_two = lax.psum_scatter(filt_two * grad_scale, "gx", scatter_dimension=0, tiled=True)
    grad_one = (grad_act * slope_one).astype(jnp.bfloat16)
    extended_one = pad_sides(with_halo(grad_one, (("gx", 0),), 1))
    stacked_one = stack_taps(extended_one, -1, z_cells)
    grad_in = back_data(stacked_one, full_first, shape).astype(jnp.bfloat16)
    extended_in = pad_sides(with_halo(inputs, (("gx", 0),), 1))
    filt_one = filter_from_inputs(stack_taps(extended_in, 1, z_cells), grad_one, shape)
    owned_one = lax.psum_scatter(filt_one * grad_scale, "gx", scatter_dimension=0, tiled=True)
    return (grad_in, owned_one, owned_two)


def solution(mesh):
    return jax.shard_map(
        on_device,
        mesh=mesh,
        in_specs=(
            P(("groups", "gx"), None, None, None),
            P(("groups", "gx"), None, None, None),
            P(("groups", "gx"), None, None, None),
            P(("groups", "gx"), None, None, None),
            P("gx", None),
            P("gx", None),
        ),
        out_specs=(P(("groups", "gx"), None, None, None), P("gx", "groups"), P("gx", "groups")),
        check_vma=False,
    )
```

profile of v0, /device:TPU:0, one launch (start us, length us, event | category | flops | bytes accessed | tf_op | source)
XLA Modules:
  0.0 242.4 jit_solution(2197010658242407389)
XLA Ops:
  8.5 2.4 collective-permute-start
  13.2 5.1 %collective-permute-start.4 = (bf16[1,4,128,128]{3,2,1,0:T(8,128)(2,1)S(1)}, bf16[1,4,128,128]{3,2,1,0:T(8,128)(2,1)S(1)}, u32[]{:S(2)}, u32[]{:S(2)}) collective-permute-start(bf16[1,4,128,128]{3,2,1,0:T(8,128)(2,1)S(1)} %get-tuple-element.73), channel_id=1, source_target_pairs={{0,1},{1,2},{2,3},{3,4},{4,5},{5,6},{6,7},{7,8},{8,9},{9,10},{10,1... | collective-permute-start | bytes 393224 | tf_op jit(solution)/shard_map/ppermute | solution.py:18
  19.7 26.8 %all_gather.6 = bf16[3456,128]{1,0:T(8,128)(2,1)S(1)} all-gather(bf16[216,128]{1,0:T(8,128)(2,1)S(1)} %copy-done.16), channel_id=1, replica_groups=mesh['groups'=2,'gx'=16] {'gx'}, dimensions={0}, use_global_device_ids=true | all-gather | bytes 940032 | tf_op jit(solution)/shard_map/all_gather | solution.py:82
  47.8 19.9 %all_gather.7 = bf16[3456,128]{1,0:T(8,128)(2,1)S(1)} all-gather(bf16[216,128]{1,0:T(8,128)(2,1)S(1)} %copy-done.17), channel_id=1, replica_groups=mesh['groups'=2,'gx'=16] {'gx'}, dimensions={0}, use_global_device_ids=true | all-gather | bytes 940032 | tf_op jit(solution)/shard_map/all_gather | solution.py:81
  78.9 2.9 %collective-permute-start.6 = (bf16[1,4,128,128]{3,2,1,0:T(8,128)(2,1)}, bf16[1,4,128,128]{3,2,1,0:T(8,128)(2,1)}, u32[]{:S(2)}, u32[]{:S(2)}) collective-permute-start(bf16[1,4,128,128]{3,2,1,0:T(8,128)(2,1)} %get-tuple-element.69), channel_id=1, source_target_pairs={{0,1},{1,2},{2,3},{3,4},{4,5},{5,6},{6,7},{7,8},{8,9},{9,10},{10,1... | collective-permute-start | bytes 393224 | tf_op jit(solution)/shard_map/ppermute | solution.py:18
  84.4 2.8 %fusion.48 = (bf16[2,4,128,384]{3,2,1,0:T(8,128)(2,1)S(1)}, bf16[2,4,128,384]{3,2,1,0:T(8,128)(2,1)S(1)}, bf16[2,4,128,384]{3,2,1,0:T(8,128)(2,1)S(1)}, bf16[2,4...) fusion(bf16[4,6,128,384]{3,2,1,0:T(8,128)(2,1)S(1)} %pad_maximu, ...), kind=kLoop, calls=%fused_computation.125 | loop fusion | bytes 14155776 | tf_op jit(solution)/shard_map/slice | solution.py:48
  87.2 2.3 copy.99
  89.5 2.3 copy.100
  91.8 2.3 copy.101
  94.1 2.3 copy.102
  96.5 2.3 copy.103
  98.8 2.3 copy.104
  111.0 4.1 %collective-permute-start.2 = (bf16[1,4,128,128]{3,2,1,0:T(8,128)(2,1)}, bf16[1,4,128,128]{3,2,1,0:T(8,128)(2,1)}, u32[]{:S(2)}, u32[]{:S(2)}) collective-permute-start(bf16[1,4,128,128]{3,2,1,0:T(8,128)(2,1)} %get-tuple-element.75), channel_id=1, source_target_pairs={{0,1},{1,2},{2,3},{3,4},{4,5},{5,6},{6,7},{7,8},{8,9},{9,10},{10,1... | collective-permute-start | bytes 393224 | tf_op jit(solution)/shard_map/ppermute | solution.py:18
  118.7 2.8 %fusion.47 = (bf16[2,4,128,384]{3,2,1,0:T(8,128)(2,1)S(1)}, bf16[2,4,128,384]{3,2,1,0:T(8,128)(2,1)S(1)}, bf16[2,4,128,384]{3,2,1,0:T(8,128)(2,1)S(1)}, bf16[2,4...) fusion(bf16[4,6,128,384]{3,2,1,0:T(8,128)(2,1)S(1)} %pad_maximu, ...), kind=kLoop, calls=%fused_computation.124 | loop fusion | bytes 14155776 | tf_op jit(solution)/shard_map/slice | solution.py:48
  121.5 2.4 copy.108
  123.9 2.4 copy.109
  130.7 2.4 copy.110
  133.0 2.3 copy.111
  135.3 2.3 copy.112
  137.6 2.3 copy.113
  143.0 2.3 fusion.10
  152.1 2.9 %broadcast_multiply_fusion = f32[9,3,128,128]{3,2,1,0:T(8,128)} fusion(f32[9,3,128,128]{3,2,1,0:T(8,128)} %fusion.4), kind=kLoop, calls=%fused_computation.73 | loop fusion | flops 442368 | bytes 3538944 | tf_op jit(solution)/shard_map/mul | solution.py:94
  160.9 11.1 %reduce-scatter.7.cloned.1.call-done = f32[216,128]{1,0:T(8,128)} async-done(((f32[3456,128]{1,0:T(8,128)}), f32[216,128]{1,0:T(8,128)}) %reduce-scatter.7.cloned.1.call-update) | async-done | bytes 110608
  172.0 63.5 %reduce-scatter.9.cloned.1.call-done = f32[216,128]{1,0:T(8,128)} async-done(((f32[3456,128]{1,0:T(8,128)}), f32[216,128]{1,0:T(8,128)}) %reduce-scatter.9.cloned.1.call-update) | async-done | bytes 110608
  (134 shorter events, 53.2 us)
Async XLA Ops:
  7.2 12.5 %copy-start.16 = (bf16[216,128]{1,0:T(8,128)(2,1)S(1)}, bf16[216,128]{1,0:T(8,128)(2,1)}, u32[]{:S(2)}) copy-start(bf16[216,128]{1,0:T(8,128)(2,1)} %param.11) | copy-start | bytes 165892
  7.2 164.8 %reduce-scatter.7.cloned.1.call-start = ((), (), s32[]{:S(2)}) async-start(), calls=%async_computation.2 | async-start | bytes 1880064
  8.5 63.5 %collective-permute-start = (bf16[1,4,128,128]{3,2,1,0:T(8,128)(2,1)S(1)}, bf16[1,4,128,128]{3,2,1,0:T(8,128)(2,1)S(1)}, u32[]{:S(2)}, u32[]{:S(2)}) collective-permute-start(bf16[1,4,128,128]{3,2,1,0:T(8,128)(2,1)S(1)} %get-tuple-element.77), channel_id=1, source_target_pairs={{0,1},{1,2},{2,3},{3,4},{4,5},{5,6},{6,7},{7,8},{8,9},{9,10},{10,1... | collective-permute-start | bytes 393224 | tf_op jit(solution)/shard_map/ppermute | solution.py:18
  10.9 61.1 %collective-permute-start.1 = (bf16[1,4,128,128]{3,2,1,0:T(8,128)(2,1)S(1)}, bf16[1,4,128,128]{3,2,1,0:T(8,128)(2,1)S(1)}, u32[]{:S(2)}, u32[]{:S(2)}) collective-permute-start(bf16[1,4,128,128]{3,2,1,0:T(8,128)(2,1)S(1)} %get-tuple-element.78), channel_id=1, source_target_pairs={{1,0},{2,1},{3,2},{4,3},{5,4},{6,5},{7,6},{8,7},{9,8},{10,9},{11,1... | collective-permute-start | bytes 393224 | tf_op jit(solution)/shard_map/ppermute | solution.py:21
  13.2 70.1 %collective-permute-start.4 = (bf16[1,4,128,128]{3,2,1,0:T(8,128)(2,1)S(1)}, bf16[1,4,128,128]{3,2,1,0:T(8,128)(2,1)S(1)}, u32[]{:S(2)}, u32[]{:S(2)}) collective-permute-start(bf16[1,4,128,128]{3,2,1,0:T(8,128)(2,1)S(1)} %get-tuple-element.73), channel_id=1, source_target_pairs={{0,1},{1,2},{2,3},{3,4},{4,5},{5,6},{6,7},{7,8},{8,9},{9,10},{10,1... | collective-permute-start | bytes 393224 | tf_op jit(solution)/shard_map/ppermute | solution.py:18
  18.4 64.9 %collective-permute-start.5 = (bf16[1,4,128,128]{3,2,1,0:T(8,128)(2,1)S(1)}, bf16[1,4,128,128]{3,2,1,0:T(8,128)(2,1)S(1)}, u32[]{:S(2)}, u32[]{:S(2)}) collective-permute-start(bf16[1,4,128,128]{3,2,1,0:T(8,128)(2,1)S(1)} %get-tuple-element.74), channel_id=1, source_target_pairs={{1,0},{2,1},{3,2},{4,3},{5,4},{6,5},{7,6},{8,7},{9,8},{10,9},{11,1... | collective-permute-start | bytes 393224 | tf_op jit(solution)/shard_map/ppermute | solution.py:21
  46.5 1.3 copy-start.17
  77.3 6.0 %copy-start.9 = (bf16[2,4,128,128]{3,2,1,0:T(8,128)(2,1)S(1)}, bf16[2,4,128,128]{3,2,1,0:T(8,128)(2,1)}, u32[]{:S(2)}) copy-start(bf16[2,4,128,128]{3,2,1,0:T(8,128)(2,1)} %param.7) | copy-start | bytes 786436
  78.9 37.7 %collective-permute-start.6 = (bf16[1,4,128,128]{3,2,1,0:T(8,128)(2,1)}, bf16[1,4,128,128]{3,2,1,0:T(8,128)(2,1)}, u32[]{:S(2)}, u32[]{:S(2)}) collective-permute-start(bf16[1,4,128,128]{3,2,1,0:T(8,128)(2,1)} %get-tuple-element.69), channel_id=1, source_target_pairs={{0,1},{1,2},{2,3},{3,4},{4,5},{5,6},{6,7},{7,8},{8,9},{9,10},{10,1... | collective-permute-start | bytes 393224 | tf_op jit(solution)/shard_map/ppermute | solution.py:18
  81.8 34.8 %collective-permute-start.7 = (bf16[1,4,128,128]{3,2,1,0:T(8,128)(2,1)}, bf16[1,4,128,128]{3,2,1,0:T(8,128)(2,1)}, u32[]{:S(2)}, u32[]{:S(2)}) collective-permute-start(bf16[1,4,128,128]{3,2,1,0:T(8,128)(2,1)} %get-tuple-element.70), channel_id=1, source_target_pairs={{1,0},{2,1},{3,2},{4,3},{5,4},{6,5},{7,6},{8,7},{9,8},{10,9},{11,1... | collective-permute-start | bytes 393224 | tf_op jit(solution)/shard_map/ppermute | solution.py:21
  102.8 3.2 %copy-start.8 = (bf16[1024,384]{0,1:T(8,128)(2,1)S(1)}, bf16[1024,384]{0,1:T(8,128)(2,1)}, u32[]{:S(2)}) copy-start(bf16[1024,384]{0,1:T(8,128)(2,1)} %copy.101) | copy-start | bytes 2359300
  102.8 3.6 %copy-start.7 = (bf16[1024,384]{0,1:T(8,128)(2,1)S(1)}, bf16[1024,384]{0,1:T(8,128)(2,1)}, u32[]{:S(2)}) copy-start(bf16[1024,384]{0,1:T(8,128)(2,1)} %copy.102) | copy-start | bytes 2359300
  104.5 2.4 copy-start.6
  106.1 1.2 copy-start.5
  106.5 1.2 copy-start.4
  110.2 125.3 %reduce-scatter.9.cloned.1.call-start = ((), (), s32[]{:S(2)}) async-start(), calls=%async_computation.3 | async-start | bytes 1880064
  111.0 30.7 %collective-permute-start.2 = (bf16[1,4,128,128]{3,2,1,0:T(8,128)(2,1)}, bf16[1,4,128,128]{3,2,1,0:T(8,128)(2,1)}, u32[]{:S(2)}, u32[]{:S(2)}) collective-permute-start(bf16[1,4,128,128]{3,2,1,0:T(8,128)(2,1)} %get-tuple-element.75), channel_id=1, source_target_pairs={{0,1},{1,2},{2,3},{3,4},{4,5},{5,6},{6,7},{7,8},{8,9},{9,10},{10,1... | collective-permute-start | bytes 393224 | tf_op jit(solution)/shard_map/ppermute | solution.py:18
  115.1 26.6 %collective-permute-start.3 = (bf16[1,4,128,128]{3,2,1,0:T(8,128)(2,1)}, bf16[1,4,128,128]{3,2,1,0:T(8,128)(2,1)}, u32[]{:S(2)}, u32[]{:S(2)}) collective-permute-start(bf16[1,4,128,128]{3,2,1,0:T(8,128)(2,1)} %get-tuple-element.76), channel_id=1, source_target_pairs={{1,0},{2,1},{3,2},{4,3},{5,4},{6,5},{7,6},{8,7},{9,8},{10,9},{11,1... | collective-permute-start | bytes 393224 | tf_op jit(solution)/shard_map/ppermute | solution.py:21
  141.7 3.6 %copy-start.3 = (bf16[1024,384]{0,1:T(8,128)(2,1)S(1)}, bf16[1024,384]{0,1:T(8,128)(2,1)}, u32[]{:S(2)}) copy-start(bf16[1024,384]{0,1:T(8,128)(2,1)} %copy.111) | copy-start | bytes 2359300
  141.7 4.6 %copy-start.2 = (bf16[1024,384]{0,1:T(8,128)(2,1)S(1)}, bf16[1024,384]{0,1:T(8,128)(2,1)}, u32[]{:S(2)}) copy-start(bf16[1024,384]{0,1:T(8,128)(2,1)} %copy.112) | copy-start | bytes 2359300
  143.0 4.4 %copy-start.1 = (bf16[1024,384]{0,1:T(8,128)(2,1)S(1)}, bf16[1024,384]{0,1:T(8,128)(2,1)}, u32[]{:S(2)}) copy-start(bf16[1024,384]{0,1:T(8,128)(2,1)} %copy.113) | copy-start | bytes 2359300
  145.3 3.1 %copy-start = (bf16[1024,384]{0,1:T(8,128)(2,1)S(1)}, bf16[1024,384]{0,1:T(8,128)(2,1)}, u32[]{:S(2)}) copy-start(bf16[1024,384]{0,1:T(8,128)(2,1)} %copy.114) | copy-start | bytes 2359300
  155.4 1.2 copy-start.14
  155.4 1.6 copy-start.13
  (4 other events, 3.7 us)
Sparse Core Ops, SparseCore 0:
  110.4 61.6 reduce-scatter.6
  176.4 59.0 reduce-scatter.8
where the time goes:
time: 244 us; the launch traced here: 242 us
  waiting for transfers between devices  74.6 us (31%)
  local copies, waits for them, and re-layouts  49.9 us (20%)
  blocking collectives  46.8 us (19%)
  matrix products  26 us (11%)
  starting transfers between devices  20.1 us (8%)
  between operations  14.8 us (6%)
  other arithmetic  10.1 us (4%)
    unnamed x4, waiting for transfers between devices  74.6 us
    reshape x18, local copies, waits for them, and re-layouts, filter_from_inputs(): window(stacked, 1, shift_x, shift_y, x_cells, y_cells)  31.3 us
    all_gather x1, blocking collectives, on_device(): lax.all_gather(filter_second, 'gx', axis=0, tiled=True)  26.8 us
    all_gather x1, blocking collectives, on_device(): lax.all_gather(filter_first, 'gx', axis=0, tiled=True)  19.9 us
    dot_general x18, matrix products, filter_from_inputs(): lax.dot_general(piece, flat_grads, (((0,), (0,)), ((), ())), preferred_el...  18.8 us
    ppermute x4, starting transfers between devices, with_halo(): lax.ppermute(lax.slice_in_dim(block, block.shape[dim] - width, None, axis...  14.5 us
    slice x4, local copies, waits for them, and re-layouts, window(): return stacked[start_x:start_x + x_cells, start_y:start_y + y_cells]  7.85 us
    dot_general x18, matrix products, back_data(): jnp.dot(piece, tap_matrix, preferred_element_type=jnp.float32)  7.27 us
  transfers between devices with their start and end apart: 10, of which 2 were waited for; matrix products, arithmetic and copies ran while one was open for 35% of the time, Pallas kernels for 0%

commit v1 on v0

v1 whole, which is shorter than its diff:
```python
import functools
import math

import jax
import jax.numpy as jnp
from jax import lax
from jax.experimental import pallas as pl
from jax.experimental.pallas import tpu as pltpu
from jax.sharding import PartitionSpec as P

inv_root_two = 0.7071067811865476
inv_root_twopi = 0.3989422804014327
shifts = (-1, 0, 1)
planes = tuple((a, b) for a in shifts for b in shifts)
bf16, f32 = jnp.bfloat16, jnp.float32
vmem = pl.BlockSpec(memory_space=pltpu.VMEM)
smem = pl.BlockSpec(memory_space=pltpu.SMEM)
vmem_bytes = 50 * 1024 * 1024


def cdf_of(value):
    return 0.5 * (1.0 + lax.erf(value * inv_root_two))


def slope_of(value):
    return cdf_of(value) + value * jnp.exp(-0.5 * value * value) * inv_root_twopi


def value_of(value):
    return value * cdf_of(value)


def shift_rows(block, c):
    rows = block.shape[0]
    if c == 0:
        return block
    place = lax.broadcasted_iota(jnp.int32, block.shape, 0)
    edge = 0 if c == 1 else rows - 1
    return jnp.where(place == edge, 0.0, pltpu.roll(block, c % rows, 0))


def zero_sides(ref):
    layers, wide = ref.shape[:2]
    blank = jnp.zeros(ref.shape[2:], ref.dtype)
    for x in range(layers):
        ref[x, 0] = blank
        ref[x, wide - 1] = blank


def first_grads(grad_out, pre_second, pre_first, own, up, down):
    nx = own.shape[0]
    for x in range(nx):
        for y in range(own.shape[1]):
            slope = slope_of(pre_second[x, y].astype(f32))
            own[x, y] = (grad_out[x, y].astype(f32) * slope).astype(bf16)
    up[0:2] = own[nx - 2 : nx]
    up[2:3] = pre_first[nx - 1 : nx]
    down[0:2] = own[0:2]
    down[2:3] = pre_first[0:1]


def filter_terms(load, padded, first, turned, total, scale):
    nx, ny = padded.shape[0] - 2 * first, padded.shape[1] - 2
    nz, ch = padded.shape[2:]
    for x in range(nx):
        for y in range(ny):
            block = load(x, y)
            for k, c in enumerate(shifts):
                at = (x * ny + y) * nz
                moved = shift_rows(block, -c).astype(bf16)
                turned[k * ch : (k + 1) * ch, at : at + nz] = moved.T
    rows = nx * ny * nz

    def piece(a, b):
        return padded[first - a : first - a + nx, 1 - b : 1 - b + ny].reshape(rows, ch)

    for i in range(0, len(planes), 2):
        pair = planes[i : i + 2]
        right = jnp.concatenate([piece(a, b) for a, b in pair], axis=1)
        part = jnp.dot(turned[...], right, preferred_element_type=f32) * scale
        for j in range(len(pair)):
            total[(i + j) * 3 * ch : (i + j + 1) * 3 * ch] = part[:, j * ch : (j + 1) * ch]


def data_layers(padded, first, weights, finish, out_x):
    ny = padded.shape[1] - 2
    nz, ch = padded.shape[2:]
    rows = ny * nz
    for x in out_x:
        total = None
        for i in range(0, len(planes), 2):
            pair = planes[i : i + 2]
            left = jnp.concatenate(
                [padded[first + x - a, 1 - b : 1 - b + ny].reshape(rows, ch) for a, b in pair], axis=1
            )
            right = jnp.concatenate(
                [weights[(i + j) * 3 * ch : (i + j + 1) * 3 * ch] for j in range(len(pair))], axis=1
            )
            part = lax.dot_general(left, right, (((1,), (1,)), ((), ())), preferred_element_type=f32)
            total = part if total is None else total + part
        for y in range(ny):
            block = total[y * nz : (y + 1) * nz]
            value = sum(shift_rows(block[:, k * ch : (k + 1) * ch], c) for k, c in enumerate(shifts))
            finish(x, y, value)


def split_halves(total, which, kept, sent):
    half, rows = kept.shape[:2]
    for k in range(half):
        kept[k] = total[pl.ds(pl.multiple_of((2 * k + which) * rows, 8), rows)]
        sent[k] = total[pl.ds(pl.multiple_of((2 * k + 1 - which) * rows, 8), rows)].astype(bf16)


def second_filter(spot, pre_first, own, low, high, kept, sent, padded, turned, total, *, scale):
    nx, ny = own.shape[:2]
    zero_sides(padded)
    padded[0, 1 : 1 + ny] = low[1]
    padded[1 : 1 + nx, 1 : 1 + ny] = own[...]
    padded[1 + nx, 1 : 1 + ny] = high[0]

    def load(x, y):
        return value_of(pre_first[x, y].astype(f32)).astype(bf16).astype(f32)

    filter_terms(load, padded, 1, turned, total, scale)
    split_halves(total, lax.rem(spot[0], 2), kept, sent)


def first_filter(spot, pre_first, inputs, own, low, high, weights, kept, sent, wide, padded, turned, total, *, scale):
    nx, ny = own.shape[:2]
    zero_sides(padded)
    padded[0:2, 1 : 1 + ny] = low[0:2]
    padded[2 : 2 + nx, 1 : 1 + ny] = own[...]
    padded[2 + nx : 4 + nx, 1 : 1 + ny] = high[0:2]
    zero_sides(wide)

    def finish(x, y, value):
        if x < 0:
            slope = slope_of(low[2, y].astype(f32))
            value = jnp.where(spot[0] > 0, value * slope, 0.0)
        elif x == nx:
            slope = slope_of(high[2, y].astype(f32))
            value = jnp.where(spot[0] < spot[1] - 1, value * slope, 0.0)
        else:
            value = value * slope_of(pre_first[x, y].astype(f32))
        wide[1 + x, 1 + y] = value.astype(bf16)

    data_layers(padded, 2, weights, finish, range(-1, nx + 1))

    def load(x, y):
        return inputs[x, y].astype(f32)

    filter_terms(load, wide, 1, turned, total, scale)
    split_halves(total, lax.rem(spot[0], 2), kept, sent)


def input_grads(wide, weights, out):
    def finish(x, y, value):
        out[x, y] = value.astype(bf16)

    data_layers(wide, 1, weights, finish, range(out.shape[0]))


def call(body, n_smem, args, outs, scratch=()):
    return pl.pallas_call(
        body,
        in_specs=[smem] * n_smem + [vmem] * (len(args) - n_smem),
        out_specs=[vmem] * len(outs),
        out_shape=[jax.ShapeDtypeStruct(s, d) for s, d in outs],
        scratch_shapes=[pltpu.VMEM(s, d) for s, d in scratch],
        compiler_params=pltpu.CompilerParams(vmem_limit_bytes=vmem_bytes),
    )(*args)


def on_device(grad_out, inputs, pre_first, pre_second, filter_first, filter_second):
    shape = grad_out.shape
    nx, ny, nz, ch = shape
    n = lax.axis_size("gx")
    me = lax.axis_index("gx")
    bits = [1 << k for k in range(n.bit_length() - 1)]
    rows = filter_first.shape[0]
    scale = 1.0 / math.sqrt(nx * n * ny * nz)
    spot = jnp.stack([me, jnp.full((), n, me.dtype)]).astype(jnp.int32)

    def swap(array, bit):
        return lax.ppermute(array, "gx", [(i, i ^ bit) for i in range(n)])

    full = jnp.stack([filter_first, filter_second])
    for bit in reversed(bits):
        other = swap(full, bit)
        low = (me & bit) == 0
        full = jnp.stack([jnp.where(low, full, other), jnp.where(low, other, full)], axis=-3)
    full = full.reshape(2, n * rows, ch)
    full_first, full_second = full[0], full[1]

    grad_two, up, down = call(
        first_grads, 0, (grad_out, pre_second, pre_first), [(shape, bf16)] + [((3,) + shape[1:], bf16)] * 2
    )
    ahead = [(i, i + 1) for i in range(n - 1)]
    low = lax.ppermute(up, "gx", ahead)
    high = lax.ppermute(down, "gx", [(b, a) for a, b in ahead])

    half = [((n // 2, rows, ch), f32), ((n // 2, rows, ch), bf16)]
    work = [((3 * ch, nx * ny * nz), bf16), ((n * rows, ch), f32)]

    def finish_scatter(kept, sent):
        total = kept + swap(sent, 1).astype(f32)
        for bit in bits[1:]:
            view = total.reshape(-1, 2, rows, ch)
            side = (me & bit) // bit
            mine = lax.dynamic_index_in_dim(view, side, 1, False)
            theirs = lax.dynamic_index_in_dim(view, 1 - side, 1, False)
            total = mine + swap(theirs.astype(bf16), bit).astype(f32)
        return total.reshape(rows, ch)

    kept_two, sent_two = call(
        functools.partial(second_filter, scale=scale),
        1,
        (spot, pre_first, grad_two, low, high),
        half,
        [((nx + 2, ny + 2, nz, ch), bf16)] + work,
    )
    owned_two = finish_scatter(kept_two, sent_two)
    kept_one, sent_one, wide = call(
        functools.partial(first_filter, scale=scale),
        1,
        (spot, pre_first, inputs, grad_two, low, high, full_second),
        half + [((nx + 2, ny + 2, nz, ch), bf16)],
        [((nx + 4, ny + 2, nz, ch), bf16)] + work,
    )
    owned_one = finish_scatter(kept_one, sent_one)
    (grad_in,) = call(input_grads, 0, (wide, full_first), [(shape, bf16)])
    return (grad_in, owned_one, owned_two)


def solution(mesh):
    return jax.shard_map(
        on_device,
        mesh=mesh,
        in_specs=(
            P(("groups", "gx"), None, None, None),
            P(("groups", "gx"), None, None, None),
            P(("groups", "gx"), None, None, None),
            P(("groups", "gx"), None, None, None),
            P("gx", None),
            P("gx", None),
        ),
        out_specs=(P(("groups", "gx"), None, None, None), P("gx", "groups"), P("gx", "groups")),
        check_vma=False,
    )
```

time: 244 us -> 78.8 us (0.32)
  local copies, waits for them, and re-layouts: 49.9 us -> 2.61 us
  blocking collectives: 46.8 us -> 0 us
  waiting for transfers between devices: 74.6 us -> 34.1 us
  matrix products: 26 us -> 0 us
  between operations: 14.8 us -> 0.81 us
  Pallas kernels: 0 us -> 10.5 us
    unnamed x4 -> x0, waiting for transfers between devices: 74.6 us -> none
    all_gather x2 -> x0, blocking collectives: 46.8 us -> none  [the longest x1 26.8 us: on_device(): lax.all_gather(filter_second, 'gx', axis=0, tiled=True)]
    ppermute x8 -> x14, waiting for transfers between devices: 0.02 us -> 34.1 us  [the longest x12 34.1 us: swap(): return lax.ppermute(array, 'gx', [(i, i ^ bit) for i in range(n)])]
    reshape x18 -> x0, local copies, waits for them, and re-layouts: 31.3 us -> none  [filter_from_inputs(): window(stacked, 1, shift_x, shift_y, x_cells, y_cells)]
    dot_general x36 -> x0, matrix products: 26 us -> none  [the longest x18 18.8 us: filter_from_inputs(): lax.dot_general(piece, flat_grads, (((0,), (0,)), ((), ())), preferred_el...]
    slice x12 -> x2, local copies, waits for them, and re-layouts: 12.5 us -> 1.06 us  [on_device(): full_first, full_second = (full[0], full[1])]
    pallas_call x0 -> x4, Pallas kernels: none -> 10.5 us  [call(): pl.pallas_call(body, in_specs=[smem] * n_smem + [vmem] * (len(args) - n_s...]
    another operation x0 -> x10, other arithmetic: none -> 6.54 us  [the longest x8 5.61 us: on_device(): jnp.stack([jnp.where(low, full, other), jnp.where(low, other, full)], axi...]
  transfers between devices with their start and end apart: 10 -> 14, of which waited for: 2 -> 8; matrix products, arithmetic and copies ran while one was open for 35% -> 12% of each run, Pallas kernels for 0% -> 13%
where the time goes in v1:
time: 78.8 us; the launch traced here: 78.4 us
  waiting for transfers between devices  34.1 us (43%)
  starting transfers between devices  20 us (25%)
  Pallas kernels  10.5 us (13%)
  other arithmetic  10.3 us (13%)
  local copies, waits for them, and re-layouts  2.61 us (3%)
  between operations  0.81 us (1%)
    ppermute x12, waiting for transfers between devices, swap(): return lax.ppermute(array, 'gx', [(i, i ^ bit) for i in range(n)])  34.1 us
    ppermute x12, starting transfers between devices, swap(): return lax.ppermute(array, 'gx', [(i, i ^ bit) for i in range(n)])  17.4 us
    pallas_call x4, Pallas kernels, call(): pl.pallas_call(body, in_specs=[smem] * n_smem + [vmem] * (len(args) - n_s...  10.5 us
    another operation x8, other arithmetic, on_device(): jnp.stack([jnp.where(low, full, other), jnp.where(low, other, full)], axi...  5.61 us
  transfers between devices with their start and end apart: 14, of which 8 were waited for; matrix products, arithmetic and copies ran while one was open for 12% of the time, Pallas kernels for 13%

profile of v1, /device:TPU:0, one launch (start us, length us, event | category | flops | bytes accessed | tf_op | source)
XLA Modules:
  0.0 78.4 jit_solution(11504878291621857195)
XLA Ops:
  1.5 4.1 %collective-permute-start.2 = (bf16[2,216,128]{2,1,0:T(8,128)(2,1)S(1)}, bf16[2,216,128]{2,1,0:T(8,128)(2,1)S(1)}, u32[]{:S(2)}, u32[]{:S(2)}) collective-permute-start(bf16[2,216,128]{2,1,0:T(8,128)(2,1)S(1)} %pad_maximum_fusion.4), channel_id=1, source_target_pairs={{0,8},{1,9},{2,10},{3,11},{4,12},{5,13},{6,14},{7,15},{8,0},{9,1},... | collective-permute-start | bytes 331784 | tf_op jit(solution)/shard_map/ppermute | solution.py:185
  5.6 5.4 %collective-permute-done.2 = bf16[2,216,128]{2,1,0:T(8,128)(2,1)S(1)} collective-permute-done((bf16[2,216,128]{2,1,0:T(8,128)(2,1)S(1)}, bf16[2,216,128]{2,1,0:T(8,128)(2,1)S(1)}, u32[]{:S(2)}, u32[]{:S(2)}) %collective-permute-start.2) | collective-permute-done | bytes 110624 | tf_op jit(solution)/shard_map/ppermute | solution.py:185
  12.7 5.9 %collective-permute-done.3 = bf16[2,2,216,128]{3,2,0,1:T(8,128)(2,1)S(1)} collective-permute-done((bf16[2,2,216,128]{3,2,0,1:T(8,128)(2,1)S(1)}, bf16[2,2,216,128]{3,2,0,1:T(8,128)(2,1)S(1)}, u32[]{:S(2)}, u32[]{:S(2)}) %collective-permute-start.3) | collective-permute-done | bytes 221216 | tf_op jit(solution)/shard_map/ppermute | solution.py:185
  19.3 1.2 %collective-permute-start.4 = (bf16[2,2,2,216,128]{4,3,0,1,2:T(8,128)(2,1)S(1)}, bf16[2,2,2,216,128]{4,3,0,1,2:T(8,128)(2,1)}, u32[]{:S(2)}, u32[]{:S(2)}) collective-permute-start(bf16[2,2,2,216,128]{4,3,0,1,2:T(8,128)(2,1)S(1)} %pad_maximum_fusion.2), channel_id=1, source_target_pairs={{0,2},{1,3},{2,0},{3,1},{4,6},{5,7},{6,4},{7,5},{8,10},{9,11},{10,... | collective-permute-start | bytes 1327112 | tf_op jit(solution)/shard_map/ppermute | solution.py:185
  20.9 1.3 %collective-permute-start = (bf16[3,4,128,128]{3,2,1,0:T(8,128)(2,1)S(1)}, bf16[3,4,128,128]{3,2,1,0:T(8,128)(2,1)S(1)}, u32[]{:S(2)}, u32[]{:S(2)}) collective-permute-start(bf16[3,4,128,128]{3,2,1,0:T(8,128)(2,1)S(1)} %get-tuple-element.12), channel_id=1, source_target_pairs={{0,1},{1,2},{2,3},{3,4},{4,5},{5,6},{6,7},{7,8},{8,9},{9,10},{10,1... | collective-permute-start | bytes 1179656 | tf_op jit(solution)/shard_map/ppermute | solution.py:199
  22.2 1.3 %collective-permute-start.1 = (bf16[3,4,128,128]{3,2,1,0:T(8,128)(2,1)S(1)}, bf16[3,4,128,128]{3,2,1,0:T(8,128)(2,1)S(1)}, u32[]{:S(2)}, u32[]{:S(2)}) collective-permute-start(bf16[3,4,128,128]{3,2,1,0:T(8,128)(2,1)S(1)} %get-tuple-element.13), channel_id=1, source_target_pairs={{1,0},{2,1},{3,2},{4,3},{5,4},{6,5},{7,6},{8,7},{9,8},{10,9},{11,1... | collective-permute-start | bytes 1179656 | tf_op jit(solution)/shard_map/ppermute | solution.py:200
  23.5 11.9 %collective-permute-done.4 = bf16[2,2,2,216,128]{4,3,0,1,2:T(8,128)(2,1)} collective-permute-done((bf16[2,2,2,216,128]{4,3,0,1,2:T(8,128)(2,1)S(1)}, bf16[2,2,2,216,128]{4,3,0,1,2:T(8,128)(2,1)}, u32[]{:S(2)}, u32[]{:S(2)}) %collective-permute-start.4) | collective-permute-done | bytes 442400 | tf_op jit(solution)/shard_map/ppermute | solution.py:185
  35.4 1.1 %select_bitcast_fusion.3 = (bf16[2,2,2,1,216,128]{5,4,0,1,2,3:T(8,128)(2,1)S(1)}, bf16[2,2,2,1,216,128]{5,4,0,1,2,3:T(8,128)(2,1)S(1)}) fusion(bf16[2,2,2,216,128]{4,3,0,1,2:T(8,128)(2,1)} %collective-permute-done.4, pred[]{:T(512)S(6)} %eq.13, bf16[2,2,1,216,128]{4,3,0,1,2:T(8,128)(2,1)} %copy-done.8, bf16[2,2,1,216,128]{4,3,0,1,2:T(8,128)(2,1)S(1)} %get-tuple-element.25), kind=kLoop, calls=%fused_computation.15 | loop fusion | flops 663552 | bytes 1769473 | tf_op jit(solution)/shard_map/stack | solution.py:191
  36.6 1.1 %pad_maximum_fusion.1 = bf16[2,2,2,2,216,128]{5,4,0,1,2,3:T(8,128)(2,1)} fusion(bf16[2,2,2,1,216,128]{5,4,0,1,2,3:T(8,128)(2,1)S(1)} %get-tuple-element.24, bf16[2,2,2,1,216,128]{5,4,0,1,2,3:T(8,128)(2,1)S(1)} %get-tuple-element.23), kind=kLoop, calls=%fused_computation.4 | loop fusion | flops 442368 | bytes 1769472 | tf_op jit(solution)/shard_map/stack | solution.py:191
  37.7 2.3 %shard_map.88 = (f32[8,216,128]{2,1,0:T(8,128)S(1)}, bf16[8,216,128]{2,1,0:T(8,128)(2,1)S(1)}) custom-call(s32[2]{0:T(128)S(1)} %pad_add_fusion.spot, bf16[2,4,128,128]{3,2,1,0:T(8,128)(2,1)S(1)} %copy-done, bf16[2,4,128,128]{3,2,1,0:T(8,128)(2,1)S(1)} %get-tuple-element.11.own, bf16[3,4,128,128]{3,2,1,0:T(8,128)(2,1)S(1)} %collective-permute-done.low, ...), custom_call_target="tpu_custom_call" | custom-call | tf_op jit(solution)/shard_map/pallas_call | solution.py:164
  40.6 1.6 %collective-permute-done.10 = bf16[8,216,128]{2,1,0:T(8,128)(2,1)} collective-permute-done((bf16[8,216,128]{2,1,0:T(8,128)(2,1)S(1)}, bf16[8,216,128]{2,1,0:T(8,128)(2,1)}, u32[]{:S(2)}, u32[]{:S(2)}) %collective-permute-start.10) | collective-permute-done | bytes 442400 | tf_op jit(solution)/shard_map/ppermute | solution.py:185
  42.1 1.1 %convert_add_fusion = f32[8,216,128]{2,1,0:T(8,128)S(1)} fusion(f32[8,216,128]{2,1,0:T(8,128)S(1)} %get-tuple-element.17, bf16[8,216,128]{2,1,0:T(8,128)(2,1)} %collective-permute-done.10), kind=kLoop, calls=%fused_computation.5 | loop fusion | flops 442368 | bytes 2211840 | tf_op jit(solution)/shard_map/add | solution.py:206
  44.0 2.6 %collective-permute-start.11 = (bf16[4,216,128]{2,1,0:T(8,128)(2,1)}, bf16[4,216,128]{2,1,0:T(8,128)(2,1)}, u32[]{:S(2)}, u32[]{:S(2)}) collective-permute-start(bf16[4,216,128]{2,1,0:T(8,128)(2,1)} %fusion.2), channel_id=1, source_target_pairs={{0,2},{1,3},{2,0},{3,1},{4,6},{5,7},{6,4},{7,5},{8,10},{9,11},{10,... | collective-permute-start | bytes 663560 | tf_op jit(solution)/shard_map/ppermute | solution.py:185
  46.7 1.3 %select_bitcast_fusion = (bf16[2,2,2,2,1,216,128]{6,5,0,1,2,3,4:T(8,128)(2,1)S(1)}, bf16[2,2,2,2,1,216,128]{6,5,0,1,2,3,4:T(8,128)(2,1)S(1)}) fusion(bf16[2,2,2,2,216,128]{5,4,0,1,2,3:T(8,128)(2,1)} %collective-permute-done.5, pred[]{:T(512)S(6)} %eq.12, bf16[2,2,2,1,216,128]{5,4,0,1,2,3:T(8,128)(2,1)S(1)} %copy-done.5, ...), kind=kLoop, calls=%fused_computation.7 | loop fusion | flops 1327104 | bytes 3538945 | tf_op jit(solution)/shard_map/stack | solution.py:191
  48.0 1.1 %pad_maximum_fusion = (bf16[1,2,2,2,2,216,128]{6,5,0,1,2,3,4:T(8,128)(2,1)}, bf16[1,2,2,2,2,216,128]{6,5,0,1,2,3,4:T(8,128)(2,1)S(1)}) fusion(bf16[2,2,2,2,1,216,128]{6,5,0,1,2,3,4:T(8,128)(2,1)S(1)} %get-tuple-element.21, bf16[2,2,2,2,1,216,128]{6,5,0,1,2,3,4:T(8,128)(2,1)S(1)} %get-tuple-element.22), kind=kLoop, calls=%fused_computation.3 | loop fusion | flops 884736 | bytes 3538944 | tf_op jit(solution)/shard_map/stack | solution.py:191
  50.1 5.7 %shard_map.86 = (f32[8,216,128]{2,1,0:T(8,128)S(1)}, bf16[8,216,128]{2,1,0:T(8,128)(2,1)S(1)}, bf16[4,6,128,128]{3,2,1,0:T(8,128)(2,1)S(1)}) custom-call(s32[2]{0:T(128)S(1)} %pad_add_fusion.spot, bf16[2,4,128,128]{3,2,1,0:T(8,128)(2,1)S(1)} %copy-done, bf16[2,4,128,128]{3,2,1,0:T(8,128)(2,1)S(1)} %copy-done.3, ...), custom_call_target="tpu_custom_call" | custom-call | tf_op jit(solution)/shard_map/pallas_call | solution.py:164
  56.0 1.2 %bitcast_add_fusion = f32[4,216,128]{2,1,0:T(8,128)S(1)} fusion(bf16[4,216,128]{2,1,0:T(8,128)(2,1)} %collective-permute-done.11, f32[4,2,216,128]{3,2,1,0:T(8,128)} %bitcast.56, s32[]{:T(128)S(6)} %select_n.102), kind=kLoop, calls=%fused_computation.12 | loop fusion | flops 221184 | bytes 1105924 | tf_op jit(solution)/shard_map/add | solution.py:212
  57.2 1.8 %collective-permute-start.12 = (bf16[2,216,128]{2,1,0:T(8,128)(2,1)S(1)}, bf16[2,216,128]{2,1,0:T(8,128)(2,1)S(1)}, u32[]{:S(2)}, u32[]{:S(2)}) collective-permute-start(bf16[2,216,128]{2,1,0:T(8,128)(2,1)S(1)} %fusion.4), channel_id=1, source_target_pairs={{0,4},{1,5},{2,6},{3,7},{4,0},{5,1},{6,2},{7,3},{8,12},{9,13},{10,... | collective-permute-start | bytes 331784 | tf_op jit(solution)/shard_map/ppermute | solution.py:185
  59.7 3.0 %collective-permute-done.12 = bf16[2,216,128]{2,1,0:T(8,128)(2,1)S(1)} collective-permute-done((bf16[2,216,128]{2,1,0:T(8,128)(2,1)S(1)}, bf16[2,216,128]{2,1,0:T(8,128)(2,1)S(1)}, u32[]{:S(2)}, u32[]{:S(2)}) %collective-permute-start.12) | collective-permute-done | bytes 110624 | tf_op jit(solution)/shard_map/ppermute | solution.py:185
  62.7 4.0 %collective-permute-done.7 = bf16[4,216,128]{2,1,0:T(8,128)(2,1)S(1)} collective-permute-done((bf16[4,216,128]{2,1,0:T(8,128)(2,1)S(1)}, bf16[4,216,128]{2,1,0:T(8,128)(2,1)S(1)}, u32[]{:S(2)}, u32[]{:S(2)}) %collective-permute-start.7) | collective-permute-done | bytes 221216 | tf_op jit(solution)/shard_map/ppermute | solution.py:185
  67.2 3.4 %collective-permute-start.13 = (bf16[1,216,128]{2,1,0:T(8,128)(2,1)S(1)}, bf16[1,216,128]{2,1,0:T(8,128)(2,1)S(1)}, u32[]{:S(2)}, u32[]{:S(2)}) collective-permute-start(bf16[1,216,128]{2,1,0:T(8,128)(2,1)S(1)} %dynamic-slice_convert_fusion.2), channel_id=1, source_target_pairs={{0,8},{1,9},{2,10},{3,11},{4,12},{5,13},{6,14},{7,15},{8,0},{9,1},... | collective-permute-start | bytes 165896 | tf_op jit(solution)/shard_map/ppermute | solution.py:185
  70.7 1.5 %collective-permute-done.8 = bf16[2,216,128]{2,1,0:T(8,128)(2,1)S(1)} collective-permute-done((bf16[2,216,128]{2,1,0:T(8,128)(2,1)S(1)}, bf16[2,216,128]{2,1,0:T(8,128)(2,1)S(1)}, u32[]{:S(2)}, u32[]{:S(2)}) %collective-permute-start.8) | collective-permute-done | bytes 110624 | tf_op jit(solution)/shard_map/ppermute | solution.py:185
  72.2 1.7 %collective-permute-start.9 = (bf16[1,216,128]{2,1,0:T(8,128)(2,1)S(1)}, bf16[1,216,128]{2,1,0:T(8,128)(2,1)S(1)}, u32[]{:S(2)}, u32[]{:S(2)}) collective-permute-start(bf16[1,216,128]{2,1,0:T(8,128)(2,1)S(1)} %dynamic-slice_convert_fusion.3), channel_id=1, source_target_pairs={{0,8},{1,9},{2,10},{3,11},{4,12},{5,13},{6,14},{7,15},{8,0},{9,1},... | collective-permute-start | bytes 165896 | tf_op jit(solution)/shard_map/ppermute | solution.py:185
  74.7 2.2 %shard_map.87 = bf16[2,4,128,128]{3,2,1,0:T(8,128)(2,1)} custom-call(bf16[4,6,128,128]{3,2,1,0:T(8,128)(2,1)S(1)} %get-tuple-element.14.wide, bf16[3456,128]{1,0:T(8,128)(2,1)S(1)} %bitcast.53), custom_call_target="tpu_custom_call" | custom-call | tf_op jit(solution)/shard_map/pallas_call | solution.py:164
  (52 shorter events, 9.8 us)
Async XLA Ops:
  1.5 9.5 %collective-permute-start.2 = (bf16[2,216,128]{2,1,0:T(8,128)(2,1)S(1)}, bf16[2,216,128]{2,1,0:T(8,128)(2,1)S(1)}, u32[]{:S(2)}, u32[]{:S(2)}) collective-permute-start(bf16[2,216,128]{2,1,0:T(8,128)(2,1)S(1)} %pad_maximum_fusion.4), channel_id=1, source_target_pairs={{0,8},{1,9},{2,10},{3,11},{4,12},{5,13},{6,14},{7,15},{8,0},{9,1},... | collective-permute-start | bytes 331784 | tf_op jit(solution)/shard_map/ppermute | solution.py:185
  11.9 6.7 %collective-permute-start.3 = (bf16[2,2,216,128]{3,2,0,1:T(8,128)(2,1)S(1)}, bf16[2,2,216,128]{3,2,0,1:T(8,128)(2,1)S(1)}, u32[]{:S(2)}, u32[]{:S(2)}) collective-permute-start(bf16[2,2,216,128]{3,2,0,1:T(8,128)(2,1)S(1)} %pad_maximum_fusion.3), channel_id=1, source_target_pairs={{0,4},{1,5},{2,6},{3,7},{4,0},{5,1},{6,2},{7,3},{8,12},{9,13},{10,... | collective-permute-start | bytes 663560 | tf_op jit(solution)/shard_map/ppermute | solution.py:185
  12.7 7.9 %copy-start = (bf16[2,4,128,128]{3,2,1,0:T(8,128)(2,1)S(1)}, bf16[2,4,128,128]{3,2,1,0:T(8,128)(2,1)}, u32[]{:S(2)}) copy-start(bf16[2,4,128,128]{3,2,1,0:T(8,128)(2,1)} %pre_first.5) | copy-start | bytes 786436
  12.7 7.9 %copy-start.1 = (bf16[2,4,128,128]{3,2,1,0:T(8,128)(2,1)S(1)}, bf16[2,4,128,128]{3,2,1,0:T(8,128)(2,1)}, u32[]{:S(2)}) copy-start(bf16[2,4,128,128]{3,2,1,0:T(8,128)(2,1)} %grad_out.1) | copy-start | bytes 786436
  12.7 7.9 %copy-start.2 = (bf16[2,4,128,128]{3,2,1,0:T(8,128)(2,1)S(1)}, bf16[2,4,128,128]{3,2,1,0:T(8,128)(2,1)}, u32[]{:S(2)}) copy-start(bf16[2,4,128,128]{3,2,1,0:T(8,128)(2,1)} %pre_second.1) | copy-start | bytes 786436
  18.6 0.7 copy-start.8
  19.3 16.1 %collective-permute-start.4 = (bf16[2,2,2,216,128]{4,3,0,1,2:T(8,128)(2,1)S(1)}, bf16[2,2,2,216,128]{4,3,0,1,2:T(8,128)(2,1)}, u32[]{:S(2)}, u32[]{:S(2)}) collective-permute-start(bf16[2,2,2,216,128]{4,3,0,1,2:T(8,128)(2,1)S(1)} %pad_maximum_fusion.2), channel_id=1, source_target_pairs={{0,2},{1,3},{2,0},{3,1},{4,6},{5,7},{6,4},{7,5},{8,10},{9,11},{10,... | collective-permute-start | bytes 1327112 | tf_op jit(solution)/shard_map/ppermute | solution.py:185
  20.9 16.8 %collective-permute-start = (bf16[3,4,128,128]{3,2,1,0:T(8,128)(2,1)S(1)}, bf16[3,4,128,128]{3,2,1,0:T(8,128)(2,1)S(1)}, u32[]{:S(2)}, u32[]{:S(2)}) collective-permute-start(bf16[3,4,128,128]{3,2,1,0:T(8,128)(2,1)S(1)} %get-tuple-element.12), channel_id=1, source_target_pairs={{0,1},{1,2},{2,3},{3,4},{4,5},{5,6},{6,7},{7,8},{8,9},{9,10},{10,1... | collective-permute-start | bytes 1179656 | tf_op jit(solution)/shard_map/ppermute | solution.py:199
  22.2 15.5 %collective-permute-start.1 = (bf16[3,4,128,128]{3,2,1,0:T(8,128)(2,1)S(1)}, bf16[3,4,128,128]{3,2,1,0:T(8,128)(2,1)S(1)}, u32[]{:S(2)}, u32[]{:S(2)}) collective-permute-start(bf16[3,4,128,128]{3,2,1,0:T(8,128)(2,1)S(1)} %get-tuple-element.13), channel_id=1, source_target_pairs={{1,0},{2,1},{3,2},{4,3},{5,4},{6,5},{7,6},{8,7},{9,8},{10,9},{11,1... | collective-permute-start | bytes 1179656 | tf_op jit(solution)/shard_map/ppermute | solution.py:200
  36.5 1.1 %copy-start.4 = (bf16[2,2,2,1,216,128]{5,4,0,1,2,3:T(8,128)(2,1)}, bf16[2,2,2,1,216,128]{5,4,0,1,2,3:T(8,128)(2,1)S(1)}, u32[]{:S(2)}) copy-start(bf16[2,2,2,1,216,128]{5,4,0,1,2,3:T(8,128)(2,1)S(1)} %get-tuple-element.24) | copy-start | bytes 1327108
  37.6 9.0 %collective-permute-start.5 = (bf16[2,2,2,2,216,128]{5,4,0,1,2,3:T(8,128)(2,1)}, bf16[2,2,2,2,216,128]{5,4,0,1,2,3:T(8,128)(2,1)}, u32[]{:S(2)}, u32[]{:S(2)}) collective-permute-start(bf16[2,2,2,2,216,128]{5,4,0,1,2,3:T(8,128)(2,1)} %pad_maximum_fusion.1), channel_id=1, source_target_pairs={{0,1},{1,0},{2,3},{3,2},{4,5},{5,4},{6,7},{7,6},{8,9},{9,8},{10,11... | collective-permute-start | bytes 2654216 | tf_op jit(solution)/shard_map/ppermute | solution.py:185
  40.0 2.1 %collective-permute-start.10 = (bf16[8,216,128]{2,1,0:T(8,128)(2,1)S(1)}, bf16[8,216,128]{2,1,0:T(8,128)(2,1)}, u32[]{:S(2)}, u32[]{:S(2)}) collective-permute-start(bf16[8,216,128]{2,1,0:T(8,128)(2,1)S(1)} %get-tuple-element.18), channel_id=1, source_target_pairs={{0,1},{1,0},{2,3},{3,2},{4,5},{5,4},{6,7},{7,6},{8,9},{9,8},{10,11... | collective-permute-start | bytes 1327112 | tf_op jit(solution)/shard_map/ppermute | solution.py:185
  42.1 4.5 %copy-start.5 = (bf16[2,2,2,1,216,128]{5,4,0,1,2,3:T(8,128)(2,1)S(1)}, bf16[2,2,2,1,216,128]{5,4,0,1,2,3:T(8,128)(2,1)}, u32[]{:S(2)}) copy-start(bf16[2,2,2,1,216,128]{5,4,0,1,2,3:T(8,128)(2,1)} %copy-done.4) | copy-start | bytes 1327108
  43.3 3.4 %copy-start.7 = (f32[8,216,128]{2,1,0:T(8,128)}, f32[8,216,128]{2,1,0:T(8,128)S(1)}, u32[]{:S(2)}) copy-start(f32[8,216,128]{2,1,0:T(8,128)S(1)} %convert_add_fusion) | copy-start | bytes 2654212
  44.0 12.0 %collective-permute-start.11 = (bf16[4,216,128]{2,1,0:T(8,128)(2,1)}, bf16[4,216,128]{2,1,0:T(8,128)(2,1)}, u32[]{:S(2)}, u32[]{:S(2)}) collective-permute-start(bf16[4,216,128]{2,1,0:T(8,128)(2,1)} %fusion.2), channel_id=1, source_target_pairs={{0,2},{1,3},{2,0},{3,1},{4,6},{5,7},{6,4},{7,5},{8,10},{9,11},{10,... | collective-permute-start | bytes 663560 | tf_op jit(solution)/shard_map/ppermute | solution.py:185
  49.1 1.0 %copy-start.3 = (bf16[2,4,128,128]{3,2,1,0:T(8,128)(2,1)S(1)}, bf16[2,4,128,128]{3,2,1,0:T(8,128)(2,1)}, u32[]{:S(2)}) copy-start(bf16[2,4,128,128]{3,2,1,0:T(8,128)(2,1)} %inputs.1) | copy-start | bytes 786436
  55.8 3.1 %collective-permute-start.6 = (bf16[8,216,128]{2,1,0:T(8,128)(2,1)S(1)}, bf16[8,216,128]{2,1,0:T(8,128)(2,1)S(1)}, u32[]{:S(2)}, u32[]{:S(2)}) collective-permute-start(bf16[8,216,128]{2,1,0:T(8,128)(2,1)S(1)} %get-tuple-element.16), channel_id=1, source_target_pairs={{0,1},{1,0},{2,3},{3,2},{4,5},{5,4},{6,7},{7,6},{8,9},{9,8},{10,11... | collective-permute-start | bytes 1327112 | tf_op jit(solution)/shard_map/ppermute | solution.py:185
  57.2 5.5 %collective-permute-start.12 = (bf16[2,216,128]{2,1,0:T(8,128)(2,1)S(1)}, bf16[2,216,128]{2,1,0:T(8,128)(2,1)S(1)}, u32[]{:S(2)}, u32[]{:S(2)}) collective-permute-start(bf16[2,216,128]{2,1,0:T(8,128)(2,1)S(1)} %fusion.4), channel_id=1, source_target_pairs={{0,4},{1,5},{2,6},{3,7},{4,0},{5,1},{6,2},{7,3},{8,12},{9,13},{10,... | collective-permute-start | bytes 331784 | tf_op jit(solution)/shard_map/ppermute | solution.py:185
  59.1 7.5 %collective-permute-start.7 = (bf16[4,216,128]{2,1,0:T(8,128)(2,1)S(1)}, bf16[4,216,128]{2,1,0:T(8,128)(2,1)S(1)}, u32[]{:S(2)}, u32[]{:S(2)}) collective-permute-start(bf16[4,216,128]{2,1,0:T(8,128)(2,1)S(1)} %fusion.1), channel_id=1, source_target_pairs={{0,2},{1,3},{2,0},{3,1},{4,6},{5,7},{6,4},{7,5},{8,10},{9,11},{10,... | collective-permute-start | bytes 663560 | tf_op jit(solution)/shard_map/ppermute | solution.py:185
  66.7 7.9 %copy-start.6 = (bf16[1,2,2,2,2,216,128]{6,5,0,1,2,3,4:T(8,128)(2,1)S(1)}, bf16[1,2,2,2,2,216,128]{6,5,0,1,2,3,4:T(8,128)(2,1)}, u32[]{:S(2)}) copy-start(bf16[1,2,2,2,2,216,128]{6,5,0,1,2,3,4:T(8,128)(2,1)} %get-tuple-element.19) | copy-start | bytes 2654212
  66.7 5.4 %collective-permute-start.8 = (bf16[2,216,128]{2,1,0:T(8,128)(2,1)S(1)}, bf16[2,216,128]{2,1,0:T(8,128)(2,1)S(1)}, u32[]{:S(2)}, u32[]{:S(2)}) collective-permute-start(bf16[2,216,128]{2,1,0:T(8,128)(2,1)S(1)} %fusion.3), channel_id=1, source_target_pairs={{0,4},{1,5},{2,6},{3,7},{4,0},{5,1},{6,2},{7,3},{8,12},{9,13},{10,... | collective-permute-start | bytes 331784 | tf_op jit(solution)/shard_map/ppermute | solution.py:185
  67.2 6.7 %collective-permute-start.13 = (bf16[1,216,128]{2,1,0:T(8,128)(2,1)S(1)}, bf16[1,216,128]{2,1,0:T(8,128)(2,1)S(1)}, u32[]{:S(2)}, u32[]{:S(2)}) collective-permute-start(bf16[1,216,128]{2,1,0:T(8,128)(2,1)S(1)} %dynamic-slice_convert_fusion.2), channel_id=1, source_target_pairs={{0,8},{1,9},{2,10},{3,11},{4,12},{5,13},{6,14},{7,15},{8,0},{9,1},... | collective-permute-start | bytes 165896 | tf_op jit(solution)/shard_map/ppermute | solution.py:185
  72.2 5.5 %collective-permute-start.9 = (bf16[1,216,128]{2,1,0:T(8,128)(2,1)S(1)}, bf16[1,216,128]{2,1,0:T(8,128)(2,1)S(1)}, u32[]{:S(2)}, u32[]{:S(2)}) collective-permute-start(bf16[1,216,128]{2,1,0:T(8,128)(2,1)S(1)} %dynamic-slice_convert_fusion.3), channel_id=1, source_target_pairs={{0,8},{1,9},{2,10},{3,11},{4,12},{5,13},{6,14},{7,15},{8,0},{9,1},... | collective-permute-start | bytes 165896 | tf_op jit(solution)/shard_map/ppermute | solution.py:185

commit v2 on v1

v2 whole, which is shorter than its diff:
```python
import functools
import math

import jax
import jax.numpy as jnp
from jax import lax
from jax.experimental import pallas as pl
from jax.experimental.pallas import tpu as pltpu
from jax.sharding import PartitionSpec as P

inv_root_two = 0.7071067811865476
inv_root_twopi = 0.3989422804014327
shifts = (-1, 0, 1)
planes = tuple((a, b) for a in shifts for b in shifts)
bf16, f32 = jnp.bfloat16, jnp.float32
vmem = pl.BlockSpec(memory_space=pltpu.VMEM)
smem = pl.BlockSpec(memory_space=pltpu.SMEM)
anywhere = pl.BlockSpec(memory_space=pl.ANY)
vmem_bytes = 14 * 1024 * 1024


def cdf_of(value):
    return 0.5 * (1.0 + lax.erf(value * inv_root_two))


def slope_of(value):
    return cdf_of(value) + value * jnp.exp(-0.5 * value * value) * inv_root_twopi


def value_of(value):
    return value * cdf_of(value)


def shift_rows(block, c):
    rows = block.shape[0]
    if c == 0:
        return block
    place = lax.broadcasted_iota(jnp.int32, block.shape, 0)
    edge = 0 if c == 1 else rows - 1
    return jnp.where(place == edge, 0.0, pltpu.roll(block, c % rows, 0))


def zero_sides(ref):
    layers, wide = ref.shape[:2]
    blank = jnp.zeros(ref.shape[2:], ref.dtype)
    for x in range(layers):
        ref[x, 0] = blank
        ref[x, wide - 1] = blank


def first_grads(spot, grad_out, pre_second, inputs, own, near, far):
    nx = own.shape[0]
    for x in range(nx):
        for y in range(own.shape[1]):
            slope = slope_of(pre_second[x, y].astype(f32))
            own[x, y] = (grad_out[x, y].astype(f32) * slope).astype(bf16)
    send_edges(spot, own, near, far)
    at = near_edge(spot, nx - 1)
    near[1] = inputs[at]
    far[1] = inputs[nx - 1 - at]


def near_edge(spot, last):
    return last * (1 - spot[2])


def send_edges(spot, own, near, far):
    last = own.shape[0] - 1
    at = near_edge(spot, last)
    near[0] = own[at]
    far[0] = own[last - at]


def filter_terms(turned, padded, emit, scale):
    nx, ny = padded.shape[0] - 2, padded.shape[1] - 2
    nz, ch = padded.shape[2:]
    rows = nx * ny * nz

    def piece(a, b):
        return padded[1 - a : 1 - a + nx, 1 - b : 1 - b + ny].reshape(rows, ch)

    for i in range(0, len(planes), 2):
        pair = planes[i : i + 2]
        right = jnp.concatenate([piece(a, b) for a, b in pair], axis=1)
        part = jnp.dot(turned[...], right, preferred_element_type=f32) * scale
        for j in range(len(pair)):
            emit(i + j, part[:, j * ch : (j + 1) * ch])


def prepare(pre_first, inputs, turned, turned_own, slope):
    nx, ny, nz, ch = pre_first.shape
    for x in range(nx):
        for y in range(ny):
            value = pre_first[x, y].astype(f32)
            slope[x, y] = slope_of(value)
            block = value_of(value).astype(bf16).astype(f32)
            at = (x * ny + y) * nz
            for k, c in enumerate(shifts):
                turned[k * ch : (k + 1) * ch, at : at + nz] = shift_rows(block, -c).T.astype(bf16)
            turned_own[x, y] = inputs[x, y].astype(f32).T.astype(bf16)


def stack_turned(stacked, turned_own, turned_sides):
    nx, ny, ch, nz = turned_own.shape
    blank = jnp.zeros((ch, nz), bf16)
    for i, (a, b) in enumerate(planes):
        for x in range(nx):
            for y in range(ny):
                if 0 <= y + b < ny:
                    inside = 0 <= x + a < nx
                    block = turned_own[x + a, y + b] if inside else turned_sides[int(x + a == nx), y + b]
                else:
                    block = blank
                at = (x * ny + y) * nz
                stacked[i * ch : (i + 1) * ch, at : at + nz] = block


def data_layers(padded, weights, finish, out_x):
    ny = padded.shape[1] - 2
    nz, ch = padded.shape[2:]
    rows = ny * nz
    for x in out_x:
        total = None
        for i in range(0, len(planes), 2):
            pair = planes[i : i + 2]
            left = jnp.concatenate(
                [padded[1 + x - a, 1 - b : 1 - b + ny].reshape(rows, ch) for a, b in pair], axis=1
            )
            right = jnp.concatenate([weights(i + j) for j in range(len(pair))], axis=1)
            part = lax.dot_general(left, right, (((1,), (1,)), ((), ())), preferred_element_type=f32)
            total = part if total is None else total + part
        for y in range(ny):
            block = total[y * nz : (y + 1) * nz]
            value = sum(shift_rows(block[:, k * ch : (k + 1) * ch], c) for k, c in enumerate(shifts))
            finish(x, y, value)


def fill_padded(spot, padded, own, near, far):
    nx, ny = own.shape[:2]
    zero_sides(padded)
    padded[1 : 1 + nx, 1 : 1 + ny] = own[...]
    at = near_edge(spot, nx + 1)
    padded[at, 1 : 1 + ny] = near[0]
    padded[nx + 1 - at, 1 : 1 + ny] = far[0]


def split_halves(total, side, kept, sent):
    half, rows = kept.shape[:2]
    for k in range(half):
        kept[k] = total[pl.ds(pl.multiple_of((2 * k + side) * rows, 8), rows)]
        sent[k] = total[pl.ds(pl.multiple_of((2 * k + 1 - side) * rows, 8), rows)].astype(bf16)


def plain_weights(full):
    ch = full.shape[1]
    return lambda plane: full[plane * 3 * ch : (plane + 1) * 3 * ch]


def placed_weights(spot, masks, mine, theirs, pairs):
    even = spot[2] == 0
    for mask, first, second in zip(masks, mine, theirs):
        one, two = first[...].astype(f32), second[...].astype(f32)
        both = jnp.concatenate([jnp.where(even, one, two), jnp.where(even, two, one)], axis=0)
        pairs[lax.bitwise_xor(spot[0] // 2, mask // 2)] = both.astype(bf16)
    wide, ch = pairs.shape[1:]

    def weights(plane):
        at, end = plane * 3 * ch, (plane + 1) * 3 * ch
        pieces = []
        while at < end:
            stop = min(end, (at // wide + 1) * wide)
            pieces.append(pairs[at // wide, at % wide : at % wide + stop - at])
            at = stop
        return jnp.concatenate(pieces, axis=0) if len(pieces) > 1 else pieces[0]

    return weights


def second_filter(spot, own, near, far, turned, *rest, scale, fast):
    total, outs = (rest[-1], rest[:2]) if fast else (rest[0], ())
    turned_sides, padded = rest[2:4] if fast else rest[1:3]
    ny = own.shape[1]
    fill_padded(spot, padded, own, near, far)

    def emit(plane, part):
        ch = part.shape[1]
        total[plane * 3 * ch : (plane + 1) * 3 * ch] = part

    filter_terms(turned, padded, emit, scale)
    if fast:
        split_halves(total, spot[2], *outs)
    high = near_edge(spot, 1)
    for y in range(ny):
        turned_sides[high, y] = near[1, y].astype(f32).T.astype(bf16)
        turned_sides[1 - high, y] = far[1, y].astype(f32).T.astype(bf16)


def both_columns(lists):
    split = [[ref.at[k] for k in range(ref.shape[0])] for ref in lists]
    return split[0] + split[1], split[2] + split[3]


def first_filter(spot, slope, own, near, far, turned_own, turned_sides, *rest, scale, masks):
    nx, ny, nz, ch = own.shape
    if masks:
        kept, sent, grads, near_one, far_one, padded, moved, stacked, total, pairs = rest[4:]
        mine, theirs = both_columns(rest[:4])
        weights = placed_weights(spot, masks, mine, theirs, pairs)
    else:
        full, total, grads, near_one, far_one, padded, moved, stacked = rest
        weights = plain_weights(full)
    fill_padded(spot, padded, own, near, far)

    def finish(x, y, value):
        value = (value * slope[x, y]).astype(bf16)
        grads[x, y] = value
        value = value.astype(f32)
        at = (x * ny + y) * nz
        for k, c in enumerate(shifts):
            moved[at : at + nz, k * ch : (k + 1) * ch] = shift_rows(value, c).astype(bf16)

    data_layers(padded, weights, finish, range(nx))
    send_edges(spot, grads, near_one, far_one)
    stack_turned(stacked, turned_own, turned_sides)
    part = jnp.dot(stacked[...], moved[...], preferred_element_type=f32) * scale
    for i in range(len(planes)):
        for k in range(len(shifts)):
            at = (i * len(shifts) + k) * ch
            total[at : at + ch] = part[i * ch : (i + 1) * ch, k * ch : (k + 1) * ch]
    if masks:
        split_halves(total, spot[2], kept, sent)


def input_grads(spot, own, near, far, *rest, masks):
    if masks:
        lists, (out, padded, pairs) = rest[:4], rest[4:]
        mine, theirs = both_columns(lists)
        weights = placed_weights(spot, masks, mine, theirs, pairs)
    else:
        full, out, padded = rest
        weights = plain_weights(full)
    fill_padded(spot, padded, own, near, far)

    def finish(x, y, value):
        out[x, y] = value.astype(bf16)

    data_layers(padded, weights, finish, range(out.shape[0]))


def first_column(part, far_part, extra, pair, handed):
    pair[0] = part[...]
    pair[1] = far_part[...]
    handed[...] = extra[...]


def second_column(pair, near_pair, part, far_part, column, pair_next):
    column[0:2] = pair[...]
    column[2:4] = near_pair[...]
    pair_next[0] = part[...]
    pair_next[1] = far_part[...]


def halve(spot, kept, got, kept_next, sent_next, *, bit):
    side = spot[bit]
    for k in range(kept_next.shape[0]):
        mine, other = 2 * k + side, 2 * k + 1 - side
        kept_next[k] = kept[mine] + got[mine].astype(f32)
        sent_next[k] = (kept[other] + got[other].astype(f32)).astype(bf16)


def halve_and_stack(spot, kept, got, pair, other, across, kept_next, sent_next, column, handed, *, bit):
    handed[...] = across[...]
    halve(spot, kept, got, kept_next, sent_next, bit=bit)
    count = pair.shape[0]
    column[0:count] = pair[...]
    column[count:] = other[...]


def last_sum(kept, got, out):
    out[...] = kept[0] + got[0].astype(f32)


def call(body, n_smem, args, outs, scratch=(), after=(), us=0.2):
    first = len(args)
    many = len(after)

    def run(*refs):
        body(*refs[:first], *refs[first + many :])

    return pl.pallas_call(
        run if many else body,
        in_specs=[smem] * n_smem + [vmem] * (len(args) - n_smem) + [anywhere] * many,
        out_specs=[vmem] * len(outs),
        out_shape=[jax.ShapeDtypeStruct(s, d) for s, d in outs],
        scratch_shapes=[pltpu.VMEM(s, d) for s, d in scratch],
        cost_estimate=pl.CostEstimate(flops=int(us * 1e9), bytes_accessed=int(us * 3e6), transcendentals=0),
        compiler_params=pltpu.CompilerParams(vmem_limit_bytes=vmem_bytes),
    )(*args, *after)


def on_device(grad_out, inputs, pre_first, pre_second, filter_first, filter_second):
    shape = grad_out.shape
    nx, ny, nz, ch = shape
    n = lax.axis_size("gx")
    me = lax.axis_index("gx")
    rows = filter_first.shape[0]
    taps = n * rows // ch
    scale = 1.0 / math.sqrt(nx * n * ny * nz)
    spot = jnp.stack([me, jnp.full((), n, me.dtype), me % 2, me // 2 % 2, me // 4 % 2, me // 8 % 2]).astype(jnp.int32)
    fast = rows % 8 == 0 and n == 1 << 4
    masks = (0, 8, 4, 12, 2, 10, 6, 14) if fast else ()
    layer = (1,) + shape[1:]
    layers = (2,) + shape[1:]
    block = (rows, ch)
    wide = ((nx + 2, ny + 2, nz, ch), bf16)
    cells = nx * ny * nz
    total = ((taps * ch, ch), f32)

    def swap(array, mask):
        return lax.ppermute(array, "gx", [(i, i ^ mask) for i in range(n)])

    def swap_far(array):
        ahead = [(i, i + 1) for i in range(1, n - 1, 2)]
        return lax.ppermute(array, "gx", ahead + [(b, a) for a, b in ahead])

    def blocks(count, dtype=bf16):
        return ((count,) + block, dtype)

    turned, turned_own, slope = call(
        prepare,
        0,
        (pre_first, inputs),
        [((3 * ch, cells), bf16), ((nx, ny, ch, nz), bf16), (shape, f32)],
    )
    terms = [blocks(n // 2, f32), blocks(n // 2)] if fast else [total]
    work = [total, ((n // 2, 2 * rows, ch), bf16)] if fast else []

    after = (turned,)
    if fast:
        pair, handed = call(
            first_column,
            0,
            (filter_second, swap(filter_second, 8), filter_first),
            [blocks(2), (block, bf16)],
            after=after,
        )
        after = (pair,)
    grad_two, near, far = call(
        first_grads,
        1,
        (spot, grad_out, pre_second, inputs),
        [(shape, bf16)] + [(layers, bf16)] * 2,
        after=after,
    )
    far = swap_far(far)
    near = swap(near, 1)
    after = ()
    if fast:
        column, pair_first = call(
            second_column,
            0,
            (pair, swap(pair, 4), handed, swap(handed, 8)),
            [blocks(4), blocks(2)],
            after=(grad_two,),
        )
        after = (column,)
    *terms_two, turned_sides = call(
        functools.partial(second_filter, scale=scale, fast=fast),
        1,
        (spot, grad_two, near, far, turned),
        terms + [((2, ny, ch, nz), bf16)],
        [wide] + work[:1],
        after=after,
        us=2,
    )
    if fast:
        across = swap(column, 2)
        kept_two, sent_two, column_first, across = call(
            functools.partial(halve_and_stack, bit=3),
            1,
            (spot, terms_two[0], swap(terms_two[1], 1), pair_first, swap(pair_first, 4), across),
            [blocks(4, f32), blocks(4), blocks(4), blocks(4)],
        )
        full_second = (column, across, swap(column, 1), swap(across, 1))
    else:
        full_second = (lax.all_gather(filter_second, "gx", axis=0, tiled=True),)

    *terms_one, grad_one, near_one, far_one = call(
        functools.partial(first_filter, scale=scale, masks=masks),
        1,
        (spot, slope, grad_two, near, far, turned_own, turned_sides, *full_second),
        terms + [(shape, bf16), (layer, bf16), (layer, bf16)],
        [wide, ((cells, 3 * ch), bf16), ((len(planes) * ch, cells), bf16)] + work,
        us=8,
    )
    near_one, far_one = swap(near_one, 1), swap_far(far_one)

    def finish(full, after=()):
        return call(
            functools.partial(input_grads, masks=masks),
            1,
            (spot, grad_one, near_one, far_one, *full),
            [(shape, bf16)],
            [wide] + work[1:],
            after=after,
            us=3,
        )[0]

    if fast:

        def step(kept, sent, bit, mask, count, after):
            return call(
                functools.partial(halve, bit=bit),
                1,
                (spot, kept, swap(sent, mask)),
                [blocks(count, f32), blocks(count)],
                after=after,
            )

        kept_two, sent_two = step(kept_two, sent_two, 4, 2, 2, (grad_one,))
        kept_one, sent_one = step(*terms_one, 3, 1, 4, (kept_two,))
        kept_two, sent_two = step(kept_two, sent_two, 5, 4, 1, (kept_one,))
        kept_one, sent_one = step(kept_one, sent_one, 4, 2, 2, (kept_two,))
        kept_one, sent_one = step(kept_one, sent_one, 5, 4, 1, ())
        across_first = swap(column_first, 2)
        mine = (column_first, across_first)
        grad_in = finish((*mine, *(swap(m, 1) for m in mine)), (kept_one,))
        (owned_two,) = call(last_sum, 0, (kept_two, swap(sent_two, 8)), [(block, f32)])
        (owned_one,) = call(last_sum, 0, (kept_one, swap(sent_one, 8)), [(block, f32)], after=(grad_in,))
    else:
        grad_in = finish((lax.all_gather(filter_first, "gx", axis=0, tiled=True),))
        owned_two, owned_one = (
            lax.psum_scatter(t[0], "gx", scatter_dimension=0, tiled=True) for t in (terms_two, terms_one)
        )
    return (grad_in, owned_one, owned_two)


def solution(mesh):
    whole = P(("groups", "gx"), None, None, None)
    return jax.shard_map(
        on_device,
        mesh=mesh,
        in_specs=(whole, whole, whole, whole, P("gx", None), P("gx", None)),
        out_specs=(whole, P("gx", "groups"), P("gx", "groups")),
        check_vma=False,
    )
```

time: 78.8 us -> 73.9 us (0.938)
  other arithmetic: 10.3 us -> 0 us
  waiting for transfers between devices: 34.1 us -> 28.4 us
  starting transfers between devices: 20 us -> 25.5 us
  Pallas kernels: 10.5 us -> 14.9 us
  local copies, waits for them, and re-layouts: 2.61 us -> 4.02 us
    another operation x10 -> x0, other arithmetic: 6.54 us -> none  [the longest x8 5.61 us: on_device(): jnp.stack([jnp.where(low, full, other), jnp.where(low, other, full)], axi...]
    ppermute x14 -> x22, waiting for transfers between devices: 34.1 us -> 28.4 us  [the longest x20 28.4 us: swap(): return lax.ppermute(array, 'gx', [(i, i ^ mask) for i in range(n)])]
    ppermute x14 -> x22, starting transfers between devices: 20 us -> 25.5 us  [the longest x20 24.2 us: swap(): return lax.ppermute(array, 'gx', [(i, i ^ mask) for i in range(n)])]
    pallas_call x4 -> x15, Pallas kernels: 10.5 us -> 14.9 us  [call(): pl.pallas_call(run if many else body, in_specs=[smem] * n_smem + [vmem] *...]
    unnamed x18 -> x16, local copies, waits for them, and re-layouts: 0.66 us -> 3.93 us
    add x6 -> x0, other arithmetic: 2.48 us -> none  [the longest x4 1.26 us: finish_scatter(): total = mine + swap(theirs.astype(bf16), bit).astype(f32)]
    reshape x2 -> x0, other arithmetic: 1.31 us -> none  [finish_scatter(): return total.reshape(rows, ch)]
    slice x2 -> x0, local copies, waits for them, and re-layouts: 1.06 us -> none  [on_device(): full_first, full_second = (full[0], full[1])]
  transfers between devices with their start and end apart: 14 -> 22, of which waited for: 8 -> 13; matrix products, arithmetic and copies ran while one was open for 12% -> 0% of each run, Pallas kernels for 13% -> 11%
where the time goes in v2:
time: 73.9 us; the launch traced here: 73.6 us
  waiting for transfers between devices  28.4 us (38%)
  starting transfers between devices  25.5 us (35%)
  Pallas kernels  14.9 us (20%)
  local copies, waits for them, and re-layouts  4.02 us (5%)
  between operations  0.81 us (1%)
    ppermute x20, waiting for transfers between devices, swap(): return lax.ppermute(array, 'gx', [(i, i ^ mask) for i in range(n)])  28.4 us
    ppermute x20, starting transfers between devices, swap(): return lax.ppermute(array, 'gx', [(i, i ^ mask) for i in range(n)])  24.2 us
    pallas_call x15, Pallas kernels, call(): pl.pallas_call(run if many else body, in_specs=[smem] * n_smem + [vmem] *...  14.9 us
    unnamed x16, local copies, waits for them, and re-layouts  3.93 us
  transfers between devices with their start and end apart: 22, of which 13 were waited for; matrix products, arithmetic and copies ran while one was open for 0% of the time, Pallas kernels for 11%

profile of v2, /device:TPU:0, one launch (start us, length us, event | category | flops | bytes accessed | tf_op | source)
XLA Modules:
  0.0 73.6 jit_solution(14121563821658312067)
XLA Ops:
  0.6 4.1 %collective-permute-start = (bf16[216,128]{1,0:T(8,128)(2,1)}, bf16[216,128]{1,0:T(8,128)(2,1)S(1)}, u32[]{:S(2)}, u32[]{:S(2)}) collective-permute-start(bf16[216,128]{1,0:T(8,128)(2,1)} %refs_0_.1), channel_id=1, source_target_pairs={{0,8},{1,9},{2,10},{3,11},{4,12},{5,13},{6,14},{7,15},{8,0},{9,1},... | collective-permute-start | bytes 165896 | tf_op jit(solution)/shard_map/ppermute | solution.py:320
  4.8 0.9 %copy-done = bf16[2,4,128,128]{3,2,1,0:T(8,128)(2,1)S(1)} copy-done((bf16[2,4,128,128]{3,2,1,0:T(8,128)(2,1)S(1)}, bf16[2,4,128,128]{3,2,1,0:T(8,128)(2,1)}, u32[]{:S(2)}) %copy-start) | copy-done | bytes 262168
  5.8 0.9 %copy-done.6 = bf16[2,4,128,128]{3,2,1,0:T(8,128)(2,1)S(1)} copy-done((bf16[2,4,128,128]{3,2,1,0:T(8,128)(2,1)S(1)}, bf16[2,4,128,128]{3,2,1,0:T(8,128)(2,1)}, u32[]{:S(2)}) %copy-start.6) | copy-done | bytes 262168
  7.7 0.9 %copy-done.1 = bf16[2,4,128,128]{3,2,1,0:T(8,128)(2,1)S(1)} copy-done((bf16[2,4,128,128]{3,2,1,0:T(8,128)(2,1)S(1)}, bf16[2,4,128,128]{3,2,1,0:T(8,128)(2,1)}, u32[]{:S(2)}) %copy-start.1) | copy-done | bytes 262168
  10.4 4.6 %collective-permute-start.3 = (bf16[2,216,128]{2,1,0:T(8,128)(2,1)S(1)}, bf16[2,216,128]{2,1,0:T(8,128)(2,1)S(1)}, u32[]{:S(2)}, u32[]{:S(2)}) collective-permute-start(bf16[2,216,128]{2,1,0:T(8,128)(2,1)S(1)} %get-tuple-element.37.refs_4_.refs_0_), channel_id=1, source_target_pairs={{0,4},{1,5},{2,6},{3,7},{4,0},{5,1},{6,2},{7,3},{8,12},{9,13},{10,... | collective-permute-start | bytes 331784 | tf_op jit(solution)/shard_map/ppermute | solution.py:320
  14.9 2.2 %collective-permute-start.4 = (bf16[216,128]{1,0:T(8,128)(2,1)S(1)}, bf16[216,128]{1,0:T(8,128)(2,1)S(1)}, u32[]{:S(2)}, u32[]{:S(2)}) collective-permute-start(bf16[216,128]{1,0:T(8,128)(2,1)S(1)} %get-tuple-element.42.refs_2_), channel_id=1, source_target_pairs={{0,8},{1,9},{2,10},{3,11},{4,12},{5,13},{6,14},{7,15},{8,0},{9,1},... | collective-permute-start | bytes 165896 | tf_op jit(solution)/shard_map/ppermute | solution.py:320
  17.1 4.7 %collective-permute-done.4.refs_3_ = bf16[216,128]{1,0:T(8,128)(2,1)S(1)} collective-permute-done((bf16[216,128]{1,0:T(8,128)(2,1)S(1)}, bf16[216,128]{1,0:T(8,128)(2,1)S(1)}, u32[]{:S(2)}, u32[]{:S(2)}) %collective-permute-start.4) | collective-permute-done | bytes 55328 | tf_op jit(solution)/shard_map/ppermute | solution.py:320
  22.5 1.9 %shard_map.89 = (f32[8,216,128]{2,1,0:T(8,128)S(1)}, bf16[8,216,128]{2,1,0:T(8,128)(2,1)S(1)}, bf16[2,4,128,128]{3,2,1,0:T(8,128)(2,1)S(1)}) custom-call(s32[6]{0:T(128)S(1)} %stack.23.refs_0_.spot, bf16[2,4,128,128]{3,2,1,0:T(8,128)(2,1)S(1)} %get-tuple-element.38.refs_4_.refs_1_.own, bf16[2,4,128,128]{3,2,1,0:T(8,128)(2,1)S(1)} %collective-permute-done.1.refs_2_.near, ...), custom_call_target="tpu_custom_call" | custom-call | flops 2000000000 | bytes 6000000 | tf_op jit(solution)/shard_map/pallas_call | solution.py:290
  24.6 2.5 %collective-permute-start.6 = (bf16[2,216,128]{2,1,0:T(8,128)(2,1)S(1)}, bf16[2,216,128]{2,1,0:T(8,128)(2,1)S(1)}, u32[]{:S(2)}, u32[]{:S(2)}) collective-permute-start(bf16[2,216,128]{2,1,0:T(8,128)(2,1)S(1)} %get-tuple-element.47.pair), channel_id=1, source_target_pairs={{0,4},{1,5},{2,6},{3,7},{4,0},{5,1},{6,2},{7,3},{8,12},{9,13},{10,... | collective-permute-start | bytes 331784 | tf_op jit(solution)/shard_map/ppermute | solution.py:320
  27.2 3.5 %collective-permute-done.6.other = bf16[2,216,128]{2,1,0:T(8,128)(2,1)S(1)} collective-permute-done((bf16[2,216,128]{2,1,0:T(8,128)(2,1)S(1)}, bf16[2,216,128]{2,1,0:T(8,128)(2,1)S(1)}, u32[]{:S(2)}, u32[]{:S(2)}) %collective-permute-start.6) | collective-permute-done | bytes 110624 | tf_op jit(solution)/shard_map/ppermute | solution.py:320
  30.7 1.6 %collective-permute-done.7.across = bf16[4,216,128]{2,1,0:T(8,128)(2,1)S(1)} collective-permute-done((bf16[4,216,128]{2,1,0:T(8,128)(2,1)S(1)}, bf16[4,216,128]{2,1,0:T(8,128)(2,1)S(1)}, u32[]{:S(2)}, u32[]{:S(2)}) %collective-permute-start.7) | collective-permute-done | bytes 221216 | tf_op jit(solution)/shard_map/ppermute | solution.py:320
  33.1 1.5 %collective-permute-done.9.rest_3_ = bf16[4,216,128]{2,1,0:T(8,128)(2,1)S(1)} collective-permute-done((bf16[4,216,128]{2,1,0:T(8,128)(2,1)S(1)}, bf16[4,216,128]{2,1,0:T(8,128)(2,1)S(1)}, u32[]{:S(2)}, u32[]{:S(2)}) %collective-permute-start.9) | collective-permute-done | bytes 221216 | tf_op jit(solution)/shard_map/ppermute | solution.py:320
  34.5 3.8 %shard_map.91 = (f32[8,216,128]{2,1,0:T(8,128)S(1)}, bf16[8,216,128]{2,1,0:T(8,128)(2,1)S(1)}, bf16[2,4,128,128]{3,2,1,0:T(8,128)(2,1)S(1)}, bf16[1,4,128,128]{3...) custom-call(s32[6]{0:T(128)S(1)} %stack.23.refs_0_.spot, f32[2,4,128,128]{3,2,1,0:T(8,128)S(1)} %get-tuple-element.35.slope, ...), custom_call_target="tpu_custom_call" | custom-call | flops 8000000000 | bytes 24000000 | tf_op jit(solution)/shard_map/pallas_call | solution.py:290
  38.8 1.8 %collective-permute-start.12 = (bf16[4,216,128]{2,1,0:T(8,128)(2,1)S(1)}, bf16[4,216,128]{2,1,0:T(8,128)(2,1)S(1)}, u32[]{:S(2)}, u32[]{:S(2)}) collective-permute-start(bf16[4,216,128]{2,1,0:T(8,128)(2,1)S(1)} %get-tuple-element.52.refs_4_), channel_id=1, source_target_pairs={{0,2},{1,3},{2,0},{3,1},{4,6},{5,7},{6,4},{7,5},{8,10},{9,11},{10,... | collective-permute-start | bytes 663560 | tf_op jit(solution)/shard_map/ppermute | solution.py:320
  40.6 6.2 %collective-permute-done.16.refs_2_ = bf16[4,216,128]{2,1,0:T(8,128)(2,1)S(1)} collective-permute-done((bf16[4,216,128]{2,1,0:T(8,128)(2,1)S(1)}, bf16[4,216,128]{2,1,0:T(8,128)(2,1)S(1)}, u32[]{:S(2)}, u32[]{:S(2)}) %collective-permute-start.16) | collective-permute-done | bytes 221216 | tf_op jit(solution)/shard_map/ppermute | solution.py:320
  48.3 2.5 %collective-permute-start.18 = (bf16[2,216,128]{2,1,0:T(8,128)(2,1)S(1)}, bf16[2,216,128]{2,1,0:T(8,128)(2,1)S(1)}, u32[]{:S(2)}, u32[]{:S(2)}) collective-permute-start(bf16[2,216,128]{2,1,0:T(8,128)(2,1)S(1)} %get-tuple-element.60), channel_id=1, source_target_pairs={{0,4},{1,5},{2,6},{3,7},{4,0},{5,1},{6,2},{7,3},{8,12},{9,13},{10,... | collective-permute-start | bytes 331784 | tf_op jit(solution)/shard_map/ppermute | solution.py:320
  51.5 2.0 %collective-permute-done.18.refs_2_ = bf16[2,216,128]{2,1,0:T(8,128)(2,1)S(1)} collective-permute-done((bf16[2,216,128]{2,1,0:T(8,128)(2,1)S(1)}, bf16[2,216,128]{2,1,0:T(8,128)(2,1)S(1)}, u32[]{:S(2)}, u32[]{:S(2)}) %collective-permute-start.18) | collective-permute-done | bytes 110624 | tf_op jit(solution)/shard_map/ppermute | solution.py:320
  54.1 1.5 %collective-permute-start.21 = (bf16[1,216,128]{2,1,0:T(8,128)(2,1)S(1)}, bf16[1,216,128]{2,1,0:T(8,128)(2,1)S(1)}, u32[]{:S(2)}, u32[]{:S(2)}) collective-permute-start(bf16[1,216,128]{2,1,0:T(8,128)(2,1)S(1)} %get-tuple-element.66), channel_id=1, source_target_pairs={{0,8},{1,9},{2,10},{3,11},{4,12},{5,13},{6,14},{7,15},{8,0},{9,1},... | collective-permute-start | bytes 165896 | tf_op jit(solution)/shard_map/ppermute | solution.py:320
  57.0 2.3 %collective-permute-done.21.got = bf16[1,216,128]{2,1,0:T(8,128)(2,1)S(1)} collective-permute-done((bf16[1,216,128]{2,1,0:T(8,128)(2,1)S(1)}, bf16[1,216,128]{2,1,0:T(8,128)(2,1)S(1)}, u32[]{:S(2)}, u32[]{:S(2)}) %collective-permute-start.21) | collective-permute-done | bytes 55328 | tf_op jit(solution)/shard_map/ppermute | solution.py:320
  59.3 2.3 %collective-permute-start.19 = (bf16[2,216,128]{2,1,0:T(8,128)(2,1)S(1)}, bf16[2,216,128]{2,1,0:T(8,128)(2,1)S(1)}, u32[]{:S(2)}, u32[]{:S(2)}) collective-permute-start(bf16[2,216,128]{2,1,0:T(8,128)(2,1)S(1)} %get-tuple-element.63), channel_id=1, source_target_pairs={{0,4},{1,5},{2,6},{3,7},{4,0},{5,1},{6,2},{7,3},{8,12},{9,13},{10,... | collective-permute-start | bytes 331784 | tf_op jit(solution)/shard_map/ppermute | solution.py:320
  62.2 4.0 %collective-permute-done.19.got = bf16[2,216,128]{2,1,0:T(8,128)(2,1)S(1)} collective-permute-done((bf16[2,216,128]{2,1,0:T(8,128)(2,1)S(1)}, bf16[2,216,128]{2,1,0:T(8,128)(2,1)S(1)}, u32[]{:S(2)}, u32[]{:S(2)}) %collective-permute-start.19) | collective-permute-done | bytes 110624 | tf_op jit(solution)/shard_map/ppermute | solution.py:320
  66.7 1.6 %collective-permute-start.20 = (bf16[1,216,128]{2,1,0:T(8,128)(2,1)S(1)}, bf16[1,216,128]{2,1,0:T(8,128)(2,1)S(1)}, u32[]{:S(2)}, u32[]{:S(2)}) collective-permute-start(bf16[1,216,128]{2,1,0:T(8,128)(2,1)S(1)} %get-tuple-element.65), channel_id=1, source_target_pairs={{0,8},{1,9},{2,10},{3,11},{4,12},{5,13},{6,14},{7,15},{8,0},{9,1},... | collective-permute-start | bytes 165896 | tf_op jit(solution)/shard_map/ppermute | solution.py:320
  68.3 3.0 %shard_map.97.refs_2_ = bf16[2,4,128,128]{3,2,1,0:T(8,128)(2,1)} custom-call(s32[6]{0:T(128)S(1)} %stack.23.refs_0_.spot, bf16[2,4,128,128]{3,2,1,0:T(8,128)(2,1)S(1)} %get-tuple-element.49.refs_3_.refs_1_, bf16[1,4,128,128]{3,2,1,0:T(8,128)(2,1)S(1)} %collective-permute-done.10.refs_2_, bf16[1,4,128,128]{3,2,1,0:T(8,128)(2,1)S(1)} %collective-permute-done.11.refs_3_, ...), custom_call_target="tpu_custom_call" | custom-call | flops 3000000000 | bytes 9000000 | tf_op jit(solution)/shard_map/pallas_call | solution.py:290
  72.0 0.9 %copy-done.7 = bf16[2,4,128,128]{3,2,1,0:T(8,128)(2,1)S(1)} copy-done((bf16[2,4,128,128]{3,2,1,0:T(8,128)(2,1)S(1)}, bf16[2,4,128,128]{3,2,1,0:T(8,128)(2,1)}, u32[]{:S(2)}) %copy-start.7) | copy-done | bytes 262168
  (52 shorter events, 11.7 us)
Async XLA Ops:
  0.6 7.0 %collective-permute-start = (bf16[216,128]{1,0:T(8,128)(2,1)}, bf16[216,128]{1,0:T(8,128)(2,1)S(1)}, u32[]{:S(2)}, u32[]{:S(2)}) collective-permute-start(bf16[216,128]{1,0:T(8,128)(2,1)} %refs_0_.1), channel_id=1, source_target_pairs={{0,8},{1,9},{2,10},{3,11},{4,12},{5,13},{6,14},{7,15},{8,0},{9,1},... | collective-permute-start | bytes 165896 | tf_op jit(solution)/shard_map/ppermute | solution.py:320
  7.7 1.0 %copy-start.2 = (bf16[2,4,128,128]{3,2,1,0:T(8,128)(2,1)S(1)}, bf16[2,4,128,128]{3,2,1,0:T(8,128)(2,1)}, u32[]{:S(2)}) copy-start(bf16[2,4,128,128]{3,2,1,0:T(8,128)(2,1)} %refs_1_.1) | copy-start | bytes 786436
  7.7 1.1 %copy-start.3 = (bf16[2,4,128,128]{3,2,1,0:T(8,128)(2,1)S(1)}, bf16[2,4,128,128]{3,2,1,0:T(8,128)(2,1)}, u32[]{:S(2)}) copy-start(bf16[2,4,128,128]{3,2,1,0:T(8,128)(2,1)} %refs_2_.3) | copy-start | bytes 786436
  9.6 12.9 %collective-permute-start.1 = (bf16[2,4,128,128]{3,2,1,0:T(8,128)(2,1)S(1)}, bf16[2,4,128,128]{3,2,1,0:T(8,128)(2,1)S(1)}, u32[]{:S(2)}, u32[]{:S(2)}) collective-permute-start(bf16[2,4,128,128]{3,2,1,0:T(8,128)(2,1)S(1)} %get-tuple-element.39), channel_id=1, source_target_pairs={{0,1},{1,0},{2,3},{3,2},{4,5},{5,4},{6,7},{7,6},{8,9},{9,8},{10,11... | collective-permute-start | bytes 786440 | tf_op jit(solution)/shard_map/ppermute | solution.py:320
  9.7 12.8 %collective-permute-start.2 = (bf16[2,4,128,128]{3,2,1,0:T(8,128)(2,1)S(1)}, bf16[2,4,128,128]{3,2,1,0:T(8,128)(2,1)S(1)}, u32[]{:S(2)}, u32[]{:S(2)}) collective-permute-start(bf16[2,4,128,128]{3,2,1,0:T(8,128)(2,1)S(1)} %get-tuple-element.40), channel_id=1, source_target_pairs={{1,2},{3,4},{5,6},{7,8},{9,10},{11,12},{13,14},{2,1},{4,3},{6,5},{... | collective-permute-start | bytes 786440 | tf_op jit(solution)/shard_map/ppermute | solution.py:324
  10.4 12.1 %collective-permute-start.3 = (bf16[2,216,128]{2,1,0:T(8,128)(2,1)S(1)}, bf16[2,216,128]{2,1,0:T(8,128)(2,1)S(1)}, u32[]{:S(2)}, u32[]{:S(2)}) collective-permute-start(bf16[2,216,128]{2,1,0:T(8,128)(2,1)S(1)} %get-tuple-element.37.refs_4_.refs_0_), channel_id=1, source_target_pairs={{0,4},{1,5},{2,6},{3,7},{4,0},{5,1},{6,2},{7,3},{8,12},{9,13},{10,... | collective-permute-start | bytes 331784 | tf_op jit(solution)/shard_map/ppermute | solution.py:320
  14.9 6.9 %collective-permute-start.4 = (bf16[216,128]{1,0:T(8,128)(2,1)S(1)}, bf16[216,128]{1,0:T(8,128)(2,1)S(1)}, u32[]{:S(2)}, u32[]{:S(2)}) collective-permute-start(bf16[216,128]{1,0:T(8,128)(2,1)S(1)} %get-tuple-element.42.refs_2_), channel_id=1, source_target_pairs={{0,8},{1,9},{2,10},{3,11},{4,12},{5,13},{6,14},{7,15},{8,0},{9,1},... | collective-permute-start | bytes 165896 | tf_op jit(solution)/shard_map/ppermute | solution.py:320
  24.4 7.9 %collective-permute-start.5 = (bf16[8,216,128]{2,1,0:T(8,128)(2,1)S(1)}, bf16[8,216,128]{2,1,0:T(8,128)(2,1)S(1)}, u32[]{:S(2)}, u32[]{:S(2)}) collective-permute-start(bf16[8,216,128]{2,1,0:T(8,128)(2,1)S(1)} %get-tuple-element.46), channel_id=1, source_target_pairs={{0,1},{1,0},{2,3},{3,2},{4,5},{5,4},{6,7},{7,6},{8,9},{9,8},{10,11... | collective-permute-start | bytes 1327112 | tf_op jit(solution)/shard_map/ppermute | solution.py:320
  24.5 7.8 %collective-permute-start.7 = (bf16[4,216,128]{2,1,0:T(8,128)(2,1)S(1)}, bf16[4,216,128]{2,1,0:T(8,128)(2,1)S(1)}, u32[]{:S(2)}, u32[]{:S(2)}) collective-permute-start(bf16[4,216,128]{2,1,0:T(8,128)(2,1)S(1)} %get-tuple-element.43.refs_5_.rest_0_), channel_id=1, source_target_pairs={{0,2},{1,3},{2,0},{3,1},{4,6},{5,7},{6,4},{7,5},{8,10},{9,11},{10,... | collective-permute-start | bytes 663560 | tf_op jit(solution)/shard_map/ppermute | solution.py:320
  24.6 6.1 %collective-permute-start.6 = (bf16[2,216,128]{2,1,0:T(8,128)(2,1)S(1)}, bf16[2,216,128]{2,1,0:T(8,128)(2,1)S(1)}, u32[]{:S(2)}, u32[]{:S(2)}) collective-permute-start(bf16[2,216,128]{2,1,0:T(8,128)(2,1)S(1)} %get-tuple-element.47.pair), channel_id=1, source_target_pairs={{0,4},{1,5},{2,6},{3,7},{4,0},{5,1},{6,2},{7,3},{8,12},{9,13},{10,... | collective-permute-start | bytes 331784 | tf_op jit(solution)/shard_map/ppermute | solution.py:320
  27.1 6.0 %collective-permute-start.8 = (bf16[4,216,128]{2,1,0:T(8,128)(2,1)S(1)}, bf16[4,216,128]{2,1,0:T(8,128)(2,1)S(1)}, u32[]{:S(2)}, u32[]{:S(2)}) collective-permute-start(bf16[4,216,128]{2,1,0:T(8,128)(2,1)S(1)} %get-tuple-element.43.refs_5_.rest_0_), channel_id=1, source_target_pairs={{0,1},{1,0},{2,3},{3,2},{4,5},{5,4},{6,7},{7,6},{8,9},{9,8},{10,11... | collective-permute-start | bytes 663560 | tf_op jit(solution)/shard_map/ppermute | solution.py:320
  33.0 1.5 %collective-permute-start.9 = (bf16[4,216,128]{2,1,0:T(8,128)(2,1)S(1)}, bf16[4,216,128]{2,1,0:T(8,128)(2,1)S(1)}, u32[]{:S(2)}, u32[]{:S(2)}) collective-permute-start(bf16[4,216,128]{2,1,0:T(8,128)(2,1)S(1)} %get-tuple-element.48.rest_1_), channel_id=1, source_target_pairs={{0,1},{1,0},{2,3},{3,2},{4,5},{5,4},{6,7},{7,6},{8,9},{9,8},{10,11... | collective-permute-start | bytes 663560 | tf_op jit(solution)/shard_map/ppermute | solution.py:320
  38.3 9.1 %collective-permute-start.15 = (bf16[8,216,128]{2,1,0:T(8,128)(2,1)S(1)}, bf16[8,216,128]{2,1,0:T(8,128)(2,1)S(1)}, u32[]{:S(2)}, u32[]{:S(2)}) collective-permute-start(bf16[8,216,128]{2,1,0:T(8,128)(2,1)S(1)} %get-tuple-element.54), channel_id=1, source_target_pairs={{0,1},{1,0},{2,3},{3,2},{4,5},{5,4},{6,7},{7,6},{8,9},{9,8},{10,11... | collective-permute-start | bytes 1327112 | tf_op jit(solution)/shard_map/ppermute | solution.py:320
  38.5 8.3 %collective-permute-start.16 = (bf16[4,216,128]{2,1,0:T(8,128)(2,1)S(1)}, bf16[4,216,128]{2,1,0:T(8,128)(2,1)S(1)}, u32[]{:S(2)}, u32[]{:S(2)}) collective-permute-start(bf16[4,216,128]{2,1,0:T(8,128)(2,1)S(1)} %get-tuple-element.56), channel_id=1, source_target_pairs={{0,2},{1,3},{2,0},{3,1},{4,6},{5,7},{6,4},{7,5},{8,10},{9,11},{10,... | collective-permute-start | bytes 663560 | tf_op jit(solution)/shard_map/ppermute | solution.py:320
  38.8 12.7 %collective-permute-start.12 = (bf16[4,216,128]{2,1,0:T(8,128)(2,1)S(1)}, bf16[4,216,128]{2,1,0:T(8,128)(2,1)S(1)}, u32[]{:S(2)}, u32[]{:S(2)}) collective-permute-start(bf16[4,216,128]{2,1,0:T(8,128)(2,1)S(1)} %get-tuple-element.52.refs_4_), channel_id=1, source_target_pairs={{0,2},{1,3},{2,0},{3,1},{4,6},{5,7},{6,4},{7,5},{8,10},{9,11},{10,... | collective-permute-start | bytes 663560 | tf_op jit(solution)/shard_map/ppermute | solution.py:320
  48.0 7.7 %collective-permute-start.17 = (bf16[4,216,128]{2,1,0:T(8,128)(2,1)S(1)}, bf16[4,216,128]{2,1,0:T(8,128)(2,1)S(1)}, u32[]{:S(2)}, u32[]{:S(2)}) collective-permute-start(bf16[4,216,128]{2,1,0:T(8,128)(2,1)S(1)} %get-tuple-element.59), channel_id=1, source_target_pairs={{0,2},{1,3},{2,0},{3,1},{4,6},{5,7},{6,4},{7,5},{8,10},{9,11},{10,... | collective-permute-start | bytes 663560 | tf_op jit(solution)/shard_map/ppermute | solution.py:320
  48.3 5.2 %collective-permute-start.18 = (bf16[2,216,128]{2,1,0:T(8,128)(2,1)S(1)}, bf16[2,216,128]{2,1,0:T(8,128)(2,1)S(1)}, u32[]{:S(2)}, u32[]{:S(2)}) collective-permute-start(bf16[2,216,128]{2,1,0:T(8,128)(2,1)S(1)} %get-tuple-element.60), channel_id=1, source_target_pairs={{0,4},{1,5},{2,6},{3,7},{4,0},{5,1},{6,2},{7,3},{8,12},{9,13},{10,... | collective-permute-start | bytes 331784 | tf_op jit(solution)/shard_map/ppermute | solution.py:320
  50.8 17.5 %collective-permute-start.13 = (bf16[4,216,128]{2,1,0:T(8,128)(2,1)S(1)}, bf16[4,216,128]{2,1,0:T(8,128)(2,1)S(1)}, u32[]{:S(2)}, u32[]{:S(2)}) collective-permute-start(bf16[4,216,128]{2,1,0:T(8,128)(2,1)S(1)} %get-tuple-element.52.refs_4_), channel_id=1, source_target_pairs={{0,1},{1,0},{2,3},{3,2},{4,5},{5,4},{6,7},{7,6},{8,9},{9,8},{10,11... | collective-permute-start | bytes 663560 | tf_op jit(solution)/shard_map/ppermute | solution.py:320
  51.5 16.8 %collective-permute-start.14 = (bf16[4,216,128]{2,1,0:T(8,128)(2,1)S(1)}, bf16[4,216,128]{2,1,0:T(8,128)(2,1)S(1)}, u32[]{:S(2)}, u32[]{:S(2)}) collective-permute-start(bf16[4,216,128]{2,1,0:T(8,128)(2,1)S(1)} %collective-permute-done.12.refs_5_), channel_id=1, source_target_pairs={{0,1},{1,0},{2,3},{3,2},{4,5},{5,4},{6,7},{7,6},{8,9},{9,8},{10,11... | collective-permute-start | bytes 663560 | tf_op jit(solution)/shard_map/ppermute | solution.py:320
  54.1 5.1 %collective-permute-start.21 = (bf16[1,216,128]{2,1,0:T(8,128)(2,1)S(1)}, bf16[1,216,128]{2,1,0:T(8,128)(2,1)S(1)}, u32[]{:S(2)}, u32[]{:S(2)}) collective-permute-start(bf16[1,216,128]{2,1,0:T(8,128)(2,1)S(1)} %get-tuple-element.66), channel_id=1, source_target_pairs={{0,8},{1,9},{2,10},{3,11},{4,12},{5,13},{6,14},{7,15},{8,0},{9,1},... | collective-permute-start | bytes 165896 | tf_op jit(solution)/shard_map/ppermute | solution.py:320
  55.6 12.7 %collective-permute-start.10 = (bf16[1,4,128,128]{3,2,1,0:T(8,128)(2,1)S(1)}, bf16[1,4,128,128]{3,2,1,0:T(8,128)(2,1)S(1)}, u32[]{:S(2)}, u32[]{:S(2)}) collective-permute-start(bf16[1,4,128,128]{3,2,1,0:T(8,128)(2,1)S(1)} %get-tuple-element.50), channel_id=1, source_target_pairs={{0,1},{1,0},{2,3},{3,2},{4,5},{5,4},{6,7},{7,6},{8,9},{9,8},{10,11... | collective-permute-start | bytes 393224 | tf_op jit(solution)/shard_map/ppermute | solution.py:320
  55.7 12.6 %collective-permute-start.11 = (bf16[1,4,128,128]{3,2,1,0:T(8,128)(2,1)S(1)}, bf16[1,4,128,128]{3,2,1,0:T(8,128)(2,1)S(1)}, u32[]{:S(2)}, u32[]{:S(2)}) collective-permute-start(bf16[1,4,128,128]{3,2,1,0:T(8,128)(2,1)S(1)} %get-tuple-element.51), channel_id=1, source_target_pairs={{1,2},{3,4},{5,6},{7,8},{9,10},{11,12},{13,14},{2,1},{4,3},{6,5},{... | collective-permute-start | bytes 393224 | tf_op jit(solution)/shard_map/ppermute | solution.py:324
  59.3 6.9 %collective-permute-start.19 = (bf16[2,216,128]{2,1,0:T(8,128)(2,1)S(1)}, bf16[2,216,128]{2,1,0:T(8,128)(2,1)S(1)}, u32[]{:S(2)}, u32[]{:S(2)}) collective-permute-start(bf16[2,216,128]{2,1,0:T(8,128)(2,1)S(1)} %get-tuple-element.63), channel_id=1, source_target_pairs={{0,4},{1,5},{2,6},{3,7},{4,0},{5,1},{6,2},{7,3},{8,12},{9,13},{10,... | collective-permute-start | bytes 331784 | tf_op jit(solution)/shard_map/ppermute | solution.py:320
  66.7 5.3 %collective-permute-start.20 = (bf16[1,216,128]{2,1,0:T(8,128)(2,1)S(1)}, bf16[1,216,128]{2,1,0:T(8,128)(2,1)S(1)}, u32[]{:S(2)}, u32[]{:S(2)}) collective-permute-start(bf16[1,216,128]{2,1,0:T(8,128)(2,1)S(1)} %get-tuple-element.65), channel_id=1, source_target_pairs={{0,8},{1,9},{2,10},{3,11},{4,12},{5,13},{6,14},{7,15},{8,0},{9,1},... | collective-permute-start | bytes 165896 | tf_op jit(solution)/shard_map/ppermute | solution.py:320
  (6 other events, 5.7 us)

commit v3 on v2

--- a/solution.py
+++ b/solution.py
@@ -144,6 +144,10 @@
     padded[nx + 1 - at, 1 : 1 + ny] = far[0]
 
 
+def widen(spot, own, near, far, padded):
+    fill_padded(spot, padded, own, near, far)
+
+
 def split_halves(total, side, kept, sent):
     half, rows = kept.shape[:2]
     for k in range(half):
@@ -176,11 +180,10 @@
     return weights
 
 
-def second_filter(spot, own, near, far, turned, *rest, scale, fast):
+def second_filter(spot, padded, near, far, turned, *rest, scale, fast):
     total, outs = (rest[-1], rest[:2]) if fast else (rest[0], ())
-    turned_sides, padded = rest[2:4] if fast else rest[1:3]
-    ny = own.shape[1]
-    fill_padded(spot, padded, own, near, far)
+    turned_sides = rest[2] if fast else rest[1]
+    ny = near.shape[1]
 
     def emit(plane, part):
         ch = part.shape[1]
@@ -200,16 +203,15 @@
     return split[0] + split[1], split[2] + split[3]
 
 
-def first_filter(spot, slope, own, near, far, turned_own, turned_sides, *rest, scale, masks):
-    nx, ny, nz, ch = own.shape
+def first_filter(spot, slope, padded, turned_own, turned_sides, *rest, scale, masks):
+    nx, ny, nz, ch = slope.shape
     if masks:
-        kept, sent, grads, near_one, far_one, padded, moved, stacked, total, pairs = rest[4:]
+        kept, sent, grads, near_one, far_one, moved, stacked, total, pairs = rest[4:]
         mine, theirs = both_columns(rest[:4])
         weights = placed_weights(spot, masks, mine, theirs, pairs)
     else:
-        full, total, grads, near_one, far_one, padded, moved, stacked = rest
+        full, total, grads, near_one, far_one, moved, stacked = rest
         weights = plain_weights(full)
-    fill_padded(spot, padded, own, near, far)
 
     def finish(x, y, value):
         value = (value * slope[x, y]).astype(bf16)
@@ -247,17 +249,18 @@
     data_layers(padded, weights, finish, range(out.shape[0]))
 
 
-def first_column(part, far_part, extra, pair, handed):
-    pair[0] = part[...]
-    pair[1] = far_part[...]
-    handed[...] = extra[...]
-
-
-def second_column(pair, near_pair, part, far_part, column, pair_next):
-    column[0:2] = pair[...]
-    column[2:4] = near_pair[...]
-    pair_next[0] = part[...]
-    pair_next[1] = far_part[...]
+def stack(*refs, counts):
+    ins, outs = refs[: sum(counts)], refs[sum(counts) :]
+    for count, out in zip(counts, outs):
+        at = 0
+        for part in ins[:count]:
+            if len(part.shape) < len(out.shape):
+                out[at] = part[...]
+                at += 1
+            else:
+                out[at : at + part.shape[0]] = part[...]
+                at += part.shape[0]
+        ins = ins[count:]
 
 
 def halve(spot, kept, got, kept_next, sent_next, *, bit):
@@ -268,16 +271,18 @@
         sent_next[k] = (kept[other] + got[other].astype(f32)).astype(bf16)
 
 
-def halve_and_stack(spot, kept, got, pair, other, across, kept_next, sent_next, column, handed, *, bit):
-    handed[...] = across[...]
-    halve(spot, kept, got, kept_next, sent_next, bit=bit)
-    count = pair.shape[0]
-    column[0:count] = pair[...]
-    column[count:] = other[...]
+def halve_both(spot, kept_a, got_a, kept_b, got_b, next_a, send_a, next_b, send_b, *, bit_a, bit_b):
+    halve(spot, kept_b, got_b, next_b, send_b, bit=bit_b)
+    halve(spot, kept_a, got_a, next_a, send_a, bit=bit_a)
 
 
 def last_sum(kept, got, out):
     out[...] = kept[0] + got[0].astype(f32)
+
+
+def last_sums(kept_a, got_a, kept_b, got_b, out_a, out_b):
+    last_sum(kept_a, got_a, out_a)
+    last_sum(kept_b, got_b, out_b)
 
 
 def call(body, n_smem, args, outs, scratch=(), after=(), us=0.2):
@@ -308,7 +313,8 @@
     scale = 1.0 / math.sqrt(nx * n * ny * nz)
     spot = jnp.stack([me, jnp.full((), n, me.dtype), me % 2, me // 2 % 2, me // 4 % 2, me // 8 % 2]).astype(jnp.int32)
     fast = rows % 8 == 0 and n == 1 << 4
-    masks = (0, 8, 4, 12, 2, 10, 6, 14) if fast else ()
+    masks_two = (0, 8, 4, 12, 2, 10, 6, 14) if fast else ()
+    masks_one = (0, 2, 8, 10, 4, 6, 12, 14) if fast else ()
     layer = (1,) + shape[1:]
     layers = (2,) + shape[1:]
     block = (rows, ch)
@@ -326,107 +332,117 @@
     def blocks(count, dtype=bf16):
         return ((count,) + block, dtype)
 
+    def stacked(groups, sizes, after, us=0.2):
+        parts = [part for group in groups for part in group]
+        body = functools.partial(stack, counts=[len(group) for group in groups])
+        return call(body, 0, parts, [blocks(size) for size in sizes], after=after, us=us)
+
+    terms = [blocks(n // 2, f32), blocks(n // 2)] if fast else [total]
+    work = [total, ((n // 2, 2 * rows, ch), bf16)] if fast else []
+
+    grad_two, near, far = call(
+        first_grads, 1, (spot, grad_out, pre_second, inputs), [(shape, bf16)] + [(layers, bf16)] * 2, us=20
+    )
+    far = swap_far(far)
+    near = swap(near, 1)
+    after = (grad_two,)
+    if fast:
+        pair, pair_first = stacked(
+            [(filter_second, swap(filter_second, 8)), (filter_first, swap(filter_first, 2))], (2, 2), after
+        )
+        after = (pair,)
     turned, turned_own, slope = call(
         prepare,
         0,
         (pre_first, inputs),
         [((3 * ch, cells), bf16), ((nx, ny, ch, nz), bf16), (shape, f32)],
+        after=after,
+        us=4,
     )
-    terms = [blocks(n // 2, f32), blocks(n // 2)] if fast else [total]
-    work = [total, ((n // 2, 2 * rows, ch), bf16)] if fast else []
-
-    after = (turned,)
-    if fast:
-        pair, handed = call(
-            first_column,
-            0,
-            (filter_second, swap(filter_second, 8), filter_first),
-            [blocks(2), (block, bf16)],
-            after=after,
-        )
-        after = (pair,)
-    grad_two, near, far = call(
-        first_grads,
-        1,
-        (spot, grad_out, pre_second, inputs),
-        [(shape, bf16)] + [(layers, bf16)] * 2,
-        after=after,
-    )
-    far = swap_far(far)
-    near = swap(near, 1)
+    (grads_wide,) = call(widen, 1, (spot, grad_two, near, far), [wide], after=(turned,), us=20)
     after = ()
     if fast:
-        column, pair_first = call(
-            second_column,
-            0,
-            (pair, swap(pair, 4), handed, swap(handed, 8)),
-            [blocks(4), blocks(2)],
-            after=(grad_two,),
-        )
+        column, pair_first = stacked([(pair, swap(pair, 4)), (pair_first,)], (4, 2), (grads_wide,), 20)
         after = (column,)
     *terms_two, turned_sides = call(
         functools.partial(second_filter, scale=scale, fast=fast),
         1,
-        (spot, grad_two, near, far, turned),
+        (spot, grads_wide, near, far, turned),
         terms + [((2, ny, ch, nz), bf16)],
-        [wide] + work[:1],
+        work[:1],
         after=after,
         us=2,
     )
     if fast:
         across = swap(column, 2)
-        kept_two, sent_two, column_first, across = call(
-            functools.partial(halve_and_stack, bit=3),
+        across, column_first = stacked([(swap(column, 2),), (pair_first, swap(pair_first, 8))], (4, 4), (turned_sides,), 20)
+        kept_two, sent_two = call(
+            functools.partial(halve, bit=3),
             1,
-            (spot, terms_two[0], swap(terms_two[1], 1), pair_first, swap(pair_first, 4), across),
-            [blocks(4, f32), blocks(4), blocks(4), blocks(4)],
+            (spot, terms_two[0], swap(terms_two[1], 1)),
+            [blocks(4, f32), blocks(4)],
+            after=(across,),
         )
         full_second = (column, across, swap(column, 1), swap(across, 1))
+        after = (kept_two,)
     else:
+        after = ()
         full_second = (lax.all_gather(filter_second, "gx", axis=0, tiled=True),)
 
     *terms_one, grad_one, near_one, far_one = call(
-        functools.partial(first_filter, scale=scale, masks=masks),
+        functools.partial(first_filter, scale=scale, masks=masks_two),
         1,
-        (spot, slope, grad_two, near, far, turned_own, turned_sides, *full_second),
+        (spot, slope, grads_wide, turned_own, turned_sides, *full_second),
         terms + [(shape, bf16), (layer, bf16), (layer, bf16)],
-        [wide, ((cells, 3 * ch), bf16), ((len(planes) * ch, cells), bf16)] + work,
+        [((cells, 3 * ch), bf16), ((len(planes) * ch, cells), bf16)] + work,
+        after=after,
         us=8,
     )
     near_one, far_one = swap(near_one, 1), swap_far(far_one)
 
     def finish(full, after=()):
         return call(
-            functools.partial(input_grads, masks=masks),
+            functools.partial(input_grads, masks=masks_one),
             1,
             (spot, grad_one, near_one, far_one, *full),
             [(shape, bf16)],
             [wide] + work[1:],
             after=after,
-            us=3,
+            us=5,
         )[0]
 
     if fast:
 
-        def step(kept, sent, bit, mask, count, after):
+
+        def step(kept, sent, bit, mask, count, after, us=0.2):
             return call(
                 functools.partial(halve, bit=bit),
                 1,
                 (spot, kept, swap(sent, mask)),
                 [blocks(count, f32), blocks(count)],
                 after=after,
+                us=us,
             )
 
-        kept_two, sent_two = step(kept_two, sent_two, 4, 2, 2, (grad_one,))
+        kept_two, sent_two = step(kept_two, sent_two, 4, 2, 2, (grad_one,), 20)
         kept_one, sent_one = step(*terms_one, 3, 1, 4, (kept_two,))
-        kept_two, sent_two = step(kept_two, sent_two, 5, 4, 1, (kept_one,))
-        kept_one, sent_one = step(kept_one, sent_one, 4, 2, 2, (kept_two,))
+        mine = (column_first, swap(column_first, 4))
+        kept_two, sent_two, kept_one, sent_one = call(
+            functools.partial(halve_both, bit_a=5, bit_b=4),
+            1,
+            (spot, kept_two, swap(sent_two, 4), kept_one, swap(sent_one, 2)),
+            [blocks(1, f32), blocks(1), blocks(2, f32), blocks(2)],
+            us=20,
+        )
         kept_one, sent_one = step(kept_one, sent_one, 5, 4, 1, ())
-        across_first = swap(column_first, 2)
-        mine = (column_first, across_first)
         grad_in = finish((*mine, *(swap(m, 1) for m in mine)), (kept_one,))
-        (owned_two,) = call(last_sum, 0, (kept_two, swap(sent_two, 8)), [(block, f32)])
-        (owned_one,) = call(last_sum, 0, (kept_one, swap(sent_one, 8)), [(block, f32)], after=(grad_in,))
+        owned_two, owned_one = call(
+            last_sums,
+            0,
+            (kept_two, swap(sent_two, 8), kept_one, swap(sent_one, 8)),
+            [(block, f32)] * 2,
+            after=(grad_in,),
+        )
     else:
         grad_in = finish((lax.all_gather(filter_first, "gx", axis=0, tiled=True),))
         owned_two, owned_one = (

time: 73.9 us -> 62.4 us (0.84)
  waiting for transfers between devices: 28.4 us -> 21.2 us
  starting transfers between devices: 25.5 us -> 21.9 us
    ppermute x20, waiting for transfers between devices: 28.4 us -> 21.2 us  [swap(): return lax.ppermute(array, 'gx', [(i, i ^ mask) for i in range(n)])]
    ppermute x20, starting transfers between devices: 24.2 us -> 20.6 us  [swap(): return lax.ppermute(array, 'gx', [(i, i ^ mask) for i in range(n)])]
  transfers between devices with their start and end apart: 22 -> 22, of which waited for: 13 -> 7; matrix products, arithmetic and copies ran while one was open for 0% -> 0% of each run, Pallas kernels for 11% -> 22%
where the time goes in v3:
time: 62.4 us; the launch traced here: 62.1 us
  starting transfers between devices  21.9 us (35%)
  waiting for transfers between devices  21.2 us (34%)
  Pallas kernels  14.2 us (23%)
  local copies, waits for them, and re-layouts  3.9 us (6%)
  between operations  0.85 us (1%)
    ppermute x20, waiting for transfers between devices, swap(): return lax.ppermute(array, 'gx', [(i, i ^ mask) for i in range(n)])  21.2 us
    ppermute x20, starting transfers between devices, swap(): return lax.ppermute(array, 'gx', [(i, i ^ mask) for i in range(n)])  20.6 us
    pallas_call x15, Pallas kernels, call(): pl.pallas_call(run if many else body, in_specs=[smem] * n_smem + [vmem] *...  14.2 us
    unnamed x16, local copies, waits for them, and re-layouts  3.82 us
    ppermute x2, starting transfers between devices, swap_far(): return lax.ppermute(array, 'gx', ahead + [(b, a) for a, b in ahead])  1.34 us
  transfers between devices with their start and end apart: 22, of which 7 were waited for; matrix products, arithmetic and copies ran while one was open for 0% of the time, Pallas kernels for 22%

profile of v3, /device:TPU:0, one launch (start us, length us, event | category | flops | bytes accessed | tf_op | source)
XLA Modules:
  0.0 62.1 jit_solution(17496485959539607204)
XLA Ops:
  0.6 4.1 %collective-permute-start = (bf16[216,128]{1,0:T(8,128)(2,1)}, bf16[216,128]{1,0:T(8,128)(2,1)S(1)}, u32[]{:S(2)}, u32[]{:S(2)}) collective-permute-start(bf16[216,128]{1,0:T(8,128)(2,1)} %refs_0_.2), channel_id=1, source_target_pairs={{0,8},{1,9},{2,10},{3,11},{4,12},{5,13},{6,14},{7,15},{8,0},{9,1},... | collective-permute-start | bytes 165896 | tf_op jit(solution)/shard_map/ppermute | solution.py:326
  4.7 1.5 %collective-permute-start.1 = (bf16[216,128]{1,0:T(8,128)(2,1)}, bf16[216,128]{1,0:T(8,128)(2,1)S(1)}, u32[]{:S(2)}, u32[]{:S(2)}) collective-permute-start(bf16[216,128]{1,0:T(8,128)(2,1)} %refs_2_.1), channel_id=1, source_target_pairs={{0,2},{1,3},{2,0},{3,1},{4,6},{5,7},{6,4},{7,5},{8,10},{9,11},{10,... | collective-permute-start | bytes 165896 | tf_op jit(solution)/shard_map/ppermute | solution.py:326
  6.3 0.9 %copy-done = bf16[2,4,128,128]{3,2,1,0:T(8,128)(2,1)S(1)} copy-done((bf16[2,4,128,128]{3,2,1,0:T(8,128)(2,1)S(1)}, bf16[2,4,128,128]{3,2,1,0:T(8,128)(2,1)}, u32[]{:S(2)}) %copy-start) | copy-done | bytes 262168
  7.3 0.9 %copy-done.1 = bf16[2,4,128,128]{3,2,1,0:T(8,128)(2,1)S(1)} copy-done((bf16[2,4,128,128]{3,2,1,0:T(8,128)(2,1)S(1)}, bf16[2,4,128,128]{3,2,1,0:T(8,128)(2,1)}, u32[]{:S(2)}) %copy-start.1) | copy-done | bytes 262168
  8.2 0.9 %copy-done.3 = bf16[2,4,128,128]{3,2,1,0:T(8,128)(2,1)S(1)} copy-done((bf16[2,4,128,128]{3,2,1,0:T(8,128)(2,1)S(1)}, bf16[2,4,128,128]{3,2,1,0:T(8,128)(2,1)}, u32[]{:S(2)}) %copy-start.3) | copy-done | bytes 262168
  9.2 0.8 %shard_map.85 = (bf16[2,4,128,128]{3,2,1,0:T(8,128)(2,1)S(1)}, bf16[2,4,128,128]{3,2,1,0:T(8,128)(2,1)S(1)}, bf16[2,4,128,128]{3,2,1,0:T(8,128)(2,1)S(1)}) custom-call(s32[6]{0:T(128)S(1)} %stack.23.spot.refs_0_, bf16[2,4,128,128]{3,2,1,0:T(8,128)(2,1)S(1)} %copy-done, bf16[2,4,128,128]{3,2,1,0:T(8,128)(2,1)S(1)} %copy-done.1, ...), custom_call_target="tpu_custom_call" | custom-call | flops 20000000000 | bytes 60000000 | tf_op jit(solution)/shard_map/pallas_call | solution.py:295
  10.8 3.4 %collective-permute-start.4 = (bf16[2,216,128]{2,1,0:T(8,128)(2,1)S(1)}, bf16[2,216,128]{2,1,0:T(8,128)(2,1)S(1)}, u32[]{:S(2)}, u32[]{:S(2)}) collective-permute-start(bf16[2,216,128]{2,1,0:T(8,128)(2,1)S(1)} %get-tuple-element.38.refs_2_.refs_0_), channel_id=1, source_target_pairs={{0,4},{1,5},{2,6},{3,7},{4,0},{5,1},{6,2},{7,3},{8,12},{9,13},{10,... | collective-permute-start | bytes 331784 | tf_op jit(solution)/shard_map/ppermute | solution.py:326
  15.4 5.2 %collective-permute-done.4.refs_1_ = bf16[2,216,128]{2,1,0:T(8,128)(2,1)S(1)} collective-permute-done((bf16[2,216,128]{2,1,0:T(8,128)(2,1)S(1)}, bf16[2,216,128]{2,1,0:T(8,128)(2,1)S(1)}, u32[]{:S(2)}, u32[]{:S(2)}) %collective-permute-start.4) | collective-permute-done | bytes 110624 | tf_op jit(solution)/shard_map/ppermute | solution.py:326
  20.6 1.2 %collective-permute-start.5 = (bf16[4,216,128]{2,1,0:T(8,128)(2,1)S(1)}, bf16[4,216,128]{2,1,0:T(8,128)(2,1)S(1)}, u32[]{:S(2)}, u32[]{:S(2)}) collective-permute-start(bf16[4,216,128]{2,1,0:T(8,128)(2,1)S(1)} %get-tuple-element.45.refs_5_), channel_id=1, source_target_pairs={{0,2},{1,3},{2,0},{3,1},{4,6},{5,7},{6,4},{7,5},{8,10},{9,11},{10,... | collective-permute-start | bytes 663560 | tf_op jit(solution)/shard_map/ppermute | solution.py:326
  22.2 1.8 %shard_map.90 = (f32[8,216,128]{2,1,0:T(8,128)S(1)}, bf16[8,216,128]{2,1,0:T(8,128)(2,1)S(1)}, bf16[2,4,128,128]{3,2,1,0:T(8,128)(2,1)S(1)}) custom-call(s32[6]{0:T(128)S(1)} %stack.23.spot.refs_0_, bf16[4,6,128,128]{3,2,1,0:T(8,128)(2,1)S(1)} %shard_map.88.refs_3_.refs_1_.refs_2_, bf16[2,4,128,128]{3,2,1,0:T(8,128)(2,1)S(1)} %collective-permute-done.2.refs_2_, ...), custom_call_target="tpu_custom_call" | custom-call | flops 2000000000 | bytes 6000000 | tf_op jit(solution)/shard_map/pallas_call | solution.py:295
  24.2 6.3 %collective-permute-done.6.refs_2_ = bf16[2,216,128]{2,1,0:T(8,128)(2,1)S(1)} collective-permute-done((bf16[2,216,128]{2,1,0:T(8,128)(2,1)S(1)}, bf16[2,216,128]{2,1,0:T(8,128)(2,1)S(1)}, u32[]{:S(2)}, u32[]{:S(2)}) %collective-permute-start.6) | collective-permute-done | bytes 110624 | tf_op jit(solution)/shard_map/ppermute | solution.py:326
  31.4 1.0 %collective-permute-start.15 = (bf16[4,216,128]{2,1,0:T(8,128)(2,1)S(1)}, bf16[4,216,128]{2,1,0:T(8,128)(2,1)S(1)}, u32[]{:S(2)}, u32[]{:S(2)}) collective-permute-start(bf16[4,216,128]{2,1,0:T(8,128)(2,1)S(1)} %get-tuple-element.56), channel_id=1, source_target_pairs={{0,2},{1,3},{2,0},{3,1},{4,6},{5,7},{6,4},{7,5},{8,10},{9,11},{10,... | collective-permute-start | bytes 663560 | tf_op jit(solution)/shard_map/ppermute | solution.py:326
  32.4 3.7 %shard_map.93 = (f32[8,216,128]{2,1,0:T(8,128)S(1)}, bf16[8,216,128]{2,1,0:T(8,128)(2,1)S(1)}, bf16[2,4,128,128]{3,2,1,0:T(8,128)(2,1)S(1)}, bf16[1,4,128,128]{3...) custom-call(s32[6]{0:T(128)S(1)} %stack.23.spot.refs_0_, f32[2,4,128,128]{3,2,1,0:T(8,128)S(1)} %get-tuple-element.39.refs_1_, ...), custom_call_target="tpu_custom_call" | custom-call | flops 8000000000 | bytes 24000000 | tf_op jit(solution)/shard_map/pallas_call | solution.py:295
  36.3 2.9 %collective-permute-done.15.refs_2_ = bf16[4,216,128]{2,1,0:T(8,128)(2,1)S(1)} collective-permute-done((bf16[4,216,128]{2,1,0:T(8,128)(2,1)S(1)}, bf16[4,216,128]{2,1,0:T(8,128)(2,1)S(1)}, u32[]{:S(2)}, u32[]{:S(2)}) %collective-permute-start.15) | collective-permute-done | bytes 221216 | tf_op jit(solution)/shard_map/ppermute | solution.py:326
  40.5 1.0 %collective-permute-start.18 = (bf16[4,216,128]{2,1,0:T(8,128)(2,1)S(1)}, bf16[4,216,128]{2,1,0:T(8,128)(2,1)S(1)}, u32[]{:S(2)}, u32[]{:S(2)}) collective-permute-start(bf16[4,216,128]{2,1,0:T(8,128)(2,1)S(1)} %get-tuple-element.62), channel_id=1, source_target_pairs={{0,2},{1,3},{2,0},{3,1},{4,6},{5,7},{6,4},{7,5},{8,10},{9,11},{10,... | collective-permute-start | bytes 663560 | tf_op jit(solution)/shard_map/ppermute | solution.py:326
  41.5 1.7 %collective-permute-start.16 = (bf16[2,216,128]{2,1,0:T(8,128)(2,1)S(1)}, bf16[2,216,128]{2,1,0:T(8,128)(2,1)S(1)}, u32[]{:S(2)}, u32[]{:S(2)}) collective-permute-start(bf16[2,216,128]{2,1,0:T(8,128)(2,1)S(1)} %get-tuple-element.58), channel_id=1, source_target_pairs={{0,4},{1,5},{2,6},{3,7},{4,0},{5,1},{6,2},{7,3},{8,12},{9,13},{10,... | collective-permute-start | bytes 331784 | tf_op jit(solution)/shard_map/ppermute | solution.py:326
  44.4 1.8 %collective-permute-done.16.got_a = bf16[2,216,128]{2,1,0:T(8,128)(2,1)S(1)} collective-permute-done((bf16[2,216,128]{2,1,0:T(8,128)(2,1)S(1)}, bf16[2,216,128]{2,1,0:T(8,128)(2,1)S(1)}, u32[]{:S(2)}, u32[]{:S(2)}) %collective-permute-start.16) | collective-permute-done | bytes 110624 | tf_op jit(solution)/shard_map/ppermute | solution.py:326
  48.1 1.5 %collective-permute-start.19 = (bf16[2,216,128]{2,1,0:T(8,128)(2,1)S(1)}, bf16[2,216,128]{2,1,0:T(8,128)(2,1)S(1)}, u32[]{:S(2)}, u32[]{:S(2)}) collective-permute-start(bf16[2,216,128]{2,1,0:T(8,128)(2,1)S(1)} %get-tuple-element.64), channel_id=1, source_target_pairs={{0,4},{1,5},{2,6},{3,7},{4,0},{5,1},{6,2},{7,3},{8,12},{9,13},{10,... | collective-permute-start | bytes 331784 | tf_op jit(solution)/shard_map/ppermute | solution.py:326
  49.6 3.5 %collective-permute-done.19.got = bf16[2,216,128]{2,1,0:T(8,128)(2,1)S(1)} collective-permute-done((bf16[2,216,128]{2,1,0:T(8,128)(2,1)S(1)}, bf16[2,216,128]{2,1,0:T(8,128)(2,1)S(1)}, u32[]{:S(2)}, u32[]{:S(2)}) %collective-permute-start.19) | collective-permute-done | bytes 110624 | tf_op jit(solution)/shard_map/ppermute | solution.py:326
  53.1 1.1 %collective-permute-start.20 = (bf16[1,216,128]{2,1,0:T(8,128)(2,1)S(1)}, bf16[1,216,128]{2,1,0:T(8,128)(2,1)S(1)}, u32[]{:S(2)}, u32[]{:S(2)}) collective-permute-start(bf16[1,216,128]{2,1,0:T(8,128)(2,1)S(1)} %get-tuple-element.67), channel_id=1, source_target_pairs={{0,8},{1,9},{2,10},{3,11},{4,12},{5,13},{6,14},{7,15},{8,0},{9,1},... | collective-permute-start | bytes 165896 | tf_op jit(solution)/shard_map/ppermute | solution.py:326
  54.8 1.9 %collective-permute-start.21 = (bf16[1,216,128]{2,1,0:T(8,128)(2,1)S(1)}, bf16[1,216,128]{2,1,0:T(8,128)(2,1)S(1)}, u32[]{:S(2)}, u32[]{:S(2)}) collective-permute-start(bf16[1,216,128]{2,1,0:T(8,128)(2,1)S(1)} %get-tuple-element.68), channel_id=1, source_target_pairs={{0,8},{1,9},{2,10},{3,11},{4,12},{5,13},{6,14},{7,15},{8,0},{9,1},... | collective-permute-start | bytes 165896 | tf_op jit(solution)/shard_map/ppermute | solution.py:326
  56.7 3.0 %shard_map.98.refs_4_ = bf16[2,4,128,128]{3,2,1,0:T(8,128)(2,1)} custom-call(s32[6]{0:T(128)S(1)} %stack.23.spot.refs_0_, bf16[2,4,128,128]{3,2,1,0:T(8,128)(2,1)S(1)} %get-tuple-element.52.refs_3_.refs_1_, bf16[1,4,128,128]{3,2,1,0:T(8,128)(2,1)S(1)} %collective-permute-done.10.refs_2_, bf16[1,4,128,128]{3,2,1,0:T(8,128)(2,1)S(1)} %collective-permute-done.11.refs_3_, ...), custom_call_target="tpu_custom_call" | custom-call | flops 5000000000 | bytes 15000000 | tf_op jit(solution)/shard_map/pallas_call | solution.py:295
  59.6 0.8 %collective-permute-done.21.refs_3_ = bf16[1,216,128]{2,1,0:T(8,128)(2,1)S(1)} collective-permute-done((bf16[1,216,128]{2,1,0:T(8,128)(2,1)S(1)}, bf16[1,216,128]{2,1,0:T(8,128)(2,1)S(1)}, u32[]{:S(2)}, u32[]{:S(2)}) %collective-permute-start.21) | collective-permute-done | bytes 55328 | tf_op jit(solution)/shard_map/ppermute | solution.py:326
  60.4 0.9 %copy-done.7 = bf16[2,4,128,128]{3,2,1,0:T(8,128)(2,1)S(1)} copy-done((bf16[2,4,128,128]{3,2,1,0:T(8,128)(2,1)S(1)}, bf16[2,4,128,128]{3,2,1,0:T(8,128)(2,1)}, u32[]{:S(2)}) %copy-start.7) | copy-done | bytes 262168
  (52 shorter events, 9.2 us)
Async XLA Ops:
  0.6 10.1 %collective-permute-start = (bf16[216,128]{1,0:T(8,128)(2,1)}, bf16[216,128]{1,0:T(8,128)(2,1)S(1)}, u32[]{:S(2)}, u32[]{:S(2)}) collective-permute-start(bf16[216,128]{1,0:T(8,128)(2,1)} %refs_0_.2), channel_id=1, source_target_pairs={{0,8},{1,9},{2,10},{3,11},{4,12},{5,13},{6,14},{7,15},{8,0},{9,1},... | collective-permute-start | bytes 165896 | tf_op jit(solution)/shard_map/ppermute | solution.py:326
  4.7 6.0 %collective-permute-start.1 = (bf16[216,128]{1,0:T(8,128)(2,1)}, bf16[216,128]{1,0:T(8,128)(2,1)S(1)}, u32[]{:S(2)}, u32[]{:S(2)}) collective-permute-start(bf16[216,128]{1,0:T(8,128)(2,1)} %refs_2_.1), channel_id=1, source_target_pairs={{0,2},{1,3},{2,0},{3,1},{4,6},{5,7},{6,4},{7,5},{8,10},{9,11},{10,... | collective-permute-start | bytes 165896 | tf_op jit(solution)/shard_map/ppermute | solution.py:326
  10.0 4.8 %collective-permute-start.2 = (bf16[2,4,128,128]{3,2,1,0:T(8,128)(2,1)S(1)}, bf16[2,4,128,128]{3,2,1,0:T(8,128)(2,1)S(1)}, u32[]{:S(2)}, u32[]{:S(2)}) collective-permute-start(bf16[2,4,128,128]{3,2,1,0:T(8,128)(2,1)S(1)} %get-tuple-element.40), channel_id=1, source_target_pairs={{0,1},{1,0},{2,3},{3,2},{4,5},{5,4},{6,7},{7,6},{8,9},{9,8},{10,11... | collective-permute-start | bytes 786440 | tf_op jit(solution)/shard_map/ppermute | solution.py:326
  10.1 4.7 %collective-permute-start.3 = (bf16[2,4,128,128]{3,2,1,0:T(8,128)(2,1)S(1)}, bf16[2,4,128,128]{3,2,1,0:T(8,128)(2,1)S(1)}, u32[]{:S(2)}, u32[]{:S(2)}) collective-permute-start(bf16[2,4,128,128]{3,2,1,0:T(8,128)(2,1)S(1)} %get-tuple-element.41), channel_id=1, source_target_pairs={{1,2},{3,4},{5,6},{7,8},{9,10},{11,12},{13,14},{2,1},{4,3},{6,5},{... | collective-permute-start | bytes 786440 | tf_op jit(solution)/shard_map/ppermute | solution.py:330
  10.8 3.4 %copy-start.2 = (bf16[2,4,128,128]{3,2,1,0:T(8,128)(2,1)S(1)}, bf16[2,4,128,128]{3,2,1,0:T(8,128)(2,1)}, u32[]{:S(2)}) copy-start(bf16[2,4,128,128]{3,2,1,0:T(8,128)(2,1)} %refs_0_.3) | copy-start | bytes 786436
  10.8 3.4 %copy-start.4 = (bf16[2,4,128,128]{3,2,1,0:T(8,128)(2,1)S(1)}, bf16[2,4,128,128]{3,2,1,0:T(8,128)(2,1)}, u32[]{:S(2)}) copy-start(bf16[2,4,128,128]{3,2,1,0:T(8,128)(2,1)} %refs_1_.1) | copy-start | bytes 786436
  10.8 9.8 %collective-permute-start.4 = (bf16[2,216,128]{2,1,0:T(8,128)(2,1)S(1)}, bf16[2,216,128]{2,1,0:T(8,128)(2,1)S(1)}, u32[]{:S(2)}, u32[]{:S(2)}) collective-permute-start(bf16[2,216,128]{2,1,0:T(8,128)(2,1)S(1)} %get-tuple-element.38.refs_2_.refs_0_), channel_id=1, source_target_pairs={{0,4},{1,5},{2,6},{3,7},{4,0},{5,1},{6,2},{7,3},{8,12},{9,13},{10,... | collective-permute-start | bytes 331784 | tf_op jit(solution)/shard_map/ppermute | solution.py:326
  20.6 9.9 %collective-permute-start.5 = (bf16[4,216,128]{2,1,0:T(8,128)(2,1)S(1)}, bf16[4,216,128]{2,1,0:T(8,128)(2,1)S(1)}, u32[]{:S(2)}, u32[]{:S(2)}) collective-permute-start(bf16[4,216,128]{2,1,0:T(8,128)(2,1)S(1)} %get-tuple-element.45.refs_5_), channel_id=1, source_target_pairs={{0,2},{1,3},{2,0},{3,1},{4,6},{5,7},{6,4},{7,5},{8,10},{9,11},{10,... | collective-permute-start | bytes 663560 | tf_op jit(solution)/shard_map/ppermute | solution.py:326
  21.8 10.6 %collective-permute-start.7 = (bf16[4,216,128]{2,1,0:T(8,128)(2,1)S(1)}, bf16[4,216,128]{2,1,0:T(8,128)(2,1)S(1)}, u32[]{:S(2)}, u32[]{:S(2)}) collective-permute-start(bf16[4,216,128]{2,1,0:T(8,128)(2,1)S(1)} %get-tuple-element.45.refs_5_), channel_id=1, source_target_pairs={{0,1},{1,0},{2,3},{3,2},{4,5},{5,4},{6,7},{7,6},{8,9},{9,8},{10,11... | collective-permute-start | bytes 663560 | tf_op jit(solution)/shard_map/ppermute | solution.py:326
  21.8 8.7 %collective-permute-start.6 = (bf16[2,216,128]{2,1,0:T(8,128)(2,1)S(1)}, bf16[2,216,128]{2,1,0:T(8,128)(2,1)S(1)}, u32[]{:S(2)}, u32[]{:S(2)}) collective-permute-start(bf16[2,216,128]{2,1,0:T(8,128)(2,1)S(1)} %get-tuple-element.47.refs_1_), channel_id=1, source_target_pairs={{0,8},{1,9},{2,10},{3,11},{4,12},{5,13},{6,14},{7,15},{8,0},{9,1},... | collective-permute-start | bytes 331784 | tf_op jit(solution)/shard_map/ppermute | solution.py:326
  24.0 6.7 %collective-permute-start.9 = (bf16[8,216,128]{2,1,0:T(8,128)(2,1)S(1)}, bf16[8,216,128]{2,1,0:T(8,128)(2,1)S(1)}, u32[]{:S(2)}, u32[]{:S(2)}) collective-permute-start(bf16[8,216,128]{2,1,0:T(8,128)(2,1)S(1)} %get-tuple-element.50), channel_id=1, source_target_pairs={{0,1},{1,0},{2,3},{3,2},{4,5},{5,4},{6,7},{7,6},{8,9},{9,8},{10,11... | collective-permute-start | bytes 1327112 | tf_op jit(solution)/shard_map/ppermute | solution.py:326
  30.6 1.8 %collective-permute-start.8 = (bf16[4,216,128]{2,1,0:T(8,128)(2,1)S(1)}, bf16[4,216,128]{2,1,0:T(8,128)(2,1)S(1)}, u32[]{:S(2)}, u32[]{:S(2)}) collective-permute-start(bf16[4,216,128]{2,1,0:T(8,128)(2,1)S(1)} %get-tuple-element.48.refs_3_.refs_6_), channel_id=1, source_target_pairs={{0,1},{1,0},{2,3},{3,2},{4,5},{5,4},{6,7},{7,6},{8,9},{9,8},{10,11... | collective-permute-start | bytes 663560 | tf_op jit(solution)/shard_map/ppermute | solution.py:326
  30.7 13.0 %collective-permute-start.12 = (bf16[4,216,128]{2,1,0:T(8,128)(2,1)S(1)}, bf16[4,216,128]{2,1,0:T(8,128)(2,1)S(1)}, u32[]{:S(2)}, u32[]{:S(2)}) collective-permute-start(bf16[4,216,128]{2,1,0:T(8,128)(2,1)S(1)} %get-tuple-element.55.refs_4_), channel_id=1, source_target_pairs={{0,4},{1,5},{2,6},{3,7},{4,0},{5,1},{6,2},{7,3},{8,12},{9,13},{10,... | collective-permute-start | bytes 663560 | tf_op jit(solution)/shard_map/ppermute | solution.py:326
  31.4 7.8 %collective-permute-start.15 = (bf16[4,216,128]{2,1,0:T(8,128)(2,1)S(1)}, bf16[4,216,128]{2,1,0:T(8,128)(2,1)S(1)}, u32[]{:S(2)}, u32[]{:S(2)}) collective-permute-start(bf16[4,216,128]{2,1,0:T(8,128)(2,1)S(1)} %get-tuple-element.56), channel_id=1, source_target_pairs={{0,2},{1,3},{2,0},{3,1},{4,6},{5,7},{6,4},{7,5},{8,10},{9,11},{10,... | collective-permute-start | bytes 663560 | tf_op jit(solution)/shard_map/ppermute | solution.py:326
  36.1 3.8 %collective-permute-start.17 = (bf16[8,216,128]{2,1,0:T(8,128)(2,1)S(1)}, bf16[8,216,128]{2,1,0:T(8,128)(2,1)S(1)}, u32[]{:S(2)}, u32[]{:S(2)}) collective-permute-start(bf16[8,216,128]{2,1,0:T(8,128)(2,1)S(1)} %get-tuple-element.60), channel_id=1, source_target_pairs={{0,1},{1,0},{2,3},{3,2},{4,5},{5,4},{6,7},{7,6},{8,9},{9,8},{10,11... | collective-permute-start | bytes 1327112 | tf_op jit(solution)/shard_map/ppermute | solution.py:326
  40.5 7.0 %collective-permute-start.18 = (bf16[4,216,128]{2,1,0:T(8,128)(2,1)S(1)}, bf16[4,216,128]{2,1,0:T(8,128)(2,1)S(1)}, u32[]{:S(2)}, u32[]{:S(2)}) collective-permute-start(bf16[4,216,128]{2,1,0:T(8,128)(2,1)S(1)} %get-tuple-element.62), channel_id=1, source_target_pairs={{0,2},{1,3},{2,0},{3,1},{4,6},{5,7},{6,4},{7,5},{8,10},{9,11},{10,... | collective-permute-start | bytes 663560 | tf_op jit(solution)/shard_map/ppermute | solution.py:326
  41.5 4.7 %collective-permute-start.16 = (bf16[2,216,128]{2,1,0:T(8,128)(2,1)S(1)}, bf16[2,216,128]{2,1,0:T(8,128)(2,1)S(1)}, u32[]{:S(2)}, u32[]{:S(2)}) collective-permute-start(bf16[2,216,128]{2,1,0:T(8,128)(2,1)S(1)} %get-tuple-element.58), channel_id=1, source_target_pairs={{0,4},{1,5},{2,6},{3,7},{4,0},{5,1},{6,2},{7,3},{8,12},{9,13},{10,... | collective-permute-start | bytes 331784 | tf_op jit(solution)/shard_map/ppermute | solution.py:326
  43.2 11.5 %collective-permute-start.13 = (bf16[4,216,128]{2,1,0:T(8,128)(2,1)S(1)}, bf16[4,216,128]{2,1,0:T(8,128)(2,1)S(1)}, u32[]{:S(2)}, u32[]{:S(2)}) collective-permute-start(bf16[4,216,128]{2,1,0:T(8,128)(2,1)S(1)} %get-tuple-element.55.refs_4_), channel_id=1, source_target_pairs={{0,1},{1,0},{2,3},{3,2},{4,5},{5,4},{6,7},{7,6},{8,9},{9,8},{10,11... | collective-permute-start | bytes 663560 | tf_op jit(solution)/shard_map/ppermute | solution.py:326
  43.2 13.5 %collective-permute-start.10 = (bf16[1,4,128,128]{3,2,1,0:T(8,128)(2,1)S(1)}, bf16[1,4,128,128]{3,2,1,0:T(8,128)(2,1)S(1)}, u32[]{:S(2)}, u32[]{:S(2)}) collective-permute-start(bf16[1,4,128,128]{3,2,1,0:T(8,128)(2,1)S(1)} %get-tuple-element.53), channel_id=1, source_target_pairs={{0,1},{1,0},{2,3},{3,2},{4,5},{5,4},{6,7},{7,6},{8,9},{9,8},{10,11... | collective-permute-start | bytes 393224 | tf_op jit(solution)/shard_map/ppermute | solution.py:326
  43.7 12.9 %collective-permute-start.11 = (bf16[1,4,128,128]{3,2,1,0:T(8,128)(2,1)S(1)}, bf16[1,4,128,128]{3,2,1,0:T(8,128)(2,1)S(1)}, u32[]{:S(2)}, u32[]{:S(2)}) collective-permute-start(bf16[1,4,128,128]{3,2,1,0:T(8,128)(2,1)S(1)} %get-tuple-element.54), channel_id=1, source_target_pairs={{1,2},{3,4},{5,6},{7,8},{9,10},{11,12},{13,14},{2,1},{4,3},{6,5},{... | collective-permute-start | bytes 393224 | tf_op jit(solution)/shard_map/ppermute | solution.py:330
  46.2 10.5 %collective-permute-start.14 = (bf16[4,216,128]{2,1,0:T(8,128)(2,1)S(1)}, bf16[4,216,128]{2,1,0:T(8,128)(2,1)S(1)}, u32[]{:S(2)}, u32[]{:S(2)}) collective-permute-start(bf16[4,216,128]{2,1,0:T(8,128)(2,1)S(1)} %collective-permute-done.12.refs_5_), channel_id=1, source_target_pairs={{0,1},{1,0},{2,3},{3,2},{4,5},{5,4},{6,7},{7,6},{8,9},{9,8},{10,11... | collective-permute-start | bytes 663560 | tf_op jit(solution)/shard_map/ppermute | solution.py:326
  48.1 5.0 %collective-permute-start.19 = (bf16[2,216,128]{2,1,0:T(8,128)(2,1)S(1)}, bf16[2,216,128]{2,1,0:T(8,128)(2,1)S(1)}, u32[]{:S(2)}, u32[]{:S(2)}) collective-permute-start(bf16[2,216,128]{2,1,0:T(8,128)(2,1)S(1)} %get-tuple-element.64), channel_id=1, source_target_pairs={{0,4},{1,5},{2,6},{3,7},{4,0},{5,1},{6,2},{7,3},{8,12},{9,13},{10,... | collective-permute-start | bytes 331784 | tf_op jit(solution)/shard_map/ppermute | solution.py:326
  53.1 6.6 %collective-permute-start.20 = (bf16[1,216,128]{2,1,0:T(8,128)(2,1)S(1)}, bf16[1,216,128]{2,1,0:T(8,128)(2,1)S(1)}, u32[]{:S(2)}, u32[]{:S(2)}) collective-permute-start(bf16[1,216,128]{2,1,0:T(8,128)(2,1)S(1)} %get-tuple-element.67), channel_id=1, source_target_pairs={{0,8},{1,9},{2,10},{3,11},{4,12},{5,13},{6,14},{7,15},{8,0},{9,1},... | collective-permute-start | bytes 165896 | tf_op jit(solution)/shard_map/ppermute | solution.py:326
  54.8 5.7 %collective-permute-start.21 = (bf16[1,216,128]{2,1,0:T(8,128)(2,1)S(1)}, bf16[1,216,128]{2,1,0:T(8,128)(2,1)S(1)}, u32[]{:S(2)}, u32[]{:S(2)}) collective-permute-start(bf16[1,216,128]{2,1,0:T(8,128)(2,1)S(1)} %get-tuple-element.68), channel_id=1, source_target_pairs={{0,8},{1,9},{2,10},{3,11},{4,12},{5,13},{6,14},{7,15},{8,0},{9,1},... | collective-permute-start | bytes 165896 | tf_op jit(solution)/shard_map/ppermute | solution.py:326
  (6 other events, 7.0 us)

commit v4 on v3

--- a/solution.py
+++ b/solution.py
@@ -14,7 +14,6 @@
 planes = tuple((a, b) for a in shifts for b in shifts)
 bf16, f32 = jnp.bfloat16, jnp.float32
 vmem = pl.BlockSpec(memory_space=pltpu.VMEM)
-smem = pl.BlockSpec(memory_space=pltpu.SMEM)
 anywhere = pl.BlockSpec(memory_space=pl.ANY)
 vmem_bytes = 14 * 1024 * 1024
 
@@ -48,20 +47,17 @@
         ref[x, wide - 1] = blank
 
 
-def first_grads(spot, grad_out, pre_second, inputs, own, near, far):
+def first_grads(spot, grad_out, pre_second, own, near, far):
     nx = own.shape[0]
     for x in range(nx):
         for y in range(own.shape[1]):
             slope = slope_of(pre_second[x, y].astype(f32))
             own[x, y] = (grad_out[x, y].astype(f32) * slope).astype(bf16)
     send_edges(spot, own, near, far)
-    at = near_edge(spot, nx - 1)
-    near[1] = inputs[at]
-    far[1] = inputs[nx - 1 - at]
 
 
 def near_edge(spot, last):
-    return last * (1 - spot[2])
+    return last * (1 - spot[1])
 
 
 def send_edges(spot, own, near, far):
@@ -87,7 +83,7 @@
             emit(i + j, part[:, j * ch : (j + 1) * ch])
 
 
-def prepare(pre_first, inputs, turned, turned_own, slope):
+def prepare(spot, pre_first, inputs, turned, turned_own, slope):
     nx, ny, nz, ch = pre_first.shape
     for x in range(nx):
         for y in range(ny):
@@ -161,11 +157,11 @@
 
 
 def placed_weights(spot, masks, mine, theirs, pairs):
-    even = spot[2] == 0
+    even = spot[1] == 0
     for mask, first, second in zip(masks, mine, theirs):
         one, two = first[...].astype(f32), second[...].astype(f32)
         both = jnp.concatenate([jnp.where(even, one, two), jnp.where(even, two, one)], axis=0)
-        pairs[lax.bitwise_xor(spot[0] // 2, mask // 2)] = both.astype(bf16)
+        pairs[lax.bitwise_xor(spot[0] >> 1, mask // 2)] = both.astype(bf16)
     wide, ch = pairs.shape[1:]
 
     def weights(plane):
@@ -180,10 +176,8 @@
     return weights
 
 
-def second_filter(spot, padded, near, far, turned, *rest, scale, fast):
+def second_filter(spot, padded, turned, *rest, scale, fast):
     total, outs = (rest[-1], rest[:2]) if fast else (rest[0], ())
-    turned_sides = rest[2] if fast else rest[1]
-    ny = near.shape[1]
 
     def emit(plane, part):
         ch = part.shape[1]
@@ -191,11 +185,20 @@
 
     filter_terms(turned, padded, emit, scale)
     if fast:
-        split_halves(total, spot[2], *outs)
+        split_halves(total, spot[1], *outs)
+
+def turn_sides(spot, near, far, turned_sides):
     high = near_edge(spot, 1)
-    for y in range(ny):
-        turned_sides[high, y] = near[1, y].astype(f32).T.astype(bf16)
-        turned_sides[1 - high, y] = far[1, y].astype(f32).T.astype(bf16)
+    for y in range(near.shape[1]):
+        turned_sides[high, y] = near[0, y].astype(f32).T.astype(bf16)
+        turned_sides[1 - high, y] = far[0, y].astype(f32).T.astype(bf16)
+
+
+def stack_and_edges(spot, pair, other, inputs, column, near, far):
+    count = pair.shape[0]
+    column[0:count] = pair[...]
+    column[count:] = other[...]
+    send_edges(spot, inputs, near, far)
 
 
 def both_columns(lists):
@@ -230,12 +233,16 @@
             at = (i * len(shifts) + k) * ch
             total[at : at + ch] = part[i * ch : (i + 1) * ch, k * ch : (k + 1) * ch]
     if masks:
-        split_halves(total, spot[2], kept, sent)
+        split_halves(total, spot[1], kept, sent)
 
 
 def input_grads(spot, own, near, far, *rest, masks):
     if masks:
-        lists, (out, padded, pairs) = rest[:4], rest[4:]
+        lists, rest = rest[:4], rest[4:]
+        (padded, pairs), rest = rest[-2:], rest[:-2]
+        kept, kept_two, got_two, out, kept_on, sum_two = rest
+        kept_on[...] = kept[...]
+        last_sum(kept_two, got_two, sum_two)
         mine, theirs = both_columns(lists)
         weights = placed_weights(spot, masks, mine, theirs, pairs)
     else:
@@ -264,37 +271,38 @@
 
 
 def halve(spot, kept, got, kept_next, sent_next, *, bit):
-    side = spot[bit]
+    side = spot[bit - 1]
     for k in range(kept_next.shape[0]):
         mine, other = 2 * k + side, 2 * k + 1 - side
         kept_next[k] = kept[mine] + got[mine].astype(f32)
         sent_next[k] = (kept[other] + got[other].astype(f32)).astype(bf16)
 
 
-def halve_both(spot, kept_a, got_a, kept_b, got_b, next_a, send_a, next_b, send_b, *, bit_a, bit_b):
-    halve(spot, kept_b, got_b, next_b, send_b, bit=bit_b)
-    halve(spot, kept_a, got_a, next_a, send_a, bit=bit_a)
+def halve_and_pass(spot, kept, got, near, far, kept_next, sent_next, near_on, far_on, *, bit):
+    halve(spot, kept, got, kept_next, sent_next, bit=bit)
+    near_on[...] = near[...]
+    far_on[...] = far[...]
 
 
 def last_sum(kept, got, out):
     out[...] = kept[0] + got[0].astype(f32)
 
 
-def last_sums(kept_a, got_a, kept_b, got_b, out_a, out_b):
-    last_sum(kept_a, got_a, out_a)
-    last_sum(kept_b, got_b, out_b)
-
-
 def call(body, n_smem, args, outs, scratch=(), after=(), us=0.2):
-    first = len(args)
-    many = len(after)
+    args = args[n_smem:]
+    first, many = len(args), len(after)
 
     def run(*refs):
-        body(*refs[:first], *refs[first + many :])
+        refs = refs[:first] + refs[first + many :]
+        if n_smem:
+            me = lax.axis_index("gx")
+            body([me] + [(me >> k) & 1 for k in range(4)], *refs)
+        else:
+            body(*refs)
 
     return pl.pallas_call(
-        run if many else body,
-        in_specs=[smem] * n_smem + [vmem] * (len(args) - n_smem) + [anywhere] * many,
+        run,
+        in_specs=[vmem] * first + [anywhere] * many,
         out_specs=[vmem] * len(outs),
         out_shape=[jax.ShapeDtypeStruct(s, d) for s, d in outs],
         scratch_shapes=[pltpu.VMEM(s, d) for s, d in scratch],
@@ -311,12 +319,11 @@
     rows = filter_first.shape[0]
     taps = n * rows // ch
     scale = 1.0 / math.sqrt(nx * n * ny * nz)
-    spot = jnp.stack([me, jnp.full((), n, me.dtype), me % 2, me // 2 % 2, me // 4 % 2, me // 8 % 2]).astype(jnp.int32)
+    spot = None
     fast = rows % 8 == 0 and n == 1 << 4
     masks_two = (0, 8, 4, 12, 2, 10, 6, 14) if fast else ()
     masks_one = (0, 2, 8, 10, 4, 6, 12, 14) if fast else ()
     layer = (1,) + shape[1:]
-    layers = (2,) + shape[1:]
     block = (rows, ch)
     wide = ((nx + 2, ny + 2, nz, ch), bf16)
     cells = nx * ny * nz
@@ -341,7 +348,7 @@
     work = [total, ((n // 2, 2 * rows, ch), bf16)] if fast else []
 
     grad_two, near, far = call(
-        first_grads, 1, (spot, grad_out, pre_second, inputs), [(shape, bf16)] + [(layers, bf16)] * 2, us=20
+        first_grads, 1, (spot, grad_out, pre_second), [(shape, bf16), (layer, bf16), (layer, bf16)], us=20
     )
     far = swap_far(far)
     near = swap(near, 1)
@@ -353,41 +360,55 @@
         after = (pair,)
     turned, turned_own, slope = call(
         prepare,
-        0,
-        (pre_first, inputs),
+        1,
+        (spot, pre_first, inputs),
         [((3 * ch, cells), bf16), ((nx, ny, ch, nz), bf16), (shape, f32)],
         after=after,
         us=4,
     )
     (grads_wide,) = call(widen, 1, (spot, grad_two, near, far), [wide], after=(turned,), us=20)
-    after = ()
-    if fast:
-        column, pair_first = stacked([(pair, swap(pair, 4)), (pair_first,)], (4, 2), (grads_wide,), 20)
+    sides = ((2, ny, ch, nz), bf16)
+    if fast:
+        column, near_in, far_in = call(
+            stack_and_edges,
+            1,
+            (spot, pair, swap(pair, 4), inputs),
+            [blocks(4), (layer, bf16), (layer, bf16)],
+            after=(grads_wide,),
+            us=20,
+        )
         after = (column,)
-    *terms_two, turned_sides = call(
+    else:
+        near_in, far_in = call(send_edges, 1, (spot, inputs), [(layer, bf16), (layer, bf16)])
+        after = ()
+    terms_two = call(
         functools.partial(second_filter, scale=scale, fast=fast),
         1,
-        (spot, grads_wide, near, far, turned),
-        terms + [((2, ny, ch, nz), bf16)],
+        (spot, grads_wide, turned),
+        terms,
         work[:1],
         after=after,
         us=2,
     )
+    near_in, far_in = swap(near_in, 1), swap_far(far_in)
     if fast:
         across = swap(column, 2)
-        across, column_first = stacked([(swap(column, 2),), (pair_first, swap(pair_first, 8))], (4, 4), (turned_sides,), 20)
+        after = (across,)
+    else:
+        full_second = (lax.all_gather(filter_second, "gx", axis=0, tiled=True),)
+        after = ()
+    (turned_sides,) = call(turn_sides, 1, (spot, near_in, far_in), [sides], after=after, us=20)
+    if fast:
         kept_two, sent_two = call(
             functools.partial(halve, bit=3),
             1,
             (spot, terms_two[0], swap(terms_two[1], 1)),
             [blocks(4, f32), blocks(4)],
-            after=(across,),
-        )
+            after=(turned_sides,),
+        )
+        (column_first,) = stacked([(pair_first, swap(pair_first, 8))], (4,), (kept_two,))
+        after = (column_first,)
         full_second = (column, across, swap(column, 1), swap(across, 1))
-        after = (kept_two,)
-    else:
-        after = ()
-        full_second = (lax.all_gather(filter_second, "gx", axis=0, tiled=True),)
 
     *terms_one, grad_one, near_one, far_one = call(
         functools.partial(first_filter, scale=scale, masks=masks_two),
@@ -398,21 +419,19 @@
         after=after,
         us=8,
     )
-    near_one, far_one = swap(near_one, 1), swap_far(far_one)
-
-    def finish(full, after=()):
+
+    def finish(near, far, full, sums=()):
+        sizes = [blocks(1, f32), (block, f32)] if sums else []
         return call(
             functools.partial(input_grads, masks=masks_one),
             1,
-            (spot, grad_one, near_one, far_one, *full),
-            [(shape, bf16)],
+            (spot, grad_one, swap(near, 1), swap_far(far), *full, *sums),
+            [(shape, bf16)] + sizes,
             [wide] + work[1:],
-            after=after,
             us=5,
-        )[0]
-
-    if fast:
-
+        )
+
+    if fast:
 
         def step(kept, sent, bit, mask, count, after, us=0.2):
             return call(
@@ -427,24 +446,24 @@
         kept_two, sent_two = step(kept_two, sent_two, 4, 2, 2, (grad_one,), 20)
         kept_one, sent_one = step(*terms_one, 3, 1, 4, (kept_two,))
         mine = (column_first, swap(column_first, 4))
-        kept_two, sent_two, kept_one, sent_one = call(
-            functools.partial(halve_both, bit_a=5, bit_b=4),
+        full_first = (*mine, *(swap(m, 1) for m in mine))
+        kept_two, sent_two = step(kept_two, sent_two, 5, 4, 1, (kept_one, *full_first), 20)
+        got_two = swap(sent_two, 8)
+        kept_one, sent_one, near_one, far_one = call(
+            functools.partial(halve_and_pass, bit=4),
             1,
-            (spot, kept_two, swap(sent_two, 4), kept_one, swap(sent_one, 2)),
-            [blocks(1, f32), blocks(1), blocks(2, f32), blocks(2)],
+            (spot, kept_one, swap(sent_one, 2), near_one, far_one),
+            [blocks(2, f32), blocks(2), (layer, bf16), (layer, bf16)],
+            after=(kept_two,),
             us=20,
         )
-        kept_one, sent_one = step(kept_one, sent_one, 5, 4, 1, ())
-        grad_in = finish((*mine, *(swap(m, 1) for m in mine)), (kept_one,))
-        owned_two, owned_one = call(
-            last_sums,
-            0,
-            (kept_two, swap(sent_two, 8), kept_one, swap(sent_one, 8)),
-            [(block, f32)] * 2,
-            after=(grad_in,),
-        )
+        kept_one, sent_one = step(kept_one, sent_one, 5, 4, 1, (), 1.5)
+        grad_in, kept_one, owned_two = finish(
+            near_one, far_one, full_first, (kept_one, kept_two, got_two)
+        )
+        (owned_one,) = call(last_sum, 0, (kept_one, swap(sent_one, 8)), [(block, f32)])
     else:
-        grad_in = finish((lax.all_gather(filter_first, "gx", axis=0, tiled=True),))
+        (grad_in,) = finish(near_one, far_one, (lax.all_gather(filter_first, "gx", axis=0, tiled=True),))
         owned_two, owned_one = (
             lax.psum_scatter(t[0], "gx", scatter_dimension=0, tiled=True) for t in (terms_two, terms_one)
         )

time: 62.4 us -> 58.7 us (0.941)
  starting transfers between devices: 21.9 us -> 27.8 us
  Pallas kernels: 14.2 us -> 9.33 us
  waiting for transfers between devices: 21.2 us -> 18.6 us
  local copies, waits for them, and re-layouts: 3.9 us -> 1.92 us
    ppermute x20 -> x21, starting transfers between devices: 20.6 us -> 25.8 us  [swap(): return lax.ppermute(array, 'gx', [(i, i ^ mask) for i in range(n)])]
    pallas_call x15 -> x17, Pallas kernels: 14.2 us -> 9.33 us  [call(): pl.pallas_call(run, in_specs=[vmem] * first + [anywhere] * many, out_spec...]
    ppermute x20 -> x21, waiting for transfers between devices: 21.2 us -> 18.6 us  [swap(): return lax.ppermute(array, 'gx', [(i, i ^ mask) for i in range(n)])]
    unnamed x16 -> x12, local copies, waits for them, and re-layouts: 3.82 us -> 1.92 us
    ppermute x2 -> x3, starting transfers between devices: 1.34 us -> 1.98 us  [swap_far(): return lax.ppermute(array, 'gx', ahead + [(b, a) for a, b in ahead])]
  transfers between devices with their start and end apart: 22 -> 24, of which waited for: 7 -> 9; matrix products, arithmetic and copies ran while one was open for 0% -> 0% of each run, Pallas kernels for 22% -> 15%
where the time goes in v4:
time: 58.7 us; the launch traced here: 58.5 us
  starting transfers between devices  27.8 us (47%)
  waiting for transfers between devices  18.6 us (32%)
  Pallas kernels  9.33 us (16%)
  local copies, waits for them, and re-layouts  1.92 us (3%)
  between operations  0.83 us (1%)
    ppermute x21, starting transfers between devices, swap(): return lax.ppermute(array, 'gx', [(i, i ^ mask) for i in range(n)])  25.8 us
    ppermute x21, waiting for transfers between devices, swap(): return lax.ppermute(array, 'gx', [(i, i ^ mask) for i in range(n)])  18.6 us
    pallas_call x17, Pallas kernels, call(): pl.pallas_call(run, in_specs=[vmem] * first + [anywhere] * many, out_spec...  9.33 us
    ppermute x3, starting transfers between devices, swap_far(): return lax.ppermute(array, 'gx', ahead + [(b, a) for a, b in ahead])  1.98 us
    unnamed x12, local copies, waits for them, and re-layouts  1.92 us
  transfers between devices with their start and end apart: 24, of which 9 were waited for; matrix products, arithmetic and copies ran while one was open for 0% of the time, Pallas kernels for 15%

profile of v4, /device:TPU:0, one launch (start us, length us, event | category | flops | bytes accessed | tf_op | source)
XLA Modules:
  0.0 58.5 jit_solution(12270004671693268907)
XLA Ops:
  0.6 3.0 %collective-permute-start.1 = (bf16[216,128]{1,0:T(8,128)(2,1)}, bf16[216,128]{1,0:T(8,128)(2,1)S(1)}, u32[]{:S(2)}, u32[]{:S(2)}) collective-permute-start(bf16[216,128]{1,0:T(8,128)(2,1)} %refs_2_.2), channel_id=1, source_target_pairs={{0,2},{1,3},{2,0},{3,1},{4,6},{5,7},{6,4},{7,5},{8,10},{9,11},{10,... | collective-permute-start | bytes 165896 | tf_op jit(solution)/shard_map/ppermute | solution.py:333
  3.6 2.6 %collective-permute-start = (bf16[216,128]{1,0:T(8,128)(2,1)}, bf16[216,128]{1,0:T(8,128)(2,1)S(1)}, u32[]{:S(2)}, u32[]{:S(2)}) collective-permute-start(bf16[216,128]{1,0:T(8,128)(2,1)} %refs_0_.4), channel_id=1, source_target_pairs={{0,8},{1,9},{2,10},{3,11},{4,12},{5,13},{6,14},{7,15},{8,0},{9,1},... | collective-permute-start | bytes 165896 | tf_op jit(solution)/shard_map/ppermute | solution.py:333
  6.2 0.9 %copy-done = bf16[2,4,128,128]{3,2,1,0:T(8,128)(2,1)S(1)} copy-done((bf16[2,4,128,128]{3,2,1,0:T(8,128)(2,1)S(1)}, bf16[2,4,128,128]{3,2,1,0:T(8,128)(2,1)}, u32[]{:S(2)}) %copy-start) | copy-done | bytes 262168
  7.2 0.9 %copy-done.1 = bf16[2,4,128,128]{3,2,1,0:T(8,128)(2,1)S(1)} copy-done((bf16[2,4,128,128]{3,2,1,0:T(8,128)(2,1)S(1)}, bf16[2,4,128,128]{3,2,1,0:T(8,128)(2,1)}, u32[]{:S(2)}) %copy-start.1) | copy-done | bytes 262168
  8.5 0.7 %collective-permute-start.3 = (bf16[1,4,128,128]{3,2,1,0:T(8,128)(2,1)S(1)}, bf16[1,4,128,128]{3,2,1,0:T(8,128)(2,1)S(1)}, u32[]{:S(2)}, u32[]{:S(2)}) collective-permute-start(bf16[1,4,128,128]{3,2,1,0:T(8,128)(2,1)S(1)} %get-tuple-element.42), channel_id=1, source_target_pairs={{1,2},{3,4},{5,6},{7,8},{9,10},{11,12},{13,14},{2,1},{4,3},{6,5},{... | collective-permute-start | bytes 393224 | tf_op jit(solution)/shard_map/ppermute | solution.py:337
  9.2 3.4 %collective-permute-start.4 = (bf16[2,216,128]{2,1,0:T(8,128)(2,1)S(1)}, bf16[2,216,128]{2,1,0:T(8,128)(2,1)S(1)}, u32[]{:S(2)}, u32[]{:S(2)}) collective-permute-start(bf16[2,216,128]{2,1,0:T(8,128)(2,1)S(1)} %get-tuple-element.39.refs_2_.refs_0_), channel_id=1, source_target_pairs={{0,4},{1,5},{2,6},{3,7},{4,0},{5,1},{6,2},{7,3},{8,12},{9,13},{10,... | collective-permute-start | bytes 331784 | tf_op jit(solution)/shard_map/ppermute | solution.py:333
  13.3 4.3 %collective-permute-done.4.refs_1_ = bf16[2,216,128]{2,1,0:T(8,128)(2,1)S(1)} collective-permute-done((bf16[2,216,128]{2,1,0:T(8,128)(2,1)S(1)}, bf16[2,216,128]{2,1,0:T(8,128)(2,1)S(1)}, u32[]{:S(2)}, u32[]{:S(2)}) %collective-permute-start.4) | collective-permute-done | bytes 110624 | tf_op jit(solution)/shard_map/ppermute | solution.py:333
  17.6 1.0 %collective-permute-start.7 = (bf16[4,216,128]{2,1,0:T(8,128)(2,1)S(1)}, bf16[4,216,128]{2,1,0:T(8,128)(2,1)S(1)}, u32[]{:S(2)}, u32[]{:S(2)}) collective-permute-start(bf16[4,216,128]{2,1,0:T(8,128)(2,1)S(1)} %get-tuple-element.47.refs_2_.refs_4_), channel_id=1, source_target_pairs={{0,2},{1,3},{2,0},{3,1},{4,6},{5,7},{6,4},{7,5},{8,10},{9,11},{10,... | collective-permute-start | bytes 663560 | tf_op jit(solution)/shard_map/ppermute | solution.py:333
  20.1 1.5 %shard_map.91 = (f32[8,216,128]{2,1,0:T(8,128)S(1)}, bf16[8,216,128]{2,1,0:T(8,128)(2,1)S(1)}) custom-call(bf16[4,6,128,128]{3,2,1,0:T(8,128)(2,1)S(1)} %shard_map.88.refs_3_.refs_0_.refs_1_, bf16[384,1024]{1,0:T(8,128)(2,1)S(1)} %get-tuple-element.43.refs_3_.refs_1_, bf16[4,216,128]{2,1,0:T(8,128)(2,1)S(1)} %get-tuple-element.47.refs_2_.refs_4_), custom_call_target="tpu_custom_call" | custom-call | flops 2000000000 | bytes 6000000 | tf_op jit(solution)/shard_map/pallas_call | solution.py:303
  21.6 3.0 %collective-permute-start.11 = (bf16[8,216,128]{2,1,0:T(8,128)(2,1)S(1)}, bf16[8,216,128]{2,1,0:T(8,128)(2,1)S(1)}, u32[]{:S(2)}, u32[]{:S(2)}) collective-permute-start(bf16[8,216,128]{2,1,0:T(8,128)(2,1)S(1)} %get-tuple-element.50), channel_id=1, source_target_pairs={{0,1},{1,0},{2,3},{3,2},{4,5},{5,4},{6,7},{7,6},{8,9},{9,8},{10,11... | collective-permute-start | bytes 1327112 | tf_op jit(solution)/shard_map/ppermute | solution.py:333
  24.9 1.2 %collective-permute-done.11.refs_1_ = bf16[8,216,128]{2,1,0:T(8,128)(2,1)S(1)} collective-permute-done((bf16[8,216,128]{2,1,0:T(8,128)(2,1)S(1)}, bf16[8,216,128]{2,1,0:T(8,128)(2,1)S(1)}, u32[]{:S(2)}, u32[]{:S(2)}) %collective-permute-start.11) | collective-permute-done | bytes 442400 | tf_op jit(solution)/shard_map/ppermute | solution.py:333
  26.9 2.3 %collective-permute-start.16 = (bf16[4,216,128]{2,1,0:T(8,128)(2,1)S(1)}, bf16[4,216,128]{2,1,0:T(8,128)(2,1)S(1)}, u32[]{:S(2)}, u32[]{:S(2)}) collective-permute-start(bf16[4,216,128]{2,1,0:T(8,128)(2,1)S(1)} %shard_map.93.refs_8_.refs_3_), channel_id=1, source_target_pairs={{0,4},{1,5},{2,6},{3,7},{4,0},{5,1},{6,2},{7,3},{8,12},{9,13},{10,... | collective-permute-start | bytes 663560 | tf_op jit(solution)/shard_map/ppermute | solution.py:333
  29.2 1.8 %collective-permute-start.13 = (bf16[4,216,128]{2,1,0:T(8,128)(2,1)S(1)}, bf16[4,216,128]{2,1,0:T(8,128)(2,1)S(1)}, u32[]{:S(2)}, u32[]{:S(2)}) collective-permute-start(bf16[4,216,128]{2,1,0:T(8,128)(2,1)S(1)} %get-tuple-element.55), channel_id=1, source_target_pairs={{0,2},{1,3},{2,0},{3,1},{4,6},{5,7},{6,4},{7,5},{8,10},{9,11},{10,... | collective-permute-start | bytes 663560 | tf_op jit(solution)/shard_map/ppermute | solution.py:333
  31.0 3.3 %shard_map.94 = (f32[8,216,128]{2,1,0:T(8,128)S(1)}, bf16[8,216,128]{2,1,0:T(8,128)(2,1)S(1)}, bf16[2,4,128,128]{3,2,1,0:T(8,128)(2,1)S(1)}, bf16[1,4,128,128]{3...) custom-call(f32[2,4,128,128]{3,2,1,0:T(8,128)S(1)} %get-tuple-element.40.refs_0_, ...), custom_call_target="tpu_custom_call" | custom-call | flops 8000000000 | bytes 24000000 | tf_op jit(solution)/shard_map/pallas_call | solution.py:303
  34.9 1.8 %collective-permute-done.13.refs_1_ = bf16[4,216,128]{2,1,0:T(8,128)(2,1)S(1)} collective-permute-done((bf16[4,216,128]{2,1,0:T(8,128)(2,1)S(1)}, bf16[4,216,128]{2,1,0:T(8,128)(2,1)S(1)}, u32[]{:S(2)}, u32[]{:S(2)}) %collective-permute-start.13) | collective-permute-done | bytes 221216 | tf_op jit(solution)/shard_map/ppermute | solution.py:333
  37.4 1.8 %collective-permute-start.14 = (bf16[4,216,128]{2,1,0:T(8,128)(2,1)S(1)}, bf16[4,216,128]{2,1,0:T(8,128)(2,1)S(1)}, u32[]{:S(2)}, u32[]{:S(2)}) collective-permute-start(bf16[4,216,128]{2,1,0:T(8,128)(2,1)S(1)} %get-tuple-element.58), channel_id=1, source_target_pairs={{0,2},{1,3},{2,0},{3,1},{4,6},{5,7},{6,4},{7,5},{8,10},{9,11},{10,... | collective-permute-start | bytes 663560 | tf_op jit(solution)/shard_map/ppermute | solution.py:333
  39.2 2.4 %collective-permute-done.15.refs_1_ = bf16[2,216,128]{2,1,0:T(8,128)(2,1)S(1)} collective-permute-done((bf16[2,216,128]{2,1,0:T(8,128)(2,1)S(1)}, bf16[2,216,128]{2,1,0:T(8,128)(2,1)S(1)}, u32[]{:S(2)}, u32[]{:S(2)}) %collective-permute-start.15) | collective-permute-done | bytes 110624 | tf_op jit(solution)/shard_map/ppermute | solution.py:333
  41.7 3.3 %collective-permute-done.14.refs_1_ = bf16[4,216,128]{2,1,0:T(8,128)(2,1)S(1)} collective-permute-done((bf16[4,216,128]{2,1,0:T(8,128)(2,1)S(1)}, bf16[4,216,128]{2,1,0:T(8,128)(2,1)S(1)}, u32[]{:S(2)}, u32[]{:S(2)}) %collective-permute-start.14) | collective-permute-done | bytes 221216 | tf_op jit(solution)/shard_map/ppermute | solution.py:333
  45.6 1.9 %collective-permute-start.22 = (bf16[1,216,128]{2,1,0:T(8,128)(2,1)S(1)}, bf16[1,216,128]{2,1,0:T(8,128)(2,1)S(1)}, u32[]{:S(2)}, u32[]{:S(2)}) collective-permute-start(bf16[1,216,128]{2,1,0:T(8,128)(2,1)S(1)} %get-tuple-element.68), channel_id=1, source_target_pairs={{0,8},{1,9},{2,10},{3,11},{4,12},{5,13},{6,14},{7,15},{8,0},{9,1},... | collective-permute-start | bytes 165896 | tf_op jit(solution)/shard_map/ppermute | solution.py:333
  48.2 1.7 %collective-permute-done.21.refs_1_ = bf16[2,216,128]{2,1,0:T(8,128)(2,1)S(1)} collective-permute-done((bf16[2,216,128]{2,1,0:T(8,128)(2,1)S(1)}, bf16[2,216,128]{2,1,0:T(8,128)(2,1)S(1)}, u32[]{:S(2)}, u32[]{:S(2)}) %collective-permute-start.21) | collective-permute-done | bytes 110624 | tf_op jit(solution)/shard_map/ppermute | solution.py:333
  50.0 2.7 %collective-permute-start.23 = (bf16[1,216,128]{2,1,0:T(8,128)(2,1)S(1)}, bf16[1,216,128]{2,1,0:T(8,128)(2,1)S(1)}, u32[]{:S(2)}, u32[]{:S(2)}) collective-permute-start(bf16[1,216,128]{2,1,0:T(8,128)(2,1)S(1)} %get-tuple-element.71), channel_id=1, source_target_pairs={{0,8},{1,9},{2,10},{3,11},{4,12},{5,13},{6,14},{7,15},{8,0},{9,1},... | collective-permute-start | bytes 165896 | tf_op jit(solution)/shard_map/ppermute | solution.py:333
  52.7 2.4 %shard_map.100 = (bf16[2,4,128,128]{3,2,1,0:T(8,128)(2,1)}, f32[1,216,128]{2,1,0:T(8,128)S(1)}, f32[216,128]{1,0:T(8,128)}) custom-call(bf16[2,4,128,128]{3,2,1,0:T(8,128)(2,1)S(1)} %get-tuple-element.52.refs_2_.refs_0_, bf16[1,4,128,128]{3,2,1,0:T(8,128)(2,1)S(1)} %collective-permute-done.19.refs_1_, ...), custom_call_target="tpu_custom_call" | custom-call | flops 5000000000 | bytes 15000000 | tf_op jit(solution)/shard_map/pallas_call | solution.py:303
  55.1 2.7 %collective-permute-done.23.refs_1_ = bf16[1,216,128]{2,1,0:T(8,128)(2,1)S(1)} collective-permute-done((bf16[1,216,128]{2,1,0:T(8,128)(2,1)S(1)}, bf16[1,216,128]{2,1,0:T(8,128)(2,1)S(1)}, u32[]{:S(2)}, u32[]{:S(2)}) %collective-permute-start.23) | collective-permute-done | bytes 55328 | tf_op jit(solution)/shard_map/ppermute | solution.py:333
  57.8 0.7 %shard_map.101 = f32[216,128]{1,0:T(8,128)} custom-call(f32[1,216,128]{2,1,0:T(8,128)S(1)} %get-tuple-element.70.refs_0_, bf16[1,216,128]{2,1,0:T(8,128)(2,1)S(1)} %collective-permute-done.23.refs_1_), custom_call_target="tpu_custom_call" | custom-call | flops 200000000 | bytes 600000 | tf_op jit(solution)/shard_map/pallas_call | solution.py:303
  (53 shorter events, 6.2 us)
Async XLA Ops:
  0.6 8.5 %collective-permute-start.1 = (bf16[216,128]{1,0:T(8,128)(2,1)}, bf16[216,128]{1,0:T(8,128)(2,1)S(1)}, u32[]{:S(2)}, u32[]{:S(2)}) collective-permute-start(bf16[216,128]{1,0:T(8,128)(2,1)} %refs_2_.2), channel_id=1, source_target_pairs={{0,2},{1,3},{2,0},{3,1},{4,6},{5,7},{6,4},{7,5},{8,10},{9,11},{10,... | collective-permute-start | bytes 165896 | tf_op jit(solution)/shard_map/ppermute | solution.py:333
  3.6 5.5 %collective-permute-start = (bf16[216,128]{1,0:T(8,128)(2,1)}, bf16[216,128]{1,0:T(8,128)(2,1)S(1)}, u32[]{:S(2)}, u32[]{:S(2)}) collective-permute-start(bf16[216,128]{1,0:T(8,128)(2,1)} %refs_0_.4), channel_id=1, source_target_pairs={{0,8},{1,9},{2,10},{3,11},{4,12},{5,13},{6,14},{7,15},{8,0},{9,1},... | collective-permute-start | bytes 165896 | tf_op jit(solution)/shard_map/ppermute | solution.py:333
  8.4 4.8 %collective-permute-start.2 = (bf16[1,4,128,128]{3,2,1,0:T(8,128)(2,1)S(1)}, bf16[1,4,128,128]{3,2,1,0:T(8,128)(2,1)S(1)}, u32[]{:S(2)}, u32[]{:S(2)}) collective-permute-start(bf16[1,4,128,128]{3,2,1,0:T(8,128)(2,1)S(1)} %get-tuple-element.41), channel_id=1, source_target_pairs={{0,1},{1,0},{2,3},{3,2},{4,5},{5,4},{6,7},{7,6},{8,9},{9,8},{10,11... | collective-permute-start | bytes 393224 | tf_op jit(solution)/shard_map/ppermute | solution.py:333
  8.5 4.7 %collective-permute-start.3 = (bf16[1,4,128,128]{3,2,1,0:T(8,128)(2,1)S(1)}, bf16[1,4,128,128]{3,2,1,0:T(8,128)(2,1)S(1)}, u32[]{:S(2)}, u32[]{:S(2)}) collective-permute-start(bf16[1,4,128,128]{3,2,1,0:T(8,128)(2,1)S(1)} %get-tuple-element.42), channel_id=1, source_target_pairs={{1,2},{3,4},{5,6},{7,8},{9,10},{11,12},{13,14},{2,1},{4,3},{6,5},{... | collective-permute-start | bytes 393224 | tf_op jit(solution)/shard_map/ppermute | solution.py:337
  9.2 8.3 %collective-permute-start.4 = (bf16[2,216,128]{2,1,0:T(8,128)(2,1)S(1)}, bf16[2,216,128]{2,1,0:T(8,128)(2,1)S(1)}, u32[]{:S(2)}, u32[]{:S(2)}) collective-permute-start(bf16[2,216,128]{2,1,0:T(8,128)(2,1)S(1)} %get-tuple-element.39.refs_2_.refs_0_), channel_id=1, source_target_pairs={{0,4},{1,5},{2,6},{3,7},{4,0},{5,1},{6,2},{7,3},{8,12},{9,13},{10,... | collective-permute-start | bytes 331784 | tf_op jit(solution)/shard_map/ppermute | solution.py:333
  17.6 7.0 %collective-permute-start.7 = (bf16[4,216,128]{2,1,0:T(8,128)(2,1)S(1)}, bf16[4,216,128]{2,1,0:T(8,128)(2,1)S(1)}, u32[]{:S(2)}, u32[]{:S(2)}) collective-permute-start(bf16[4,216,128]{2,1,0:T(8,128)(2,1)S(1)} %get-tuple-element.47.refs_2_.refs_4_), channel_id=1, source_target_pairs={{0,2},{1,3},{2,0},{3,1},{4,6},{5,7},{6,4},{7,5},{8,10},{9,11},{10,... | collective-permute-start | bytes 663560 | tf_op jit(solution)/shard_map/ppermute | solution.py:333
  18.6 8.2 %collective-permute-start.10 = (bf16[2,216,128]{2,1,0:T(8,128)(2,1)S(1)}, bf16[2,216,128]{2,1,0:T(8,128)(2,1)S(1)}, u32[]{:S(2)}, u32[]{:S(2)}) collective-permute-start(bf16[2,216,128]{2,1,0:T(8,128)(2,1)S(1)} %get-tuple-element.48.refs_0_), channel_id=1, source_target_pairs={{0,8},{1,9},{2,10},{3,11},{4,12},{5,13},{6,14},{7,15},{8,0},{9,1},... | collective-permute-start | bytes 331784 | tf_op jit(solution)/shard_map/ppermute | solution.py:333
  19.0 12.0 %collective-permute-start.8 = (bf16[4,216,128]{2,1,0:T(8,128)(2,1)S(1)}, bf16[4,216,128]{2,1,0:T(8,128)(2,1)S(1)}, u32[]{:S(2)}, u32[]{:S(2)}) collective-permute-start(bf16[4,216,128]{2,1,0:T(8,128)(2,1)S(1)} %get-tuple-element.47.refs_2_.refs_4_), channel_id=1, source_target_pairs={{0,1},{1,0},{2,3},{3,2},{4,5},{5,4},{6,7},{7,6},{8,9},{9,8},{10,11... | collective-permute-start | bytes 663560 | tf_op jit(solution)/shard_map/ppermute | solution.py:333
  19.0 2.7 %collective-permute-start.5 = (bf16[1,4,128,128]{3,2,1,0:T(8,128)(2,1)S(1)}, bf16[1,4,128,128]{3,2,1,0:T(8,128)(2,1)S(1)}, u32[]{:S(2)}, u32[]{:S(2)}) collective-permute-start(bf16[1,4,128,128]{3,2,1,0:T(8,128)(2,1)S(1)} %get-tuple-element.45), channel_id=1, source_target_pairs={{0,1},{1,0},{2,3},{3,2},{4,5},{5,4},{6,7},{7,6},{8,9},{9,8},{10,11... | collective-permute-start | bytes 393224 | tf_op jit(solution)/shard_map/ppermute | solution.py:333
  19.5 5.2 %collective-permute-start.6 = (bf16[1,4,128,128]{3,2,1,0:T(8,128)(2,1)S(1)}, bf16[1,4,128,128]{3,2,1,0:T(8,128)(2,1)S(1)}, u32[]{:S(2)}, u32[]{:S(2)}) collective-permute-start(bf16[1,4,128,128]{3,2,1,0:T(8,128)(2,1)S(1)} %get-tuple-element.46), channel_id=1, source_target_pairs={{1,2},{3,4},{5,6},{7,8},{9,10},{11,12},{13,14},{2,1},{4,3},{6,5},{... | collective-permute-start | bytes 393224 | tf_op jit(solution)/shard_map/ppermute | solution.py:337
  21.6 4.4 %collective-permute-start.11 = (bf16[8,216,128]{2,1,0:T(8,128)(2,1)S(1)}, bf16[8,216,128]{2,1,0:T(8,128)(2,1)S(1)}, u32[]{:S(2)}, u32[]{:S(2)}) collective-permute-start(bf16[8,216,128]{2,1,0:T(8,128)(2,1)S(1)} %get-tuple-element.50), channel_id=1, source_target_pairs={{0,1},{1,0},{2,3},{3,2},{4,5},{5,4},{6,7},{7,6},{8,9},{9,8},{10,11... | collective-permute-start | bytes 1327112 | tf_op jit(solution)/shard_map/ppermute | solution.py:333
  24.6 6.4 %collective-permute-start.9 = (bf16[4,216,128]{2,1,0:T(8,128)(2,1)S(1)}, bf16[4,216,128]{2,1,0:T(8,128)(2,1)S(1)}, u32[]{:S(2)}, u32[]{:S(2)}) collective-permute-start(bf16[4,216,128]{2,1,0:T(8,128)(2,1)S(1)} %collective-permute-done.7.refs_2_.refs_5_), channel_id=1, source_target_pairs={{0,1},{1,0},{2,3},{3,2},{4,5},{5,4},{6,7},{7,6},{8,9},{9,8},{10,11... | collective-permute-start | bytes 663560 | tf_op jit(solution)/shard_map/ppermute | solution.py:333
  26.8 12.4 %collective-permute-start.17 = (bf16[4,216,128]{2,1,0:T(8,128)(2,1)S(1)}, bf16[4,216,128]{2,1,0:T(8,128)(2,1)S(1)}, u32[]{:S(2)}, u32[]{:S(2)}) collective-permute-start(bf16[4,216,128]{2,1,0:T(8,128)(2,1)S(1)} %shard_map.93.refs_8_.refs_3_), channel_id=1, source_target_pairs={{0,1},{1,0},{2,3},{3,2},{4,5},{5,4},{6,7},{7,6},{8,9},{9,8},{10,11... | collective-permute-start | bytes 663560 | tf_op jit(solution)/shard_map/ppermute | solution.py:333
  26.9 8.0 %collective-permute-start.16 = (bf16[4,216,128]{2,1,0:T(8,128)(2,1)S(1)}, bf16[4,216,128]{2,1,0:T(8,128)(2,1)S(1)}, u32[]{:S(2)}, u32[]{:S(2)}) collective-permute-start(bf16[4,216,128]{2,1,0:T(8,128)(2,1)S(1)} %shard_map.93.refs_8_.refs_3_), channel_id=1, source_target_pairs={{0,4},{1,5},{2,6},{3,7},{4,0},{5,1},{6,2},{7,3},{8,12},{9,13},{10,... | collective-permute-start | bytes 663560 | tf_op jit(solution)/shard_map/ppermute | solution.py:333
  29.2 7.5 %collective-permute-start.13 = (bf16[4,216,128]{2,1,0:T(8,128)(2,1)S(1)}, bf16[4,216,128]{2,1,0:T(8,128)(2,1)S(1)}, u32[]{:S(2)}, u32[]{:S(2)}) collective-permute-start(bf16[4,216,128]{2,1,0:T(8,128)(2,1)S(1)} %get-tuple-element.55), channel_id=1, source_target_pairs={{0,2},{1,3},{2,0},{3,1},{4,6},{5,7},{6,4},{7,5},{8,10},{9,11},{10,... | collective-permute-start | bytes 663560 | tf_op jit(solution)/shard_map/ppermute | solution.py:333
  34.3 2.9 %collective-permute-start.12 = (bf16[8,216,128]{2,1,0:T(8,128)(2,1)S(1)}, bf16[8,216,128]{2,1,0:T(8,128)(2,1)S(1)}, u32[]{:S(2)}, u32[]{:S(2)}) collective-permute-start(bf16[8,216,128]{2,1,0:T(8,128)(2,1)S(1)} %get-tuple-element.54), channel_id=1, source_target_pairs={{0,1},{1,0},{2,3},{3,2},{4,5},{5,4},{6,7},{7,6},{8,9},{9,8},{10,11... | collective-permute-start | bytes 1327112 | tf_op jit(solution)/shard_map/ppermute | solution.py:333
  34.9 6.7 %collective-permute-start.18 = (bf16[4,216,128]{2,1,0:T(8,128)(2,1)S(1)}, bf16[4,216,128]{2,1,0:T(8,128)(2,1)S(1)}, u32[]{:S(2)}, u32[]{:S(2)}) collective-permute-start(bf16[4,216,128]{2,1,0:T(8,128)(2,1)S(1)} %collective-permute-done.16.refs_4_), channel_id=1, source_target_pairs={{0,1},{1,0},{2,3},{3,2},{4,5},{5,4},{6,7},{7,6},{8,9},{9,8},{10,11... | collective-permute-start | bytes 663560 | tf_op jit(solution)/shard_map/ppermute | solution.py:333
  36.8 4.8 %collective-permute-start.15 = (bf16[2,216,128]{2,1,0:T(8,128)(2,1)S(1)}, bf16[2,216,128]{2,1,0:T(8,128)(2,1)S(1)}, u32[]{:S(2)}, u32[]{:S(2)}) collective-permute-start(bf16[2,216,128]{2,1,0:T(8,128)(2,1)S(1)} %get-tuple-element.61), channel_id=1, source_target_pairs={{0,4},{1,5},{2,6},{3,7},{4,0},{5,1},{6,2},{7,3},{8,12},{9,13},{10,... | collective-permute-start | bytes 331784 | tf_op jit(solution)/shard_map/ppermute | solution.py:333
  37.4 7.5 %collective-permute-start.14 = (bf16[4,216,128]{2,1,0:T(8,128)(2,1)S(1)}, bf16[4,216,128]{2,1,0:T(8,128)(2,1)S(1)}, u32[]{:S(2)}, u32[]{:S(2)}) collective-permute-start(bf16[4,216,128]{2,1,0:T(8,128)(2,1)S(1)} %get-tuple-element.58), channel_id=1, source_target_pairs={{0,2},{1,3},{2,0},{3,1},{4,6},{5,7},{6,4},{7,5},{8,10},{9,11},{10,... | collective-permute-start | bytes 663560 | tf_op jit(solution)/shard_map/ppermute | solution.py:333
  45.0 4.9 %collective-permute-start.21 = (bf16[2,216,128]{2,1,0:T(8,128)(2,1)S(1)}, bf16[2,216,128]{2,1,0:T(8,128)(2,1)S(1)}, u32[]{:S(2)}, u32[]{:S(2)}) collective-permute-start(bf16[2,216,128]{2,1,0:T(8,128)(2,1)S(1)} %get-tuple-element.66), channel_id=1, source_target_pairs={{0,4},{1,5},{2,6},{3,7},{4,0},{5,1},{6,2},{7,3},{8,12},{9,13},{10,... | collective-permute-start | bytes 331784 | tf_op jit(solution)/shard_map/ppermute | solution.py:333
  45.6 7.0 %collective-permute-start.22 = (bf16[1,216,128]{2,1,0:T(8,128)(2,1)S(1)}, bf16[1,216,128]{2,1,0:T(8,128)(2,1)S(1)}, u32[]{:S(2)}, u32[]{:S(2)}) collective-permute-start(bf16[1,216,128]{2,1,0:T(8,128)(2,1)S(1)} %get-tuple-element.68), channel_id=1, source_target_pairs={{0,8},{1,9},{2,10},{3,11},{4,12},{5,13},{6,14},{7,15},{8,0},{9,1},... | collective-permute-start | bytes 165896 | tf_op jit(solution)/shard_map/ppermute | solution.py:333
  47.6 5.1 %collective-permute-start.19 = (bf16[1,4,128,128]{3,2,1,0:T(8,128)(2,1)S(1)}, bf16[1,4,128,128]{3,2,1,0:T(8,128)(2,1)S(1)}, u32[]{:S(2)}, u32[]{:S(2)}) collective-permute-start(bf16[1,4,128,128]{3,2,1,0:T(8,128)(2,1)S(1)} %get-tuple-element.63), channel_id=1, source_target_pairs={{0,1},{1,0},{2,3},{3,2},{4,5},{5,4},{6,7},{7,6},{8,9},{9,8},{10,11... | collective-permute-start | bytes 393224 | tf_op jit(solution)/shard_map/ppermute | solution.py:333
  47.6 5.1 %collective-permute-start.20 = (bf16[1,4,128,128]{3,2,1,0:T(8,128)(2,1)S(1)}, bf16[1,4,128,128]{3,2,1,0:T(8,128)(2,1)S(1)}, u32[]{:S(2)}, u32[]{:S(2)}) collective-permute-start(bf16[1,4,128,128]{3,2,1,0:T(8,128)(2,1)S(1)} %get-tuple-element.64), channel_id=1, source_target_pairs={{1,2},{3,4},{5,6},{7,8},{9,10},{11,12},{13,14},{2,1},{4,3},{6,5},{... | collective-permute-start | bytes 393224 | tf_op jit(solution)/shard_map/ppermute | solution.py:337
  50.0 7.9 %collective-permute-start.23 = (bf16[1,216,128]{2,1,0:T(8,128)(2,1)S(1)}, bf16[1,216,128]{2,1,0:T(8,128)(2,1)S(1)}, u32[]{:S(2)}, u32[]{:S(2)}) collective-permute-start(bf16[1,216,128]{2,1,0:T(8,128)(2,1)S(1)} %get-tuple-element.71), channel_id=1, source_target_pairs={{0,8},{1,9},{2,10},{3,11},{4,12},{5,13},{6,14},{7,15},{8,0},{9,1},... | collective-permute-start | bytes 165896 | tf_op jit(solution)/shard_map/ppermute | solution.py:333
  (6 other events, 10.9 us)

commit v5 on v4

--- a/solution.py
+++ b/solution.py
@@ -45,15 +45,6 @@
     for x in range(layers):
         ref[x, 0] = blank
         ref[x, wide - 1] = blank
-
-
-def first_grads(spot, grad_out, pre_second, own, near, far):
-    nx = own.shape[0]
-    for x in range(nx):
-        for y in range(own.shape[1]):
-            slope = slope_of(pre_second[x, y].astype(f32))
-            own[x, y] = (grad_out[x, y].astype(f32) * slope).astype(bf16)
-    send_edges(spot, own, near, far)
 
 
 def near_edge(spot, last):
@@ -240,9 +231,9 @@
     if masks:
         lists, rest = rest[:4], rest[4:]
         (padded, pairs), rest = rest[-2:], rest[:-2]
-        kept, kept_two, got_two, out, kept_on, sum_two = rest
-        kept_on[...] = kept[...]
-        last_sum(kept_two, got_two, sum_two)
+        kept_one, kept_two, out, one_on, two_on = rest
+        one_on[...] = kept_one[...]
+        two_on[...] = kept_two[...]
         mine, theirs = both_columns(lists)
         weights = placed_weights(spot, masks, mine, theirs, pairs)
     else:
@@ -284,8 +275,9 @@
     far_on[...] = far[...]
 
 
-def last_sum(kept, got, out):
-    out[...] = kept[0] + got[0].astype(f32)
+def last_sums(kept_a, got_a, kept_b, got_b, out_a, out_b):
+    out_a[...] = kept_a[0] + got_a[0].astype(f32)
+    out_b[...] = kept_b[0] + got_b[0].astype(f32)
 
 
 def call(body, n_smem, args, outs, scratch=(), after=(), us=0.2):
@@ -347,12 +339,11 @@
     terms = [blocks(n // 2, f32), blocks(n // 2)] if fast else [total]
     work = [total, ((n // 2, 2 * rows, ch), bf16)] if fast else []
 
-    grad_two, near, far = call(
-        first_grads, 1, (spot, grad_out, pre_second), [(shape, bf16), (layer, bf16), (layer, bf16)], us=20
-    )
+    grad_two = (grad_out.astype(f32) * slope_of(pre_second.astype(f32))).astype(bf16)
+    near, far = call(send_edges, 1, (spot, grad_two), [(layer, bf16), (layer, bf16)], us=20)
+    after = (near,)
     far = swap_far(far)
     near = swap(near, 1)
-    after = (grad_two,)
     if fast:
         pair, pair_first = stacked(
             [(filter_second, swap(filter_second, 8)), (filter_first, swap(filter_first, 2))], (2, 2), after
@@ -421,7 +412,7 @@
     )
 
     def finish(near, far, full, sums=()):
-        sizes = [blocks(1, f32), (block, f32)] if sums else []
+        sizes = [blocks(1, f32)] * len(sums)
         return call(
             functools.partial(input_grads, masks=masks_one),
             1,
@@ -447,7 +438,7 @@
         kept_one, sent_one = step(*terms_one, 3, 1, 4, (kept_two,))
         mine = (column_first, swap(column_first, 4))
         full_first = (*mine, *(swap(m, 1) for m in mine))
-        kept_two, sent_two = step(kept_two, sent_two, 5, 4, 1, (kept_one, *full_first), 20)
+        kept_two, sent_two = step(kept_two, sent_two, 5, 4, 1, (kept_one, *full_first), 0.2)
         got_two = swap(sent_two, 8)
         kept_one, sent_one, near_one, far_one = call(
             functools.partial(halve_and_pass, bit=4),
@@ -458,10 +449,10 @@
             us=20,
         )
         kept_one, sent_one = step(kept_one, sent_one, 5, 4, 1, (), 1.5)
-        grad_in, kept_one, owned_two = finish(
-            near_one, far_one, full_first, (kept_one, kept_two, got_two)
-        )
-        (owned_one,) = call(last_sum, 0, (kept_one, swap(sent_one, 8)), [(block, f32)])
+        grad_in, kept_one, kept_two = finish(near_one, far_one, full_first, (kept_one, kept_two))
+        owned_two, owned_one = call(
+            last_sums, 0, (kept_two, got_two, kept_one, swap(sent_one, 8)), [(block, f32)] * 2
+        )
     else:
         (grad_in,) = finish(near_one, far_one, (lax.all_gather(filter_first, "gx", axis=0, tiled=True),))
         owned_two, owned_one = (

time: 58.7 us -> 57 us (0.971)
  waiting for transfers between devices: 18.6 us -> 16.5 us
  local copies, waits for them, and re-layouts: 1.92 us -> 0.03 us
  other arithmetic: 0 us -> 1.29 us
  starting transfers between devices: 27.8 us -> 28.9 us
    ppermute x21, waiting for transfers between devices: 18.6 us -> 16.5 us  [swap(): return lax.ppermute(array, 'gx', [(i, i ^ mask) for i in range(n)])]
    unnamed x12 -> x8, local copies, waits for them, and re-layouts: 1.92 us -> 0.03 us
    convert_element_type x0 -> x1, other arithmetic: none -> 1.29 us  [on_device(): (grad_out.astype(f32) * slope_of(pre_second.astype(f32))).astype(bf16)]
    ppermute x21, starting transfers between devices: 25.8 us -> 26.9 us  [swap(): return lax.ppermute(array, 'gx', [(i, i ^ mask) for i in range(n)])]
  transfers between devices with their start and end apart: 24 -> 24, of which waited for: 9 -> 9; matrix products, arithmetic and copies ran while one was open for 0% -> 2% of each run, Pallas kernels for 15% -> 15%
where the time goes in v5:
time: 57 us; the launch traced here: 56.7 us
  starting transfers between devices  28.9 us (51%)
  waiting for transfers between devices  16.5 us (29%)
  Pallas kernels  9.18 us (16%)
  other arithmetic  1.29 us (2%)
  between operations  0.82 us (1%)
    ppermute x21, starting transfers between devices, swap(): return lax.ppermute(array, 'gx', [(i, i ^ mask) for i in range(n)])  26.9 us
    ppermute x21, waiting for transfers between devices, swap(): return lax.ppermute(array, 'gx', [(i, i ^ mask) for i in range(n)])  16.5 us
    pallas_call x17, Pallas kernels, call(): pl.pallas_call(run, in_specs=[vmem] * first + [anywhere] * many, out_spec...  9.18 us
    ppermute x3, starting transfers between devices, swap_far(): return lax.ppermute(array, 'gx', ahead + [(b, a) for a, b in ahead])  1.98 us
    convert_element_type x1, other arithmetic, on_device(): (grad_out.astype(f32) * slope_of(pre_second.astype(f32))).astype(bf16)  1.29 us
  transfers between devices with their start and end apart: 24, of which 9 were waited for; matrix products, arithmetic and copies ran while one was open for 2% of the time, Pallas kernels for 15%

profile of v5, /device:TPU:0, one launch (start us, length us, event | category | flops | bytes accessed | tf_op | source)
XLA Modules:
  0.0 56.7 jit_solution(2055908967567597768)
XLA Ops:
  0.6 3.0 %collective-permute-start.1 = (bf16[216,128]{1,0:T(8,128)(2,1)}, bf16[216,128]{1,0:T(8,128)(2,1)S(1)}, u32[]{:S(2)}, u32[]{:S(2)}) collective-permute-start(bf16[216,128]{1,0:T(8,128)(2,1)} %refs_2_.2), channel_id=1, source_target_pairs={{0,2},{1,3},{2,0},{3,1},{4,6},{5,7},{6,4},{7,5},{8,10},{9,11},{10,... | collective-permute-start | bytes 165896 | tf_op jit(solution)/shard_map/ppermute | solution.py:325
  3.6 2.6 %collective-permute-start = (bf16[216,128]{1,0:T(8,128)(2,1)}, bf16[216,128]{1,0:T(8,128)(2,1)S(1)}, u32[]{:S(2)}, u32[]{:S(2)}) collective-permute-start(bf16[216,128]{1,0:T(8,128)(2,1)} %refs_0_.2), channel_id=1, source_target_pairs={{0,8},{1,9},{2,10},{3,11},{4,12},{5,13},{6,14},{7,15},{8,0},{9,1},... | collective-permute-start | bytes 165896 | tf_op jit(solution)/shard_map/ppermute | solution.py:325
  6.2 1.3 %fusion.7.refs_0_ = bf16[2,4,128,128]{3,2,1,0:T(8,128)(2,1)S(1)} fusion(bf16[2,4,128,128]{3,2,1,0:T(8,128)(2,1)} %param.9, bf16[2,4,128,128]{3,2,1,0:T(8,128)(2,1)} %param.6), kind=kLoop, calls=%fused_computation.11 | loop fusion | flops 1572864 | bytes 786432 | tf_op jit(solution)/shard_map/convert_element_type | solution.py:342
  8.3 2.0 %collective-permute-start.2 = (bf16[1,4,128,128]{3,2,1,0:T(8,128)(2,1)S(1)}, bf16[1,4,128,128]{3,2,1,0:T(8,128)(2,1)S(1)}, u32[]{:S(2)}, u32[]{:S(2)}) collective-permute-start(bf16[1,4,128,128]{3,2,1,0:T(8,128)(2,1)S(1)} %get-tuple-element.39.refs_4_), channel_id=1, source_target_pairs={{0,1},{1,0},{2,3},{3,2},{4,5},{5,4},{6,7},{7,6},{8,9},{9,8},{10,11... | collective-permute-start | bytes 393224 | tf_op jit(solution)/shard_map/ppermute | solution.py:325
  10.3 1.6 %collective-permute-start.4 = (bf16[2,216,128]{2,1,0:T(8,128)(2,1)S(1)}, bf16[2,216,128]{2,1,0:T(8,128)(2,1)S(1)}, u32[]{:S(2)}, u32[]{:S(2)}) collective-permute-start(bf16[2,216,128]{2,1,0:T(8,128)(2,1)S(1)} %get-tuple-element.40.refs_2_.refs_0_), channel_id=1, source_target_pairs={{0,4},{1,5},{2,6},{3,7},{4,0},{5,1},{6,2},{7,3},{8,12},{9,13},{10,... | collective-permute-start | bytes 331784 | tf_op jit(solution)/shard_map/ppermute | solution.py:325
  12.5 3.8 %collective-permute-done.4.refs_1_ = bf16[2,216,128]{2,1,0:T(8,128)(2,1)S(1)} collective-permute-done((bf16[2,216,128]{2,1,0:T(8,128)(2,1)S(1)}, bf16[2,216,128]{2,1,0:T(8,128)(2,1)S(1)}, u32[]{:S(2)}, u32[]{:S(2)}) %collective-permute-start.4) | collective-permute-done | bytes 110624 | tf_op jit(solution)/shard_map/ppermute | solution.py:325
  16.4 1.5 %collective-permute-start.7 = (bf16[4,216,128]{2,1,0:T(8,128)(2,1)S(1)}, bf16[4,216,128]{2,1,0:T(8,128)(2,1)S(1)}, u32[]{:S(2)}, u32[]{:S(2)}) collective-permute-start(bf16[4,216,128]{2,1,0:T(8,128)(2,1)S(1)} %get-tuple-element.47.refs_2_.refs_4_), channel_id=1, source_target_pairs={{0,2},{1,3},{2,0},{3,1},{4,6},{5,7},{6,4},{7,5},{8,10},{9,11},{10,... | collective-permute-start | bytes 663560 | tf_op jit(solution)/shard_map/ppermute | solution.py:325
  19.5 1.5 %shard_map.91 = (f32[8,216,128]{2,1,0:T(8,128)S(1)}, bf16[8,216,128]{2,1,0:T(8,128)(2,1)S(1)}) custom-call(bf16[4,6,128,128]{3,2,1,0:T(8,128)(2,1)S(1)} %shard_map.88.refs_3_.refs_0_.refs_1_, bf16[384,1024]{1,0:T(8,128)(2,1)S(1)} %get-tuple-element.43.refs_3_.refs_1_, bf16[4,216,128]{2,1,0:T(8,128)(2,1)S(1)} %get-tuple-element.47.refs_2_.refs_4_), custom_call_target="tpu_custom_call" | custom-call | flops 2000000000 | bytes 6000000 | tf_op jit(solution)/shard_map/pallas_call | solution.py:295
  21.0 2.3 %collective-permute-start.11 = (bf16[8,216,128]{2,1,0:T(8,128)(2,1)S(1)}, bf16[8,216,128]{2,1,0:T(8,128)(2,1)S(1)}, u32[]{:S(2)}, u32[]{:S(2)}) collective-permute-start(bf16[8,216,128]{2,1,0:T(8,128)(2,1)S(1)} %get-tuple-element.50), channel_id=1, source_target_pairs={{0,1},{1,0},{2,3},{3,2},{4,5},{5,4},{6,7},{7,6},{8,9},{9,8},{10,11... | collective-permute-start | bytes 1327112 | tf_op jit(solution)/shard_map/ppermute | solution.py:325
  23.5 1.2 %collective-permute-done.11.refs_1_ = bf16[8,216,128]{2,1,0:T(8,128)(2,1)S(1)} collective-permute-done((bf16[8,216,128]{2,1,0:T(8,128)(2,1)S(1)}, bf16[8,216,128]{2,1,0:T(8,128)(2,1)S(1)}, u32[]{:S(2)}, u32[]{:S(2)}) %collective-permute-start.11) | collective-permute-done | bytes 442400 | tf_op jit(solution)/shard_map/ppermute | solution.py:325
  25.7 2.5 %collective-permute-start.16 = (bf16[4,216,128]{2,1,0:T(8,128)(2,1)S(1)}, bf16[4,216,128]{2,1,0:T(8,128)(2,1)S(1)}, u32[]{:S(2)}, u32[]{:S(2)}) collective-permute-start(bf16[4,216,128]{2,1,0:T(8,128)(2,1)S(1)} %shard_map.93.refs_8_.refs_3_), channel_id=1, source_target_pairs={{0,4},{1,5},{2,6},{3,7},{4,0},{5,1},{6,2},{7,3},{8,12},{9,13},{10,... | collective-permute-start | bytes 663560 | tf_op jit(solution)/shard_map/ppermute | solution.py:325
  28.3 1.5 %collective-permute-start.13 = (bf16[4,216,128]{2,1,0:T(8,128)(2,1)S(1)}, bf16[4,216,128]{2,1,0:T(8,128)(2,1)S(1)}, u32[]{:S(2)}, u32[]{:S(2)}) collective-permute-start(bf16[4,216,128]{2,1,0:T(8,128)(2,1)S(1)} %get-tuple-element.55), channel_id=1, source_target_pairs={{0,2},{1,3},{2,0},{3,1},{4,6},{5,7},{6,4},{7,5},{8,10},{9,11},{10,... | collective-permute-start | bytes 663560 | tf_op jit(solution)/shard_map/ppermute | solution.py:325
  29.8 3.3 %shard_map.94 = (f32[8,216,128]{2,1,0:T(8,128)S(1)}, bf16[8,216,128]{2,1,0:T(8,128)(2,1)S(1)}, bf16[2,4,128,128]{3,2,1,0:T(8,128)(2,1)S(1)}, bf16[1,4,128,128]{3...) custom-call(f32[2,4,128,128]{3,2,1,0:T(8,128)S(1)} %get-tuple-element.41.refs_0_, ...), custom_call_target="tpu_custom_call" | custom-call | flops 8000000000 | bytes 24000000 | tf_op jit(solution)/shard_map/pallas_call | solution.py:295
  33.2 0.8 %collective-permute-done.16.refs_4_ = bf16[4,216,128]{2,1,0:T(8,128)(2,1)S(1)} collective-permute-done((bf16[4,216,128]{2,1,0:T(8,128)(2,1)S(1)}, bf16[4,216,128]{2,1,0:T(8,128)(2,1)S(1)}, u32[]{:S(2)}, u32[]{:S(2)}) %collective-permute-start.16) | collective-permute-done | bytes 221216 | tf_op jit(solution)/shard_map/ppermute | solution.py:325
  34.0 1.6 %collective-permute-done.13.refs_1_ = bf16[4,216,128]{2,1,0:T(8,128)(2,1)S(1)} collective-permute-done((bf16[4,216,128]{2,1,0:T(8,128)(2,1)S(1)}, bf16[4,216,128]{2,1,0:T(8,128)(2,1)S(1)}, u32[]{:S(2)}, u32[]{:S(2)}) %collective-permute-start.13) | collective-permute-done | bytes 221216 | tf_op jit(solution)/shard_map/ppermute | solution.py:325
  35.7 1.8 %collective-permute-start.14 = (bf16[4,216,128]{2,1,0:T(8,128)(2,1)S(1)}, bf16[4,216,128]{2,1,0:T(8,128)(2,1)S(1)}, u32[]{:S(2)}, u32[]{:S(2)}) collective-permute-start(bf16[4,216,128]{2,1,0:T(8,128)(2,1)S(1)} %get-tuple-element.58), channel_id=1, source_target_pairs={{0,2},{1,3},{2,0},{3,1},{4,6},{5,7},{6,4},{7,5},{8,10},{9,11},{10,... | collective-permute-start | bytes 663560 | tf_op jit(solution)/shard_map/ppermute | solution.py:325
  37.8 4.5 %collective-permute-done.15.refs_1_ = bf16[2,216,128]{2,1,0:T(8,128)(2,1)S(1)} collective-permute-done((bf16[2,216,128]{2,1,0:T(8,128)(2,1)S(1)}, bf16[2,216,128]{2,1,0:T(8,128)(2,1)S(1)}, u32[]{:S(2)}, u32[]{:S(2)}) %collective-permute-start.15) | collective-permute-done | bytes 110624 | tf_op jit(solution)/shard_map/ppermute | solution.py:325
  42.7 1.4 %collective-permute-start.21 = (bf16[2,216,128]{2,1,0:T(8,128)(2,1)S(1)}, bf16[2,216,128]{2,1,0:T(8,128)(2,1)S(1)}, u32[]{:S(2)}, u32[]{:S(2)}) collective-permute-start(bf16[2,216,128]{2,1,0:T(8,128)(2,1)S(1)} %get-tuple-element.66), channel_id=1, source_target_pairs={{0,4},{1,5},{2,6},{3,7},{4,0},{5,1},{6,2},{7,3},{8,12},{9,13},{10,... | collective-permute-start | bytes 331784 | tf_op jit(solution)/shard_map/ppermute | solution.py:325
  44.0 2.0 %collective-permute-start.22 = (bf16[1,216,128]{2,1,0:T(8,128)(2,1)S(1)}, bf16[1,216,128]{2,1,0:T(8,128)(2,1)S(1)}, u32[]{:S(2)}, u32[]{:S(2)}) collective-permute-start(bf16[1,216,128]{2,1,0:T(8,128)(2,1)S(1)} %get-tuple-element.70), channel_id=1, source_target_pairs={{0,8},{1,9},{2,10},{3,11},{4,12},{5,13},{6,14},{7,15},{8,0},{9,1},... | collective-permute-start | bytes 165896 | tf_op jit(solution)/shard_map/ppermute | solution.py:325
  46.7 1.2 %collective-permute-done.21.refs_1_ = bf16[2,216,128]{2,1,0:T(8,128)(2,1)S(1)} collective-permute-done((bf16[2,216,128]{2,1,0:T(8,128)(2,1)S(1)}, bf16[2,216,128]{2,1,0:T(8,128)(2,1)S(1)}, u32[]{:S(2)}, u32[]{:S(2)}) %collective-permute-start.21) | collective-permute-done | bytes 110624 | tf_op jit(solution)/shard_map/ppermute | solution.py:325
  47.9 3.2 %collective-permute-start.23 = (bf16[1,216,128]{2,1,0:T(8,128)(2,1)S(1)}, bf16[1,216,128]{2,1,0:T(8,128)(2,1)S(1)}, u32[]{:S(2)}, u32[]{:S(2)}) collective-permute-start(bf16[1,216,128]{2,1,0:T(8,128)(2,1)S(1)} %get-tuple-element.72), channel_id=1, source_target_pairs={{0,8},{1,9},{2,10},{3,11},{4,12},{5,13},{6,14},{7,15},{8,0},{9,1},... | collective-permute-start | bytes 165896 | tf_op jit(solution)/shard_map/ppermute | solution.py:325
  51.1 2.4 %shard_map.100 = (bf16[2,4,128,128]{3,2,1,0:T(8,128)(2,1)}, f32[1,216,128]{2,1,0:T(8,128)S(1)}, f32[1,216,128]{2,1,0:T(8,128)S(1)}) custom-call(bf16[2,4,128,128]{3,2,1,0:T(8,128)(2,1)S(1)} %get-tuple-element.52.refs_2_.refs_0_, bf16[1,4,128,128]{3,2,1,0:T(8,128)(2,1)S(1)} %collective-permute-done.19.refs_1_, ...), custom_call_target="tpu_custom_call" | custom-call | flops 5000000000 | bytes 15000000 | tf_op jit(solution)/shard_map/pallas_call | solution.py:295
  53.6 2.5 %collective-permute-done.23.refs_3_ = bf16[1,216,128]{2,1,0:T(8,128)(2,1)S(1)} collective-permute-done((bf16[1,216,128]{2,1,0:T(8,128)(2,1)S(1)}, bf16[1,216,128]{2,1,0:T(8,128)(2,1)S(1)}, u32[]{:S(2)}, u32[]{:S(2)}) %collective-permute-start.23) | collective-permute-done | bytes 55328 | tf_op jit(solution)/shard_map/ppermute | solution.py:325
  56.0 0.7 %shard_map.101 = (f32[216,128]{1,0:T(8,128)}, f32[216,128]{1,0:T(8,128)}) custom-call(f32[1,216,128]{2,1,0:T(8,128)S(1)} %get-tuple-element.69.refs_0_, bf16[1,216,128]{2,1,0:T(8,128)(2,1)S(1)} %collective-permute-done.22.refs_1_, f32[1,216,128]{2,1,0:T(8,128)S(1)} %get-tuple-element.71.refs_2_, bf16[1,216,128]{2,1,0:T(8,128)(2,1)S(1)} %collective-permute-done.23.refs_3_), custom_call_target="tpu_custom_call" | custom-call | flops 200000000 | bytes 600000 | tf_op jit(solution)/shard_map/pallas_call | solution.py:295
  (50 shorter events, 5.8 us)
Async XLA Ops:
  0.6 9.6 %collective-permute-start.1 = (bf16[216,128]{1,0:T(8,128)(2,1)}, bf16[216,128]{1,0:T(8,128)(2,1)S(1)}, u32[]{:S(2)}, u32[]{:S(2)}) collective-permute-start(bf16[216,128]{1,0:T(8,128)(2,1)} %refs_2_.2), channel_id=1, source_target_pairs={{0,2},{1,3},{2,0},{3,1},{4,6},{5,7},{6,4},{7,5},{8,10},{9,11},{10,... | collective-permute-start | bytes 165896 | tf_op jit(solution)/shard_map/ppermute | solution.py:325
  3.6 6.6 %collective-permute-start = (bf16[216,128]{1,0:T(8,128)(2,1)}, bf16[216,128]{1,0:T(8,128)(2,1)S(1)}, u32[]{:S(2)}, u32[]{:S(2)}) collective-permute-start(bf16[216,128]{1,0:T(8,128)(2,1)} %refs_0_.2), channel_id=1, source_target_pairs={{0,8},{1,9},{2,10},{3,11},{4,12},{5,13},{6,14},{7,15},{8,0},{9,1},... | collective-permute-start | bytes 165896 | tf_op jit(solution)/shard_map/ppermute | solution.py:325
  7.6 4.9 %collective-permute-start.3 = (bf16[1,4,128,128]{3,2,1,0:T(8,128)(2,1)S(1)}, bf16[1,4,128,128]{3,2,1,0:T(8,128)(2,1)S(1)}, u32[]{:S(2)}, u32[]{:S(2)}) collective-permute-start(bf16[1,4,128,128]{3,2,1,0:T(8,128)(2,1)S(1)} %get-tuple-element.42), channel_id=1, source_target_pairs={{1,2},{3,4},{5,6},{7,8},{9,10},{11,12},{13,14},{2,1},{4,3},{6,5},{... | collective-permute-start | bytes 393224 | tf_op jit(solution)/shard_map/ppermute | solution.py:329
  8.3 4.2 %collective-permute-start.2 = (bf16[1,4,128,128]{3,2,1,0:T(8,128)(2,1)S(1)}, bf16[1,4,128,128]{3,2,1,0:T(8,128)(2,1)S(1)}, u32[]{:S(2)}, u32[]{:S(2)}) collective-permute-start(bf16[1,4,128,128]{3,2,1,0:T(8,128)(2,1)S(1)} %get-tuple-element.39.refs_4_), channel_id=1, source_target_pairs={{0,1},{1,0},{2,3},{3,2},{4,5},{5,4},{6,7},{7,6},{8,9},{9,8},{10,11... | collective-permute-start | bytes 393224 | tf_op jit(solution)/shard_map/ppermute | solution.py:325
  10.3 6.1 %collective-permute-start.4 = (bf16[2,216,128]{2,1,0:T(8,128)(2,1)S(1)}, bf16[2,216,128]{2,1,0:T(8,128)(2,1)S(1)}, u32[]{:S(2)}, u32[]{:S(2)}) collective-permute-start(bf16[2,216,128]{2,1,0:T(8,128)(2,1)S(1)} %get-tuple-element.40.refs_2_.refs_0_), channel_id=1, source_target_pairs={{0,4},{1,5},{2,6},{3,7},{4,0},{5,1},{6,2},{7,3},{8,12},{9,13},{10,... | collective-permute-start | bytes 331784 | tf_op jit(solution)/shard_map/ppermute | solution.py:325
  16.4 6.9 %collective-permute-start.7 = (bf16[4,216,128]{2,1,0:T(8,128)(2,1)S(1)}, bf16[4,216,128]{2,1,0:T(8,128)(2,1)S(1)}, u32[]{:S(2)}, u32[]{:S(2)}) collective-permute-start(bf16[4,216,128]{2,1,0:T(8,128)(2,1)S(1)} %get-tuple-element.47.refs_2_.refs_4_), channel_id=1, source_target_pairs={{0,2},{1,3},{2,0},{3,1},{4,6},{5,7},{6,4},{7,5},{8,10},{9,11},{10,... | collective-permute-start | bytes 663560 | tf_op jit(solution)/shard_map/ppermute | solution.py:325
  17.9 7.5 %collective-permute-start.10 = (bf16[2,216,128]{2,1,0:T(8,128)(2,1)S(1)}, bf16[2,216,128]{2,1,0:T(8,128)(2,1)S(1)}, u32[]{:S(2)}, u32[]{:S(2)}) collective-permute-start(bf16[2,216,128]{2,1,0:T(8,128)(2,1)S(1)} %get-tuple-element.48.refs_0_), channel_id=1, source_target_pairs={{0,8},{1,9},{2,10},{3,11},{4,12},{5,13},{6,14},{7,15},{8,0},{9,1},... | collective-permute-start | bytes 331784 | tf_op jit(solution)/shard_map/ppermute | solution.py:325
  18.3 11.5 %collective-permute-start.8 = (bf16[4,216,128]{2,1,0:T(8,128)(2,1)S(1)}, bf16[4,216,128]{2,1,0:T(8,128)(2,1)S(1)}, u32[]{:S(2)}, u32[]{:S(2)}) collective-permute-start(bf16[4,216,128]{2,1,0:T(8,128)(2,1)S(1)} %get-tuple-element.47.refs_2_.refs_4_), channel_id=1, source_target_pairs={{0,1},{1,0},{2,3},{3,2},{4,5},{5,4},{6,7},{7,6},{8,9},{9,8},{10,11... | collective-permute-start | bytes 663560 | tf_op jit(solution)/shard_map/ppermute | solution.py:325
  18.3 2.7 %collective-permute-start.5 = (bf16[1,4,128,128]{3,2,1,0:T(8,128)(2,1)S(1)}, bf16[1,4,128,128]{3,2,1,0:T(8,128)(2,1)S(1)}, u32[]{:S(2)}, u32[]{:S(2)}) collective-permute-start(bf16[1,4,128,128]{3,2,1,0:T(8,128)(2,1)S(1)} %get-tuple-element.45), channel_id=1, source_target_pairs={{0,1},{1,0},{2,3},{3,2},{4,5},{5,4},{6,7},{7,6},{8,9},{9,8},{10,11... | collective-permute-start | bytes 393224 | tf_op jit(solution)/shard_map/ppermute | solution.py:325
  18.8 4.6 %collective-permute-start.6 = (bf16[1,4,128,128]{3,2,1,0:T(8,128)(2,1)S(1)}, bf16[1,4,128,128]{3,2,1,0:T(8,128)(2,1)S(1)}, u32[]{:S(2)}, u32[]{:S(2)}) collective-permute-start(bf16[1,4,128,128]{3,2,1,0:T(8,128)(2,1)S(1)} %get-tuple-element.46), channel_id=1, source_target_pairs={{1,2},{3,4},{5,6},{7,8},{9,10},{11,12},{13,14},{2,1},{4,3},{6,5},{... | collective-permute-start | bytes 393224 | tf_op jit(solution)/shard_map/ppermute | solution.py:329
  21.0 3.7 %collective-permute-start.11 = (bf16[8,216,128]{2,1,0:T(8,128)(2,1)S(1)}, bf16[8,216,128]{2,1,0:T(8,128)(2,1)S(1)}, u32[]{:S(2)}, u32[]{:S(2)}) collective-permute-start(bf16[8,216,128]{2,1,0:T(8,128)(2,1)S(1)} %get-tuple-element.50), channel_id=1, source_target_pairs={{0,1},{1,0},{2,3},{3,2},{4,5},{5,4},{6,7},{7,6},{8,9},{9,8},{10,11... | collective-permute-start | bytes 1327112 | tf_op jit(solution)/shard_map/ppermute | solution.py:325
  23.3 6.5 %collective-permute-start.9 = (bf16[4,216,128]{2,1,0:T(8,128)(2,1)S(1)}, bf16[4,216,128]{2,1,0:T(8,128)(2,1)S(1)}, u32[]{:S(2)}, u32[]{:S(2)}) collective-permute-start(bf16[4,216,128]{2,1,0:T(8,128)(2,1)S(1)} %collective-permute-done.7.refs_2_.refs_5_), channel_id=1, source_target_pairs={{0,1},{1,0},{2,3},{3,2},{4,5},{5,4},{6,7},{7,6},{8,9},{9,8},{10,11... | collective-permute-start | bytes 663560 | tf_op jit(solution)/shard_map/ppermute | solution.py:325
  25.5 12.3 %collective-permute-start.17 = (bf16[4,216,128]{2,1,0:T(8,128)(2,1)S(1)}, bf16[4,216,128]{2,1,0:T(8,128)(2,1)S(1)}, u32[]{:S(2)}, u32[]{:S(2)}) collective-permute-start(bf16[4,216,128]{2,1,0:T(8,128)(2,1)S(1)} %shard_map.93.refs_8_.refs_3_), channel_id=1, source_target_pairs={{0,1},{1,0},{2,3},{3,2},{4,5},{5,4},{6,7},{7,6},{8,9},{9,8},{10,11... | collective-permute-start | bytes 663560 | tf_op jit(solution)/shard_map/ppermute | solution.py:325
  25.7 8.2 %collective-permute-start.16 = (bf16[4,216,128]{2,1,0:T(8,128)(2,1)S(1)}, bf16[4,216,128]{2,1,0:T(8,128)(2,1)S(1)}, u32[]{:S(2)}, u32[]{:S(2)}) collective-permute-start(bf16[4,216,128]{2,1,0:T(8,128)(2,1)S(1)} %shard_map.93.refs_8_.refs_3_), channel_id=1, source_target_pairs={{0,4},{1,5},{2,6},{3,7},{4,0},{5,1},{6,2},{7,3},{8,12},{9,13},{10,... | collective-permute-start | bytes 663560 | tf_op jit(solution)/shard_map/ppermute | solution.py:325
  28.3 7.3 %collective-permute-start.13 = (bf16[4,216,128]{2,1,0:T(8,128)(2,1)S(1)}, bf16[4,216,128]{2,1,0:T(8,128)(2,1)S(1)}, u32[]{:S(2)}, u32[]{:S(2)}) collective-permute-start(bf16[4,216,128]{2,1,0:T(8,128)(2,1)S(1)} %get-tuple-element.55), channel_id=1, source_target_pairs={{0,2},{1,3},{2,0},{3,1},{4,6},{5,7},{6,4},{7,5},{8,10},{9,11},{10,... | collective-permute-start | bytes 663560 | tf_op jit(solution)/shard_map/ppermute | solution.py:325
  33.1 2.5 %collective-permute-start.12 = (bf16[8,216,128]{2,1,0:T(8,128)(2,1)S(1)}, bf16[8,216,128]{2,1,0:T(8,128)(2,1)S(1)}, u32[]{:S(2)}, u32[]{:S(2)}) collective-permute-start(bf16[8,216,128]{2,1,0:T(8,128)(2,1)S(1)} %get-tuple-element.54), channel_id=1, source_target_pairs={{0,1},{1,0},{2,3},{3,2},{4,5},{5,4},{6,7},{7,6},{8,9},{9,8},{10,11... | collective-permute-start | bytes 1327112 | tf_op jit(solution)/shard_map/ppermute | solution.py:325
  34.0 8.3 %collective-permute-start.18 = (bf16[4,216,128]{2,1,0:T(8,128)(2,1)S(1)}, bf16[4,216,128]{2,1,0:T(8,128)(2,1)S(1)}, u32[]{:S(2)}, u32[]{:S(2)}) collective-permute-start(bf16[4,216,128]{2,1,0:T(8,128)(2,1)S(1)} %collective-permute-done.16.refs_4_), channel_id=1, source_target_pairs={{0,1},{1,0},{2,3},{3,2},{4,5},{5,4},{6,7},{7,6},{8,9},{9,8},{10,11... | collective-permute-start | bytes 663560 | tf_op jit(solution)/shard_map/ppermute | solution.py:325
  35.7 6.9 %collective-permute-start.14 = (bf16[4,216,128]{2,1,0:T(8,128)(2,1)S(1)}, bf16[4,216,128]{2,1,0:T(8,128)(2,1)S(1)}, u32[]{:S(2)}, u32[]{:S(2)}) collective-permute-start(bf16[4,216,128]{2,1,0:T(8,128)(2,1)S(1)} %get-tuple-element.58), channel_id=1, source_target_pairs={{0,2},{1,3},{2,0},{3,1},{4,6},{5,7},{6,4},{7,5},{8,10},{9,11},{10,... | collective-permute-start | bytes 663560 | tf_op jit(solution)/shard_map/ppermute | solution.py:325
  37.5 4.7 %collective-permute-start.15 = (bf16[2,216,128]{2,1,0:T(8,128)(2,1)S(1)}, bf16[2,216,128]{2,1,0:T(8,128)(2,1)S(1)}, u32[]{:S(2)}, u32[]{:S(2)}) collective-permute-start(bf16[2,216,128]{2,1,0:T(8,128)(2,1)S(1)} %get-tuple-element.61), channel_id=1, source_target_pairs={{0,4},{1,5},{2,6},{3,7},{4,0},{5,1},{6,2},{7,3},{8,12},{9,13},{10,... | collective-permute-start | bytes 331784 | tf_op jit(solution)/shard_map/ppermute | solution.py:325
  42.7 5.2 %collective-permute-start.21 = (bf16[2,216,128]{2,1,0:T(8,128)(2,1)S(1)}, bf16[2,216,128]{2,1,0:T(8,128)(2,1)S(1)}, u32[]{:S(2)}, u32[]{:S(2)}) collective-permute-start(bf16[2,216,128]{2,1,0:T(8,128)(2,1)S(1)} %get-tuple-element.66), channel_id=1, source_target_pairs={{0,4},{1,5},{2,6},{3,7},{4,0},{5,1},{6,2},{7,3},{8,12},{9,13},{10,... | collective-permute-start | bytes 331784 | tf_op jit(solution)/shard_map/ppermute | solution.py:325
  44.0 9.5 %collective-permute-start.22 = (bf16[1,216,128]{2,1,0:T(8,128)(2,1)S(1)}, bf16[1,216,128]{2,1,0:T(8,128)(2,1)S(1)}, u32[]{:S(2)}, u32[]{:S(2)}) collective-permute-start(bf16[1,216,128]{2,1,0:T(8,128)(2,1)S(1)} %get-tuple-element.70), channel_id=1, source_target_pairs={{0,8},{1,9},{2,10},{3,11},{4,12},{5,13},{6,14},{7,15},{8,0},{9,1},... | collective-permute-start | bytes 165896 | tf_op jit(solution)/shard_map/ppermute | solution.py:325
  46.0 5.1 %collective-permute-start.19 = (bf16[1,4,128,128]{3,2,1,0:T(8,128)(2,1)S(1)}, bf16[1,4,128,128]{3,2,1,0:T(8,128)(2,1)S(1)}, u32[]{:S(2)}, u32[]{:S(2)}) collective-permute-start(bf16[1,4,128,128]{3,2,1,0:T(8,128)(2,1)S(1)} %get-tuple-element.63), channel_id=1, source_target_pairs={{0,1},{1,0},{2,3},{3,2},{4,5},{5,4},{6,7},{7,6},{8,9},{9,8},{10,11... | collective-permute-start | bytes 393224 | tf_op jit(solution)/shard_map/ppermute | solution.py:325
  46.0 5.1 %collective-permute-start.20 = (bf16[1,4,128,128]{3,2,1,0:T(8,128)(2,1)S(1)}, bf16[1,4,128,128]{3,2,1,0:T(8,128)(2,1)S(1)}, u32[]{:S(2)}, u32[]{:S(2)}) collective-permute-start(bf16[1,4,128,128]{3,2,1,0:T(8,128)(2,1)S(1)} %get-tuple-element.64), channel_id=1, source_target_pairs={{1,2},{3,4},{5,6},{7,8},{9,10},{11,12},{13,14},{2,1},{4,3},{6,5},{... | collective-permute-start | bytes 393224 | tf_op jit(solution)/shard_map/ppermute | solution.py:329
  47.9 8.1 %collective-permute-start.23 = (bf16[1,216,128]{2,1,0:T(8,128)(2,1)S(1)}, bf16[1,216,128]{2,1,0:T(8,128)(2,1)S(1)}, u32[]{:S(2)}, u32[]{:S(2)}) collective-permute-start(bf16[1,216,128]{2,1,0:T(8,128)(2,1)S(1)} %get-tuple-element.72), channel_id=1, source_target_pairs={{0,8},{1,9},{2,10},{3,11},{4,12},{5,13},{6,14},{7,15},{8,0},{9,1},... | collective-permute-start | bytes 165896 | tf_op jit(solution)/shard_map/ppermute | solution.py:325
  (4 other events, 12.8 us)

commit v6 on v5

--- a/solution.py
+++ b/solution.py
@@ -434,7 +434,7 @@
                 us=us,
             )
 
-        kept_two, sent_two = step(kept_two, sent_two, 4, 2, 2, (grad_one,), 20)
+        kept_two, sent_two = step(kept_two, sent_two, 4, 2, 2, (grad_one,), 3)
         kept_one, sent_one = step(*terms_one, 3, 1, 4, (kept_two,))
         mine = (column_first, swap(column_first, 4))
         full_first = (*mine, *(swap(m, 1) for m in mine))

time: 57 us -> 56.5 us (level)
  no operation moved by 1% of the time
where the time goes in v6:
time: 56.5 us; the launch traced here: 56.2 us
  starting transfers between devices  28.5 us (50%)
  waiting for transfers between devices  16.4 us (29%)
  Pallas kernels  9.16 us (16%)
  other arithmetic  1.29 us (2%)
  between operations  0.82 us (1%)
    ppermute x21, starting transfers between devices, swap(): return lax.ppermute(array, 'gx', [(i, i ^ mask) for i in range(n)])  26.5 us
    ppermute x21, waiting for transfers between devices, swap(): return lax.ppermute(array, 'gx', [(i, i ^ mask) for i in range(n)])  16.4 us
    pallas_call x17, Pallas kernels, call(): pl.pallas_call(run, in_specs=[vmem] * first + [anywhere] * many, out_spec...  9.16 us
    ppermute x3, starting transfers between devices, swap_far(): return lax.ppermute(array, 'gx', ahead + [(b, a) for a, b in ahead])  1.98 us
    convert_element_type x1, other arithmetic, on_device(): (grad_out.astype(f32) * slope_of(pre_second.astype(f32))).astype(bf16)  1.29 us
  transfers between devices with their start and end apart: 24, of which 9 were waited for; matrix products, arithmetic and copies ran while one was open for 2% of the time, Pallas kernels for 15%

profile of v6, /device:TPU:0, one launch (start us, length us, event | category | flops | bytes accessed | tf_op | source)
XLA Modules:
  0.0 56.2 jit_solution(12238872761456228302)
XLA Ops:
  0.6 3.0 %collective-permute-start.1 = (bf16[216,128]{1,0:T(8,128)(2,1)}, bf16[216,128]{1,0:T(8,128)(2,1)S(1)}, u32[]{:S(2)}, u32[]{:S(2)}) collective-permute-start(bf16[216,128]{1,0:T(8,128)(2,1)} %refs_2_.2), channel_id=1, source_target_pairs={{0,2},{1,3},{2,0},{3,1},{4,6},{5,7},{6,4},{7,5},{8,10},{9,11},{10,... | collective-permute-start | bytes 165896 | tf_op jit(solution)/shard_map/ppermute | solution.py:325
  3.6 2.6 %collective-permute-start = (bf16[216,128]{1,0:T(8,128)(2,1)}, bf16[216,128]{1,0:T(8,128)(2,1)S(1)}, u32[]{:S(2)}, u32[]{:S(2)}) collective-permute-start(bf16[216,128]{1,0:T(8,128)(2,1)} %refs_0_.2), channel_id=1, source_target_pairs={{0,8},{1,9},{2,10},{3,11},{4,12},{5,13},{6,14},{7,15},{8,0},{9,1},... | collective-permute-start | bytes 165896 | tf_op jit(solution)/shard_map/ppermute | solution.py:325
  6.2 1.3 %fusion.7.refs_0_ = bf16[2,4,128,128]{3,2,1,0:T(8,128)(2,1)S(1)} fusion(bf16[2,4,128,128]{3,2,1,0:T(8,128)(2,1)} %param.9, bf16[2,4,128,128]{3,2,1,0:T(8,128)(2,1)} %param.6), kind=kLoop, calls=%fused_computation.11 | loop fusion | flops 1572864 | bytes 786432 | tf_op jit(solution)/shard_map/convert_element_type | solution.py:342
  8.3 2.0 %collective-permute-start.2 = (bf16[1,4,128,128]{3,2,1,0:T(8,128)(2,1)S(1)}, bf16[1,4,128,128]{3,2,1,0:T(8,128)(2,1)S(1)}, u32[]{:S(2)}, u32[]{:S(2)}) collective-permute-start(bf16[1,4,128,128]{3,2,1,0:T(8,128)(2,1)S(1)} %get-tuple-element.39.refs_4_), channel_id=1, source_target_pairs={{0,1},{1,0},{2,3},{3,2},{4,5},{5,4},{6,7},{7,6},{8,9},{9,8},{10,11... | collective-permute-start | bytes 393224 | tf_op jit(solution)/shard_map/ppermute | solution.py:325
  10.3 1.6 %collective-permute-start.4 = (bf16[2,216,128]{2,1,0:T(8,128)(2,1)S(1)}, bf16[2,216,128]{2,1,0:T(8,128)(2,1)S(1)}, u32[]{:S(2)}, u32[]{:S(2)}) collective-permute-start(bf16[2,216,128]{2,1,0:T(8,128)(2,1)S(1)} %get-tuple-element.40.refs_2_.refs_0_), channel_id=1, source_target_pairs={{0,4},{1,5},{2,6},{3,7},{4,0},{5,1},{6,2},{7,3},{8,12},{9,13},{10,... | collective-permute-start | bytes 331784 | tf_op jit(solution)/shard_map/ppermute | solution.py:325
  12.5 3.8 %collective-permute-done.4.refs_1_ = bf16[2,216,128]{2,1,0:T(8,128)(2,1)S(1)} collective-permute-done((bf16[2,216,128]{2,1,0:T(8,128)(2,1)S(1)}, bf16[2,216,128]{2,1,0:T(8,128)(2,1)S(1)}, u32[]{:S(2)}, u32[]{:S(2)}) %collective-permute-start.4) | collective-permute-done | bytes 110624 | tf_op jit(solution)/shard_map/ppermute | solution.py:325
  16.4 1.5 %collective-permute-start.7 = (bf16[4,216,128]{2,1,0:T(8,128)(2,1)S(1)}, bf16[4,216,128]{2,1,0:T(8,128)(2,1)S(1)}, u32[]{:S(2)}, u32[]{:S(2)}) collective-permute-start(bf16[4,216,128]{2,1,0:T(8,128)(2,1)S(1)} %get-tuple-element.47.refs_2_.refs_4_), channel_id=1, source_target_pairs={{0,2},{1,3},{2,0},{3,1},{4,6},{5,7},{6,4},{7,5},{8,10},{9,11},{10,... | collective-permute-start | bytes 663560 | tf_op jit(solution)/shard_map/ppermute | solution.py:325
  19.5 1.5 %shard_map.91 = (f32[8,216,128]{2,1,0:T(8,128)S(1)}, bf16[8,216,128]{2,1,0:T(8,128)(2,1)S(1)}) custom-call(bf16[4,6,128,128]{3,2,1,0:T(8,128)(2,1)S(1)} %shard_map.88.refs_3_.refs_0_.refs_1_, bf16[384,1024]{1,0:T(8,128)(2,1)S(1)} %get-tuple-element.43.refs_3_.refs_1_, bf16[4,216,128]{2,1,0:T(8,128)(2,1)S(1)} %get-tuple-element.47.refs_2_.refs_4_), custom_call_target="tpu_custom_call" | custom-call | flops 2000000000 | bytes 6000000 | tf_op jit(solution)/shard_map/pallas_call | solution.py:295
  20.9 2.3 %collective-permute-start.11 = (bf16[8,216,128]{2,1,0:T(8,128)(2,1)S(1)}, bf16[8,216,128]{2,1,0:T(8,128)(2,1)S(1)}, u32[]{:S(2)}, u32[]{:S(2)}) collective-permute-start(bf16[8,216,128]{2,1,0:T(8,128)(2,1)S(1)} %get-tuple-element.50), channel_id=1, source_target_pairs={{0,1},{1,0},{2,3},{3,2},{4,5},{5,4},{6,7},{7,6},{8,9},{9,8},{10,11... | collective-permute-start | bytes 1327112 | tf_op jit(solution)/shard_map/ppermute | solution.py:325
  23.5 1.2 %collective-permute-done.11.refs_1_ = bf16[8,216,128]{2,1,0:T(8,128)(2,1)S(1)} collective-permute-done((bf16[8,216,128]{2,1,0:T(8,128)(2,1)S(1)}, bf16[8,216,128]{2,1,0:T(8,128)(2,1)S(1)}, u32[]{:S(2)}, u32[]{:S(2)}) %collective-permute-start.11) | collective-permute-done | bytes 442400 | tf_op jit(solution)/shard_map/ppermute | solution.py:325
  25.5 2.4 %collective-permute-start.16 = (bf16[4,216,128]{2,1,0:T(8,128)(2,1)S(1)}, bf16[4,216,128]{2,1,0:T(8,128)(2,1)S(1)}, u32[]{:S(2)}, u32[]{:S(2)}) collective-permute-start(bf16[4,216,128]{2,1,0:T(8,128)(2,1)S(1)} %shard_map.93.refs_8_.refs_3_), channel_id=1, source_target_pairs={{0,4},{1,5},{2,6},{3,7},{4,0},{5,1},{6,2},{7,3},{8,12},{9,13},{10,... | collective-permute-start | bytes 663560 | tf_op jit(solution)/shard_map/ppermute | solution.py:325
  27.9 1.8 %collective-permute-start.13 = (bf16[4,216,128]{2,1,0:T(8,128)(2,1)S(1)}, bf16[4,216,128]{2,1,0:T(8,128)(2,1)S(1)}, u32[]{:S(2)}, u32[]{:S(2)}) collective-permute-start(bf16[4,216,128]{2,1,0:T(8,128)(2,1)S(1)} %get-tuple-element.55), channel_id=1, source_target_pairs={{0,2},{1,3},{2,0},{3,1},{4,6},{5,7},{6,4},{7,5},{8,10},{9,11},{10,... | collective-permute-start | bytes 663560 | tf_op jit(solution)/shard_map/ppermute | solution.py:325
  29.7 3.3 %shard_map.94 = (f32[8,216,128]{2,1,0:T(8,128)S(1)}, bf16[8,216,128]{2,1,0:T(8,128)(2,1)S(1)}, bf16[2,4,128,128]{3,2,1,0:T(8,128)(2,1)S(1)}, bf16[1,4,128,128]{3...) custom-call(f32[2,4,128,128]{3,2,1,0:T(8,128)S(1)} %get-tuple-element.41.refs_0_, ...), custom_call_target="tpu_custom_call" | custom-call | flops 8000000000 | bytes 24000000 | tf_op jit(solution)/shard_map/pallas_call | solution.py:295
  33.9 1.5 %collective-permute-done.13.refs_1_ = bf16[4,216,128]{2,1,0:T(8,128)(2,1)S(1)} collective-permute-done((bf16[4,216,128]{2,1,0:T(8,128)(2,1)S(1)}, bf16[4,216,128]{2,1,0:T(8,128)(2,1)S(1)}, u32[]{:S(2)}, u32[]{:S(2)}) %collective-permute-start.13) | collective-permute-done | bytes 221216 | tf_op jit(solution)/shard_map/ppermute | solution.py:325
  35.5 0.9 %collective-permute-start.14 = (bf16[4,216,128]{2,1,0:T(8,128)(2,1)S(1)}, bf16[4,216,128]{2,1,0:T(8,128)(2,1)S(1)}, u32[]{:S(2)}, u32[]{:S(2)}) collective-permute-start(bf16[4,216,128]{2,1,0:T(8,128)(2,1)S(1)} %get-tuple-element.58), channel_id=1, source_target_pairs={{0,2},{1,3},{2,0},{3,1},{4,6},{5,7},{6,4},{7,5},{8,10},{9,11},{10,... | collective-permute-start | bytes 663560 | tf_op jit(solution)/shard_map/ppermute | solution.py:325
  36.5 1.2 %collective-permute-start.15 = (bf16[2,216,128]{2,1,0:T(8,128)(2,1)S(1)}, bf16[2,216,128]{2,1,0:T(8,128)(2,1)S(1)}, u32[]{:S(2)}, u32[]{:S(2)}) collective-permute-start(bf16[2,216,128]{2,1,0:T(8,128)(2,1)S(1)} %get-tuple-element.61), channel_id=1, source_target_pairs={{0,4},{1,5},{2,6},{3,7},{4,0},{5,1},{6,2},{7,3},{8,12},{9,13},{10,... | collective-permute-start | bytes 331784 | tf_op jit(solution)/shard_map/ppermute | solution.py:325
  37.6 3.6 %collective-permute-done.15.refs_1_ = bf16[2,216,128]{2,1,0:T(8,128)(2,1)S(1)} collective-permute-done((bf16[2,216,128]{2,1,0:T(8,128)(2,1)S(1)}, bf16[2,216,128]{2,1,0:T(8,128)(2,1)S(1)}, u32[]{:S(2)}, u32[]{:S(2)}) %collective-permute-start.15) | collective-permute-done | bytes 110624 | tf_op jit(solution)/shard_map/ppermute | solution.py:325
  41.2 1.3 %collective-permute-done.14.refs_1_ = bf16[4,216,128]{2,1,0:T(8,128)(2,1)S(1)} collective-permute-done((bf16[4,216,128]{2,1,0:T(8,128)(2,1)S(1)}, bf16[4,216,128]{2,1,0:T(8,128)(2,1)S(1)}, u32[]{:S(2)}, u32[]{:S(2)}) %collective-permute-start.14) | collective-permute-done | bytes 221216 | tf_op jit(solution)/shard_map/ppermute | solution.py:325
  42.6 1.3 %collective-permute-start.21 = (bf16[2,216,128]{2,1,0:T(8,128)(2,1)S(1)}, bf16[2,216,128]{2,1,0:T(8,128)(2,1)S(1)}, u32[]{:S(2)}, u32[]{:S(2)}) collective-permute-start(bf16[2,216,128]{2,1,0:T(8,128)(2,1)S(1)} %get-tuple-element.66), channel_id=1, source_target_pairs={{0,4},{1,5},{2,6},{3,7},{4,0},{5,1},{6,2},{7,3},{8,12},{9,13},{10,... | collective-permute-start | bytes 331784 | tf_op jit(solution)/shard_map/ppermute | solution.py:325
  43.9 2.1 %collective-permute-start.22 = (bf16[1,216,128]{2,1,0:T(8,128)(2,1)S(1)}, bf16[1,216,128]{2,1,0:T(8,128)(2,1)S(1)}, u32[]{:S(2)}, u32[]{:S(2)}) collective-permute-start(bf16[1,216,128]{2,1,0:T(8,128)(2,1)S(1)} %get-tuple-element.70), channel_id=1, source_target_pairs={{0,8},{1,9},{2,10},{3,11},{4,12},{5,13},{6,14},{7,15},{8,0},{9,1},... | collective-permute-start | bytes 165896 | tf_op jit(solution)/shard_map/ppermute | solution.py:325
  46.6 1.4 %collective-permute-done.21.refs_1_ = bf16[2,216,128]{2,1,0:T(8,128)(2,1)S(1)} collective-permute-done((bf16[2,216,128]{2,1,0:T(8,128)(2,1)S(1)}, bf16[2,216,128]{2,1,0:T(8,128)(2,1)S(1)}, u32[]{:S(2)}, u32[]{:S(2)}) %collective-permute-start.21) | collective-permute-done | bytes 110624 | tf_op jit(solution)/shard_map/ppermute | solution.py:325
  48.0 2.3 %collective-permute-start.23 = (bf16[1,216,128]{2,1,0:T(8,128)(2,1)S(1)}, bf16[1,216,128]{2,1,0:T(8,128)(2,1)S(1)}, u32[]{:S(2)}, u32[]{:S(2)}) collective-permute-start(bf16[1,216,128]{2,1,0:T(8,128)(2,1)S(1)} %get-tuple-element.72), channel_id=1, source_target_pairs={{0,8},{1,9},{2,10},{3,11},{4,12},{5,13},{6,14},{7,15},{8,0},{9,1},... | collective-permute-start | bytes 165896 | tf_op jit(solution)/shard_map/ppermute | solution.py:325
  50.4 2.4 %shard_map.100 = (bf16[2,4,128,128]{3,2,1,0:T(8,128)(2,1)}, f32[1,216,128]{2,1,0:T(8,128)S(1)}, f32[1,216,128]{2,1,0:T(8,128)S(1)}) custom-call(bf16[2,4,128,128]{3,2,1,0:T(8,128)(2,1)S(1)} %get-tuple-element.52.refs_2_.refs_0_, bf16[1,4,128,128]{3,2,1,0:T(8,128)(2,1)S(1)} %collective-permute-done.19.refs_1_, ...), custom_call_target="tpu_custom_call" | custom-call | flops 5000000000 | bytes 15000000 | tf_op jit(solution)/shard_map/pallas_call | solution.py:295
  52.8 2.7 %collective-permute-done.23.refs_3_ = bf16[1,216,128]{2,1,0:T(8,128)(2,1)S(1)} collective-permute-done((bf16[1,216,128]{2,1,0:T(8,128)(2,1)S(1)}, bf16[1,216,128]{2,1,0:T(8,128)(2,1)S(1)}, u32[]{:S(2)}, u32[]{:S(2)}) %collective-permute-start.23) | collective-permute-done | bytes 55328 | tf_op jit(solution)/shard_map/ppermute | solution.py:325
  (50 shorter events, 6.4 us)
Async XLA Ops:
  0.6 9.6 %collective-permute-start.1 = (bf16[216,128]{1,0:T(8,128)(2,1)}, bf16[216,128]{1,0:T(8,128)(2,1)S(1)}, u32[]{:S(2)}, u32[]{:S(2)}) collective-permute-start(bf16[216,128]{1,0:T(8,128)(2,1)} %refs_2_.2), channel_id=1, source_target_pairs={{0,2},{1,3},{2,0},{3,1},{4,6},{5,7},{6,4},{7,5},{8,10},{9,11},{10,... | collective-permute-start | bytes 165896 | tf_op jit(solution)/shard_map/ppermute | solution.py:325
  3.6 6.6 %collective-permute-start = (bf16[216,128]{1,0:T(8,128)(2,1)}, bf16[216,128]{1,0:T(8,128)(2,1)S(1)}, u32[]{:S(2)}, u32[]{:S(2)}) collective-permute-start(bf16[216,128]{1,0:T(8,128)(2,1)} %refs_0_.2), channel_id=1, source_target_pairs={{0,8},{1,9},{2,10},{3,11},{4,12},{5,13},{6,14},{7,15},{8,0},{9,1},... | collective-permute-start | bytes 165896 | tf_op jit(solution)/shard_map/ppermute | solution.py:325
  7.6 4.9 %collective-permute-start.3 = (bf16[1,4,128,128]{3,2,1,0:T(8,128)(2,1)S(1)}, bf16[1,4,128,128]{3,2,1,0:T(8,128)(2,1)S(1)}, u32[]{:S(2)}, u32[]{:S(2)}) collective-permute-start(bf16[1,4,128,128]{3,2,1,0:T(8,128)(2,1)S(1)} %get-tuple-element.42), channel_id=1, source_target_pairs={{1,2},{3,4},{5,6},{7,8},{9,10},{11,12},{13,14},{2,1},{4,3},{6,5},{... | collective-permute-start | bytes 393224 | tf_op jit(solution)/shard_map/ppermute | solution.py:329
  8.3 4.2 %collective-permute-start.2 = (bf16[1,4,128,128]{3,2,1,0:T(8,128)(2,1)S(1)}, bf16[1,4,128,128]{3,2,1,0:T(8,128)(2,1)S(1)}, u32[]{:S(2)}, u32[]{:S(2)}) collective-permute-start(bf16[1,4,128,128]{3,2,1,0:T(8,128)(2,1)S(1)} %get-tuple-element.39.refs_4_), channel_id=1, source_target_pairs={{0,1},{1,0},{2,3},{3,2},{4,5},{5,4},{6,7},{7,6},{8,9},{9,8},{10,11... | collective-permute-start | bytes 393224 | tf_op jit(solution)/shard_map/ppermute | solution.py:325
  10.3 6.1 %collective-permute-start.4 = (bf16[2,216,128]{2,1,0:T(8,128)(2,1)S(1)}, bf16[2,216,128]{2,1,0:T(8,128)(2,1)S(1)}, u32[]{:S(2)}, u32[]{:S(2)}) collective-permute-start(bf16[2,216,128]{2,1,0:T(8,128)(2,1)S(1)} %get-tuple-element.40.refs_2_.refs_0_), channel_id=1, source_target_pairs={{0,4},{1,5},{2,6},{3,7},{4,0},{5,1},{6,2},{7,3},{8,12},{9,13},{10,... | collective-permute-start | bytes 331784 | tf_op jit(solution)/shard_map/ppermute | solution.py:325
  16.4 6.9 %collective-permute-start.7 = (bf16[4,216,128]{2,1,0:T(8,128)(2,1)S(1)}, bf16[4,216,128]{2,1,0:T(8,128)(2,1)S(1)}, u32[]{:S(2)}, u32[]{:S(2)}) collective-permute-start(bf16[4,216,128]{2,1,0:T(8,128)(2,1)S(1)} %get-tuple-element.47.refs_2_.refs_4_), channel_id=1, source_target_pairs={{0,2},{1,3},{2,0},{3,1},{4,6},{5,7},{6,4},{7,5},{8,10},{9,11},{10,... | collective-permute-start | bytes 663560 | tf_op jit(solution)/shard_map/ppermute | solution.py:325
  17.9 7.5 %collective-permute-start.10 = (bf16[2,216,128]{2,1,0:T(8,128)(2,1)S(1)}, bf16[2,216,128]{2,1,0:T(8,128)(2,1)S(1)}, u32[]{:S(2)}, u32[]{:S(2)}) collective-permute-start(bf16[2,216,128]{2,1,0:T(8,128)(2,1)S(1)} %get-tuple-element.48.refs_0_), channel_id=1, source_target_pairs={{0,8},{1,9},{2,10},{3,11},{4,12},{5,13},{6,14},{7,15},{8,0},{9,1},... | collective-permute-start | bytes 331784 | tf_op jit(solution)/shard_map/ppermute | solution.py:325
  18.3 11.4 %collective-permute-start.8 = (bf16[4,216,128]{2,1,0:T(8,128)(2,1)S(1)}, bf16[4,216,128]{2,1,0:T(8,128)(2,1)S(1)}, u32[]{:S(2)}, u32[]{:S(2)}) collective-permute-start(bf16[4,216,128]{2,1,0:T(8,128)(2,1)S(1)} %get-tuple-element.47.refs_2_.refs_4_), channel_id=1, source_target_pairs={{0,1},{1,0},{2,3},{3,2},{4,5},{5,4},{6,7},{7,6},{8,9},{9,8},{10,11... | collective-permute-start | bytes 663560 | tf_op jit(solution)/shard_map/ppermute | solution.py:325
  18.3 2.7 %collective-permute-start.5 = (bf16[1,4,128,128]{3,2,1,0:T(8,128)(2,1)S(1)}, bf16[1,4,128,128]{3,2,1,0:T(8,128)(2,1)S(1)}, u32[]{:S(2)}, u32[]{:S(2)}) collective-permute-start(bf16[1,4,128,128]{3,2,1,0:T(8,128)(2,1)S(1)} %get-tuple-element.45), channel_id=1, source_target_pairs={{0,1},{1,0},{2,3},{3,2},{4,5},{5,4},{6,7},{7,6},{8,9},{9,8},{10,11... | collective-permute-start | bytes 393224 | tf_op jit(solution)/shard_map/ppermute | solution.py:325
  18.8 4.6 %collective-permute-start.6 = (bf16[1,4,128,128]{3,2,1,0:T(8,128)(2,1)S(1)}, bf16[1,4,128,128]{3,2,1,0:T(8,128)(2,1)S(1)}, u32[]{:S(2)}, u32[]{:S(2)}) collective-permute-start(bf16[1,4,128,128]{3,2,1,0:T(8,128)(2,1)S(1)} %get-tuple-element.46), channel_id=1, source_target_pairs={{1,2},{3,4},{5,6},{7,8},{9,10},{11,12},{13,14},{2,1},{4,3},{6,5},{... | collective-permute-start | bytes 393224 | tf_op jit(solution)/shard_map/ppermute | solution.py:329
  20.9 3.8 %collective-permute-start.11 = (bf16[8,216,128]{2,1,0:T(8,128)(2,1)S(1)}, bf16[8,216,128]{2,1,0:T(8,128)(2,1)S(1)}, u32[]{:S(2)}, u32[]{:S(2)}) collective-permute-start(bf16[8,216,128]{2,1,0:T(8,128)(2,1)S(1)} %get-tuple-element.50), channel_id=1, source_target_pairs={{0,1},{1,0},{2,3},{3,2},{4,5},{5,4},{6,7},{7,6},{8,9},{9,8},{10,11... | collective-permute-start | bytes 1327112 | tf_op jit(solution)/shard_map/ppermute | solution.py:325
  23.3 6.4 %collective-permute-start.9 = (bf16[4,216,128]{2,1,0:T(8,128)(2,1)S(1)}, bf16[4,216,128]{2,1,0:T(8,128)(2,1)S(1)}, u32[]{:S(2)}, u32[]{:S(2)}) collective-permute-start(bf16[4,216,128]{2,1,0:T(8,128)(2,1)S(1)} %collective-permute-done.7.refs_2_.refs_5_), channel_id=1, source_target_pairs={{0,1},{1,0},{2,3},{3,2},{4,5},{5,4},{6,7},{7,6},{8,9},{9,8},{10,11... | collective-permute-start | bytes 663560 | tf_op jit(solution)/shard_map/ppermute | solution.py:325
  25.5 8.3 %collective-permute-start.16 = (bf16[4,216,128]{2,1,0:T(8,128)(2,1)S(1)}, bf16[4,216,128]{2,1,0:T(8,128)(2,1)S(1)}, u32[]{:S(2)}, u32[]{:S(2)}) collective-permute-start(bf16[4,216,128]{2,1,0:T(8,128)(2,1)S(1)} %shard_map.93.refs_8_.refs_3_), channel_id=1, source_target_pairs={{0,4},{1,5},{2,6},{3,7},{4,0},{5,1},{6,2},{7,3},{8,12},{9,13},{10,... | collective-permute-start | bytes 663560 | tf_op jit(solution)/shard_map/ppermute | solution.py:325
  27.9 7.5 %collective-permute-start.13 = (bf16[4,216,128]{2,1,0:T(8,128)(2,1)S(1)}, bf16[4,216,128]{2,1,0:T(8,128)(2,1)S(1)}, u32[]{:S(2)}, u32[]{:S(2)}) collective-permute-start(bf16[4,216,128]{2,1,0:T(8,128)(2,1)S(1)} %get-tuple-element.55), channel_id=1, source_target_pairs={{0,2},{1,3},{2,0},{3,1},{4,6},{5,7},{6,4},{7,5},{8,10},{9,11},{10,... | collective-permute-start | bytes 663560 | tf_op jit(solution)/shard_map/ppermute | solution.py:325
  33.0 2.4 %collective-permute-start.12 = (bf16[8,216,128]{2,1,0:T(8,128)(2,1)S(1)}, bf16[8,216,128]{2,1,0:T(8,128)(2,1)S(1)}, u32[]{:S(2)}, u32[]{:S(2)}) collective-permute-start(bf16[8,216,128]{2,1,0:T(8,128)(2,1)S(1)} %get-tuple-element.54), channel_id=1, source_target_pairs={{0,1},{1,0},{2,3},{3,2},{4,5},{5,4},{6,7},{7,6},{8,9},{9,8},{10,11... | collective-permute-start | bytes 1327112 | tf_op jit(solution)/shard_map/ppermute | solution.py:325
  33.1 4.5 %collective-permute-start.17 = (bf16[4,216,128]{2,1,0:T(8,128)(2,1)S(1)}, bf16[4,216,128]{2,1,0:T(8,128)(2,1)S(1)}, u32[]{:S(2)}, u32[]{:S(2)}) collective-permute-start(bf16[4,216,128]{2,1,0:T(8,128)(2,1)S(1)} %shard_map.93.refs_8_.refs_3_), channel_id=1, source_target_pairs={{0,1},{1,0},{2,3},{3,2},{4,5},{5,4},{6,7},{7,6},{8,9},{9,8},{10,11... | collective-permute-start | bytes 663560 | tf_op jit(solution)/shard_map/ppermute | solution.py:325
  33.9 7.3 %collective-permute-start.18 = (bf16[4,216,128]{2,1,0:T(8,128)(2,1)S(1)}, bf16[4,216,128]{2,1,0:T(8,128)(2,1)S(1)}, u32[]{:S(2)}, u32[]{:S(2)}) collective-permute-start(bf16[4,216,128]{2,1,0:T(8,128)(2,1)S(1)} %collective-permute-done.16.refs_4_), channel_id=1, source_target_pairs={{0,1},{1,0},{2,3},{3,2},{4,5},{5,4},{6,7},{7,6},{8,9},{9,8},{10,11... | collective-permute-start | bytes 663560 | tf_op jit(solution)/shard_map/ppermute | solution.py:325
  35.5 7.0 %collective-permute-start.14 = (bf16[4,216,128]{2,1,0:T(8,128)(2,1)S(1)}, bf16[4,216,128]{2,1,0:T(8,128)(2,1)S(1)}, u32[]{:S(2)}, u32[]{:S(2)}) collective-permute-start(bf16[4,216,128]{2,1,0:T(8,128)(2,1)S(1)} %get-tuple-element.58), channel_id=1, source_target_pairs={{0,2},{1,3},{2,0},{3,1},{4,6},{5,7},{6,4},{7,5},{8,10},{9,11},{10,... | collective-permute-start | bytes 663560 | tf_op jit(solution)/shard_map/ppermute | solution.py:325
  36.5 4.7 %collective-permute-start.15 = (bf16[2,216,128]{2,1,0:T(8,128)(2,1)S(1)}, bf16[2,216,128]{2,1,0:T(8,128)(2,1)S(1)}, u32[]{:S(2)}, u32[]{:S(2)}) collective-permute-start(bf16[2,216,128]{2,1,0:T(8,128)(2,1)S(1)} %get-tuple-element.61), channel_id=1, source_target_pairs={{0,4},{1,5},{2,6},{3,7},{4,0},{5,1},{6,2},{7,3},{8,12},{9,13},{10,... | collective-permute-start | bytes 331784 | tf_op jit(solution)/shard_map/ppermute | solution.py:325
  42.6 5.4 %collective-permute-start.21 = (bf16[2,216,128]{2,1,0:T(8,128)(2,1)S(1)}, bf16[2,216,128]{2,1,0:T(8,128)(2,1)S(1)}, u32[]{:S(2)}, u32[]{:S(2)}) collective-permute-start(bf16[2,216,128]{2,1,0:T(8,128)(2,1)S(1)} %get-tuple-element.66), channel_id=1, source_target_pairs={{0,4},{1,5},{2,6},{3,7},{4,0},{5,1},{6,2},{7,3},{8,12},{9,13},{10,... | collective-permute-start | bytes 331784 | tf_op jit(solution)/shard_map/ppermute | solution.py:325
  43.9 9.0 %collective-permute-start.22 = (bf16[1,216,128]{2,1,0:T(8,128)(2,1)S(1)}, bf16[1,216,128]{2,1,0:T(8,128)(2,1)S(1)}, u32[]{:S(2)}, u32[]{:S(2)}) collective-permute-start(bf16[1,216,128]{2,1,0:T(8,128)(2,1)S(1)} %get-tuple-element.70), channel_id=1, source_target_pairs={{0,8},{1,9},{2,10},{3,11},{4,12},{5,13},{6,14},{7,15},{8,0},{9,1},... | collective-permute-start | bytes 165896 | tf_op jit(solution)/shard_map/ppermute | solution.py:325
  46.0 4.4 %collective-permute-start.19 = (bf16[1,4,128,128]{3,2,1,0:T(8,128)(2,1)S(1)}, bf16[1,4,128,128]{3,2,1,0:T(8,128)(2,1)S(1)}, u32[]{:S(2)}, u32[]{:S(2)}) collective-permute-start(bf16[1,4,128,128]{3,2,1,0:T(8,128)(2,1)S(1)} %get-tuple-element.63), channel_id=1, source_target_pairs={{0,1},{1,0},{2,3},{3,2},{4,5},{5,4},{6,7},{7,6},{8,9},{9,8},{10,11... | collective-permute-start | bytes 393224 | tf_op jit(solution)/shard_map/ppermute | solution.py:325
  46.0 4.4 %collective-permute-start.20 = (bf16[1,4,128,128]{3,2,1,0:T(8,128)(2,1)S(1)}, bf16[1,4,128,128]{3,2,1,0:T(8,128)(2,1)S(1)}, u32[]{:S(2)}, u32[]{:S(2)}) collective-permute-start(bf16[1,4,128,128]{3,2,1,0:T(8,128)(2,1)S(1)} %get-tuple-element.64), channel_id=1, source_target_pairs={{1,2},{3,4},{5,6},{7,8},{9,10},{11,12},{13,14},{2,1},{4,3},{6,5},{... | collective-permute-start | bytes 393224 | tf_op jit(solution)/shard_map/ppermute | solution.py:329
  48.0 7.5 %collective-permute-start.23 = (bf16[1,216,128]{2,1,0:T(8,128)(2,1)S(1)}, bf16[1,216,128]{2,1,0:T(8,128)(2,1)S(1)}, u32[]{:S(2)}, u32[]{:S(2)}) collective-permute-start(bf16[1,216,128]{2,1,0:T(8,128)(2,1)S(1)} %get-tuple-element.72), channel_id=1, source_target_pairs={{0,8},{1,9},{2,10},{3,11},{4,12},{5,13},{6,14},{7,15},{8,0},{9,1},... | collective-permute-start | bytes 165896 | tf_op jit(solution)/shard_map/ppermute | solution.py:325
  (4 other events, 12.8 us)
